TPU v7x, 32 devices: a whole 2x2x4 slice. The times are simulated.
32 devices in a mesh: dp: 2 (over z_hi), seq: 8 (over y, x, core), tensor: 2 (over z_lo).
Axes of the slice: x: 2, y: 2, z: 4 (z_hi: 2, z_lo: 2; z = z_hi * 2 + z_lo), core: 2. Of those that a mesh axis runs over, the one named last changes fastest.
Arguments:
- hidden_in: bfloat16 [4096, 2048], P(('dp', 'seq')), may hold values from -6 to 6
- doc_lengths: int32 [2, 2], P('dp'), may hold values from 1 to 2047, as said below
- attention_gain: float32 [2048], replicated, may hold values from 0.1 to 1.9
- query_weight: bfloat16 [2048, 2048], P(('dp', 'seq'), 'tensor'), may hold values from -0.125 to 0.125
- key_projection: bfloat16 [2048, 512], P(('dp', 'seq'), 'tensor'), may hold values from -0.125 to 0.125
- value_projection: bfloat16 [2048, 512], P(('dp', 'seq'), 'tensor'), may hold values from -0.125 to 0.125
- output_weight: bfloat16 [2048, 2048], P('tensor', ('dp', 'seq')), may hold values from -0.5 to 0.5
- query_down: bfloat16 [2048, 8], replicated, may hold values from -0.125 to 0.125
- query_up: bfloat16 [8, 2048], P(None, 'tensor'), may hold values from -2 to 2
- key_down: bfloat16 [2048, 8], replicated, may hold values from -0.125 to 0.125
- key_adapter_up: bfloat16 [8, 512], P(None, 'tensor'), may hold values from -2 to 2
- value_down: bfloat16 [2048, 8], replicated, may hold values from -0.125 to 0.125
- value_adapter_up: bfloat16 [8, 512], P(None, 'tensor'), may hold values from -2 to 2
- output_down: bfloat16 [2048, 8], P('tensor'), may hold values from -0.5 to 0.5
- output_up: bfloat16 [8, 2048], replicated, may hold values from -2 to 2
- query_feature_maps: bfloat16 [32, 64, 64], P('tensor'), may hold values from -0.75 to 0.75
- key_feature_maps: bfloat16 [32, 64, 64], P('tensor'), may hold values from -0.75 to 0.75
- feedforward_gain: float32 [2048], replicated, may hold values from 0.1 to 1.9
- gate_weight: bfloat16 [2048, 8192], P(('dp', 'seq'), 'tensor'), may hold values from -0.125 to 0.125
- up_weight: bfloat16 [2048, 8192], P(('dp', 'seq'), 'tensor'), may hold values from -0.125 to 0.125
- down_weight: bfloat16 [8192, 2048], P('tensor', ('dp', 'seq')), may hold values from -0.0625 to 0.0625
- block_cotangent: bfloat16 [4096, 2048], P(('dp', 'seq')), may hold values from -6 to 6
Outputs:
- block_output: bfloat16 [4096, 2048], P(('dp', 'seq'))
- input_grad: bfloat16 [4096, 2048], P(('dp', 'seq'))
- attention_gain_grad: float32 [2048], replicated
- query_weight_grad: float32 [2048, 2048], P(('dp', 'seq'), 'tensor')
- key_weight_grad: float32 [2048, 512], P(('dp', 'seq'), 'tensor')
- value_weight_grad: float32 [2048, 512], P(('dp', 'seq'), 'tensor')
- output_weight_grad: float32 [2048, 2048], P('tensor', ('dp', 'seq'))
- query_down_grad: float32 [2048, 8], replicated
- query_up_grad: float32 [8, 2048], P(None, 'tensor')
- key_down_grad: float32 [2048, 8], replicated
- key_up_grad: float32 [8, 512], P(None, 'tensor')
- value_down_grad: float32 [2048, 8], replicated
- value_up_grad: float32 [8, 512], P(None, 'tensor')
- output_down_grad: float32 [2048, 8], P('tensor')
- output_up_grad: float32 [8, 2048], replicated
- query_features_grad: float32 [32, 64, 64], P('tensor')
- key_features_grad: float32 [32, 64, 64], P('tensor')
- feedforward_gain_grad: float32 [2048], replicated
- gate_weight_grad: float32 [2048, 8192], P(('dp', 'seq'), 'tensor')
- up_weight_grad: float32 [2048, 8192], P(('dp', 'seq'), 'tensor')
- down_weight_grad: float32 [8192, 2048], P('tensor', ('dp', 'seq'))
Inputs may be any that keep to these rules, and one draw needn't show every extreme that they name: `doc_lengths`: row g lists the lengths of group g's 2 documents in order; they sum to 2048, and one of them, the first or the second, is shorter than 256.
All inputs are finite; a program needn't handle non-finite values.
Results may differ from a plain program's by a relative error of at most 0.02.
The roundings to bfloat16 on the way count: a program that leaves them out, or rounds other values in their place, can miss the bound.
Values may be sent and summed in bfloat16 or wider, within the bound.
A program may use at most 320 MiB of HBM per device.

v0:
```python
import jax
import jax.numpy as jnp
import numpy as np
from jax import lax
from jax.sharding import PartitionSpec as P

HEAD_SIZE = 64
FEATURE_HALF = 64
SOFTMAX_KEYS = 64


EPS = 1e-05
HIGHEST = lax.Precision.HIGHEST
FLOAT = jnp.float32
BFLOAT = jnp.bfloat16


def from_behind(value, axis, steps):
    count = lax.axis_size(axis)
    leading, last = (max(0, -steps), min(count, count - steps))
    return lax.ppermute(value, axis, [(source, source + steps) for source in range(leading, last)])


def prefix(x, axis, combine, identity, reverse):
    count, position = (lax.axis_size(axis), lax.axis_index(axis))
    everything = jax.tree.map(lambda part: lax.all_gather(part, axis), x)
    start = jax.tree.map(
        lambda part, zero: jnp.broadcast_to(jnp.asarray(zero, part.dtype), part.shape), x, identity
    )

    def step(k, before):
        at = count - 1 - k if reverse else k
        reached = at > position if reverse else at < position
        new = combine(before, jax.tree.map(lambda part: part[at], everything))
        return jax.tree.map(lambda a, b: jnp.where(reached, a, b), new, before)

    return lax.fori_loop(0, count, step, start)


def frequencies(head_width):
    inverse = 1.0 / 500000.0 ** (np.arange(0, head_width, 2) / head_width)
    wavelen = 2.0 * np.pi / inverse
    smooth = (8192.0 / wavelen - 1.0) / 3.0
    blended = (1.0 - smooth) * inverse / 32.0 + smooth * inverse
    return np.where(wavelen > 8192.0, inverse / 32.0, np.where(wavelen < 2048.0, inverse, blended))


def rotation(positions, head_width):
    freq_table = jnp.asarray(frequencies(head_width), FLOAT)
    turned = positions.astype(FLOAT)[:, None] * freq_table[None, :]
    doubled = jnp.concatenate([turned, turned], axis=-1)
    return (jnp.cos(doubled), jnp.sin(doubled))


def apply_rotary(values, cosine_table, sine_table):
    half_width = values.shape[-1] // 2
    turned = jnp.concatenate([-values[..., half_width:], values[..., :half_width]], axis=-1)
    return values * cosine_table[:, None, :] + turned * sine_table[:, None, :]


def rotate_back(grad_in, cosine_table, sine_table):
    half_width = grad_in.shape[-1] // 2
    scaled = grad_in * sine_table[:, None, :]
    turned_back = jnp.concatenate([scaled[..., half_width:], -scaled[..., :half_width]], axis=-1)
    return grad_in * cosine_table[:, None, :] + turned_back


def locate(places, lengths):
    doc_ends = jnp.cumsum(lengths)
    passed = places[:, None] >= doc_ends[None, :]
    segment = jnp.sum(passed.astype(jnp.int32), axis=1)
    doc_begin = jnp.sum(jnp.where(passed, lengths[None, :], 0), axis=1)
    return (jnp.where(places < 0, -1, segment), places - doc_begin)


def norm_scale(inputs):
    return lax.rsqrt(jnp.mean(inputs * inputs, axis=-1, keepdims=True) + EPS)


def norm_back(inputs, gain_vec, grad_normed):
    scale_vec = norm_scale(inputs)
    weighted = grad_normed * gain_vec
    grad_inputs = scale_vec * weighted - inputs * scale_vec * scale_vec * scale_vec * jnp.mean(
        weighted * inputs, axis=-1, keepdims=True
    )
    return (grad_inputs, jnp.sum(grad_normed * inputs * scale_vec, axis=0))


def feature_map(mixed_in):
    return jnp.concatenate(
        [jax.nn.softmax(mixed_in, axis=-1), jax.nn.softmax(-mixed_in, axis=-1)], axis=-1
    )


def feature_back(mixed_in, grad_phi):
    half_width = mixed_in.shape[-1]
    first_half = jax.nn.softmax(mixed_in, axis=-1)
    second = jax.nn.softmax(-mixed_in, axis=-1)
    grad_first = grad_phi[..., :half_width]
    grad_second = grad_phi[..., half_width:]
    return first_half * (
        grad_first - jnp.sum(grad_first * first_half, axis=-1, keepdims=True)
    ) - second * (grad_second - jnp.sum(grad_second * second, axis=-1, keepdims=True))


def product(left, right):
    return jnp.dot(left, right, preferred_element_type=FLOAT)


def exact(left, right):
    return jnp.dot(left, right, precision=HIGHEST, preferred_element_type=FLOAT)


def combine(earlier_part, later_part):
    keep_prior = 1.0 - later_part[0]
    return (
        jnp.maximum(earlier_part[0], later_part[0]),
        later_part[1] + keep_prior * earlier_part[1],
        later_part[2] + keep_prior * earlier_part[2],
    )


def on_device(
    hidden_in,
    doc_lengths,
    attention_gain,
    query_weight,
    key_projection,
    value_projection,
    output_weight,
    query_down,
    query_up,
    key_down,
    key_adapter_up,
    value_down,
    value_adapter_up,
    output_down,
    output_up,
    query_feature_maps,
    key_feature_maps,
    feedforward_gain,
    gate_weight,
    up_weight,
    down_weight,
    block_cotangent,
):
    token_row_count = hidden_in.shape[0]
    local_heads = query_feature_maps.shape[0]
    local_kv = key_projection.shape[1] // HEAD_SIZE
    heads_per_group = local_heads // local_kv
    rank_width = query_down.shape[1]
    score_scale = HEAD_SIZE ** (-0.5)
    ext_count = token_row_count + SOFTMAX_KEYS
    first_row = lax.axis_index("seq") * token_row_count
    lengths = doc_lengths[0]
    seg_rows, pos_rows = locate(first_row + jnp.arange(token_row_count, dtype=jnp.int32), lengths)
    seg_rim = locate(first_row - SOFTMAX_KEYS + jnp.arange(SOFTMAX_KEYS, dtype=jnp.int32), lengths)[
        0
    ]
    seg_first = locate(jnp.reshape(first_row - 1, (1,)), lengths)[0][0]
    seg_ext = jnp.concatenate([seg_rim, seg_rows])
    seg_last = seg_rows[token_row_count - 1]
    row_at = jnp.arange(token_row_count)[:, None]
    key_at = jnp.arange(ext_count)[None, :]
    same_doc = seg_rows[:, None] == seg_ext[None, :]
    window = same_doc & (key_at > row_at) & (key_at <= row_at + SOFTMAX_KEYS)
    earlier = same_doc & (key_at <= row_at)
    continuing = (seg_rows == seg_first).astype(FLOAT)[:, None, None]
    carry_mask = ((jnp.arange(ext_count) < token_row_count) & (seg_ext == seg_last)).astype(FLOAT)[
        :, None, None
    ]
    resets = (seg_last != seg_first).astype(FLOAT)
    cosine_table, sine_table = rotation(pos_rows, HEAD_SIZE)
    query_feature_table = query_feature_maps.reshape(
        local_kv, heads_per_group, HEAD_SIZE, FEATURE_HALF
    )
    key_feature_table = key_feature_maps.reshape(local_kv, heads_per_group, HEAD_SIZE, FEATURE_HALF)
    downs = jnp.concatenate([query_down, key_down, value_down], axis=1)
    gathered = (
        lax.all_gather(query_weight, ("dp", "seq"), axis=0, tiled=True),
        lax.all_gather(key_projection, ("dp", "seq"), axis=0, tiled=True),
        lax.all_gather(value_projection, ("dp", "seq"), axis=0, tiled=True),
        lax.all_gather(gate_weight, ("dp", "seq"), axis=0, tiled=True),
        lax.all_gather(up_weight, ("dp", "seq"), axis=0, tiled=True),
        lax.all_gather(output_weight, ("dp", "seq"), axis=1, tiled=True),
        lax.all_gather(down_weight, ("dp", "seq"), axis=1, tiled=True),
    )
    full_query, full_key, full_value, full_gate, full_up, full_output, full_down = gathered
    hidden32 = hidden_in.astype(FLOAT)
    normalized_input = (hidden32 * norm_scale(hidden32) * attention_gain).astype(BFLOAT)
    low_rank = product(normalized_input, downs).astype(BFLOAT)
    low_q = low_rank[:, :rank_width]
    low_k = low_rank[:, rank_width : 2 * rank_width]
    value_adapter_hidden = low_rank[:, 2 * rank_width :]
    query_before_rotation = product(normalized_input, full_query) + product(low_q, query_up)
    query_heads_rows = (
        apply_rotary(
            query_before_rotation.reshape(token_row_count, local_heads, HEAD_SIZE),
            cosine_table,
            sine_table,
        )
        .astype(BFLOAT)
        .reshape(token_row_count, local_kv, heads_per_group, HEAD_SIZE)
    )
    key_before_rotation = product(normalized_input, full_key) + product(low_k, key_adapter_up)
    projected_keys = apply_rotary(
        key_before_rotation.reshape(token_row_count, local_kv, HEAD_SIZE), cosine_table, sine_table
    ).astype(BFLOAT)
    projected_values = (
        (product(normalized_input, full_value) + product(value_adapter_hidden, value_adapter_up))
        .astype(BFLOAT)
        .reshape(token_row_count, local_kv, HEAD_SIZE)
    )
    rim_keys, rim_values = from_behind(
        (
            projected_keys[token_row_count - SOFTMAX_KEYS :],
            projected_values[token_row_count - SOFTMAX_KEYS :],
        ),
        "seq",
        1,
    )
    key_ext = jnp.concatenate([rim_keys, projected_keys], axis=0)
    value_ext = jnp.concatenate([rim_values, projected_values], axis=0)
    value_ext32 = value_ext.astype(FLOAT)

    def recompute():
        mixed_q = jnp.einsum(
            "tkgd,kgdf->tkgf", query_heads_rows, query_feature_table, preferred_element_type=FLOAT
        )
        mixed_k = jnp.einsum(
            "ekd,kgdf->ekgf", key_ext, key_feature_table, preferred_element_type=FLOAT
        )
        phi_q = feature_map(mixed_q).astype(BFLOAT)
        phi_k = feature_map(mixed_k).astype(BFLOAT)
        raw_scores = jnp.einsum(
            "tkgd,ekd->kgte", query_heads_rows, key_ext, preferred_element_type=FLOAT
        )
        linear = jnp.einsum("tkgf,ekgf->kgte", phi_q, phi_k, preferred_element_type=FLOAT)
        window_exp = jnp.where(
            window, jnp.exp(jnp.where(window, score_scale * raw_scores, 0.0)), 0.0
        )
        linear_old = jnp.where(earlier, linear, 0.0)
        return (mixed_q, mixed_k, phi_q, phi_k, window_exp, linear_old)

    mixed_q, mixed_k, phi_q, phi_k, window_exp, linear_old = recompute()
    masked_phi = phi_k * carry_mask.astype(BFLOAT)[..., None]
    new_kv = jnp.einsum("ekgf,ekd->kgfd", masked_phi, value_ext, preferred_element_type=FLOAT)
    new_norm = jnp.sum(masked_phi.astype(FLOAT), axis=0)
    empty = (jnp.zeros((), FLOAT), jnp.zeros_like(new_kv), jnp.zeros_like(new_norm))
    incoming = prefix((resets, new_kv, new_norm), "seq", combine, empty, False)
    state_kv, state_norm = (incoming[1], incoming[2])
    phi_q32 = phi_q.astype(FLOAT)
    numerator = (
        jnp.einsum(
            "kgte,ekd->tkgd", window_exp.astype(BFLOAT), value_ext, preferred_element_type=FLOAT
        )
        + jnp.einsum("kgte,ekd->tkgd", linear_old, value_ext32, precision=HIGHEST)
        + continuing[..., None]
        * jnp.einsum("tkgf,kgfd->tkgd", phi_q32, state_kv, precision=HIGHEST)
    )
    denominator = jnp.sum(window_exp + linear_old, axis=-1).transpose(
        2, 0, 1
    ) + continuing * jnp.einsum("tkgf,kgf->tkg", phi_q32, state_norm, precision=HIGHEST)
    quotient = numerator / denominator[..., None]
    attended = quotient.reshape(token_row_count, local_heads * HEAD_SIZE).astype(BFLOAT)
    branch_part, mid_part = lax.psum(
        (product(attended, full_output), product(attended, output_down)), "tensor"
    )
    low_mid = mid_part.astype(BFLOAT)
    residual = hidden32 + branch_part + product(low_mid, output_up)
    normed_ff = (residual * norm_scale(residual) * feedforward_gain).astype(BFLOAT)
    gate_act = product(normed_ff, full_gate)
    up_act = product(normed_ff, full_up)
    gate_sigmoid = jax.nn.sigmoid(gate_act)
    gate_silu = gate_act * gate_sigmoid
    hidden_units = (gate_silu * up_act).astype(BFLOAT)
    feedforward_sum = lax.psum(
        product(hidden_units, full_down).astype(jnp.bfloat16), "tensor"
    ).astype(jnp.float32)
    block_output = (residual + feedforward_sum).astype(BFLOAT)
    regathered = (
        lax.all_gather(query_weight, ("dp", "seq"), axis=0, tiled=True),
        lax.all_gather(key_projection, ("dp", "seq"), axis=0, tiled=True),
        lax.all_gather(value_projection, ("dp", "seq"), axis=0, tiled=True),
        lax.all_gather(gate_weight, ("dp", "seq"), axis=0, tiled=True),
        lax.all_gather(up_weight, ("dp", "seq"), axis=0, tiled=True),
        lax.all_gather(output_weight, ("dp", "seq"), axis=1, tiled=True),
        lax.all_gather(down_weight, ("dp", "seq"), axis=1, tiled=True),
    )
    back_query, back_key, back_value, back_gate, back_up, back_output, back_down = regathered
    grad_units = product(block_cotangent, back_down.T)
    grad_gate = (
        grad_units * up_act * gate_sigmoid * (1.0 + gate_act * (1.0 - gate_sigmoid))
    ).astype(BFLOAT)
    grad_up = (grad_units * gate_silu).astype(BFLOAT)
    grad_normed_ff = lax.psum(
        product(grad_gate, back_gate.T) + product(grad_up, back_up.T), "tensor"
    )
    grad_res_part, feedforward_gain_grad = norm_back(residual, feedforward_gain, grad_normed_ff)
    grad_residual = block_cotangent.astype(FLOAT) + grad_res_part
    grad_branch = grad_residual.astype(BFLOAT)
    grad_mid = product(grad_branch, output_up.T)
    output_up_grad = product(low_mid.T, grad_branch)
    grad_attended = product(grad_branch, back_output.T) + exact(
        grad_mid, output_down.astype(FLOAT).T
    )
    output_down_grad = exact(attended.astype(FLOAT).T, grad_mid)
    output_weight_full = product(attended.T, grad_branch)
    grad_quotient = grad_attended.reshape(token_row_count, local_kv, heads_per_group, HEAD_SIZE)
    grad_numer = (grad_quotient / denominator[..., None]).astype(BFLOAT)
    grad_denom = -jnp.sum(grad_quotient * quotient, axis=-1) / denominator
    mixed_q, mixed_k, phi_q, phi_k, window_exp, linear_old = recompute()
    phi_q32 = phi_q.astype(FLOAT)
    local_kv_grad = jnp.einsum(
        "tkgf,tkgd->kgfd",
        phi_q * continuing.astype(BFLOAT)[..., None],
        grad_numer,
        preferred_element_type=FLOAT,
    )
    local_norm_grad = jnp.einsum(
        "tkgf,tkg->kgf", phi_q32 * continuing[..., None], grad_denom, precision=HIGHEST
    )
    outgoing = prefix((resets, local_kv_grad, local_norm_grad), "seq", combine, empty, True)
    grad_out_kv, grad_out_norm = (outgoing[1], outgoing[2])
    grad_weights = (
        jnp.einsum("tkgd,ekd->kgte", grad_numer, value_ext, preferred_element_type=FLOAT)
        + grad_denom.transpose(1, 2, 0)[..., None]
    )
    grad_raw = (score_scale * grad_weights * window_exp).astype(BFLOAT)
    grad_linear = jnp.where(earlier, grad_weights, 0.0).astype(BFLOAT)
    grad_numer32 = grad_numer.astype(FLOAT)
    grad_value_ext = (
        jnp.einsum(
            "kgte,tkgd->ekd", window_exp.astype(BFLOAT), grad_numer, preferred_element_type=FLOAT
        )
        + jnp.einsum("kgte,tkgd->ekd", linear_old, grad_numer32, precision=HIGHEST)
        + jnp.einsum("ekgf,kgfd->ekd", masked_phi.astype(FLOAT), grad_out_kv, precision=HIGHEST)
    )
    grad_phi_q = jnp.einsum(
        "kgte,ekgf->tkgf", grad_linear, phi_k, preferred_element_type=FLOAT
    ) + continuing[..., None] * (
        jnp.einsum("tkgd,kgfd->tkgf", grad_numer32, state_kv, precision=HIGHEST)
        + grad_denom[..., None] * state_norm[None]
    )
    grad_phi_k = jnp.einsum(
        "kgte,tkgf->ekgf", grad_linear, phi_q, preferred_element_type=FLOAT
    ) + carry_mask[..., None] * (
        jnp.einsum("ekd,kgfd->ekgf", value_ext32, grad_out_kv, precision=HIGHEST)
        + grad_out_norm[None]
    )
    grad_mixed_q = feature_back(mixed_q, grad_phi_q).astype(BFLOAT)
    grad_mixed_k = feature_back(mixed_k, grad_phi_k).astype(BFLOAT)
    grad_queries = jnp.einsum(
        "kgte,ekd->tkgd", grad_raw, key_ext, preferred_element_type=FLOAT
    ) + jnp.einsum(
        "tkgf,kgdf->tkgd", grad_mixed_q, query_feature_table, preferred_element_type=FLOAT
    )
    grad_key_ext = jnp.einsum(
        "kgte,tkgd->ekd", grad_raw, query_heads_rows, preferred_element_type=FLOAT
    ) + jnp.einsum("ekgf,kgdf->ekd", grad_mixed_k, key_feature_table, preferred_element_type=FLOAT)
    query_table_grad = jnp.einsum(
        "tkgd,tkgf->kgdf", query_heads_rows, grad_mixed_q, preferred_element_type=FLOAT
    )
    key_table_grad = jnp.einsum(
        "ekd,ekgf->kgdf", key_ext, grad_mixed_k, preferred_element_type=FLOAT
    )
    rim_key_grad, rim_value_grad = from_behind(
        (grad_key_ext[:SOFTMAX_KEYS], grad_value_ext[:SOFTMAX_KEYS]), "seq", -1
    )
    grad_keys = grad_key_ext[SOFTMAX_KEYS:].at[token_row_count - SOFTMAX_KEYS :].add(rim_key_grad)
    grad_values = (
        grad_value_ext[SOFTMAX_KEYS:].at[token_row_count - SOFTMAX_KEYS :].add(rim_value_grad)
    )
    grad_query_pre = (
        rotate_back(
            grad_queries.reshape(token_row_count, local_heads, HEAD_SIZE), cosine_table, sine_table
        )
        .reshape(token_row_count, local_heads * HEAD_SIZE)
        .astype(BFLOAT)
    )
    grad_key_pre = (
        rotate_back(grad_keys, cosine_table, sine_table)
        .reshape(token_row_count, local_kv * HEAD_SIZE)
        .astype(BFLOAT)
    )
    grad_value_pre = grad_values.reshape(token_row_count, local_kv * HEAD_SIZE).astype(BFLOAT)
    grad_low_part = jnp.concatenate(
        [
            product(grad_query_pre, query_up.T),
            product(grad_key_pre, key_adapter_up.T),
            product(grad_value_pre, value_adapter_up.T),
        ],
        axis=1,
    )
    grad_normed_part = (
        product(grad_query_pre, back_query.T)
        + product(grad_key_pre, back_key.T)
        + product(grad_value_pre, back_value.T)
    )
    grad_normed_sum, grad_low = lax.psum((grad_normed_part, grad_low_part), "tensor")
    grad_normed = grad_normed_sum + exact(grad_low, downs.astype(FLOAT).T)
    downs_grad = exact(normalized_input.astype(FLOAT).T, grad_low)
    grad_in_part, attention_gain_grad = norm_back(hidden32, attention_gain, grad_normed)
    input_grad = (grad_residual + grad_in_part).astype(BFLOAT)
    query_up_grad = product(low_q.T, grad_query_pre)
    key_up_grad = product(low_k.T, grad_key_pre)
    value_up_grad = product(value_adapter_hidden.T, grad_value_pre)
    shards = (
        lax.psum_scatter(
            product(normalized_input.T, grad_query_pre),
            ("dp", "seq"),
            scatter_dimension=0,
            tiled=True,
        ),
        lax.psum_scatter(
            product(normalized_input.T, grad_key_pre),
            ("dp", "seq"),
            scatter_dimension=0,
            tiled=True,
        ),
        lax.psum_scatter(
            product(normalized_input.T, grad_value_pre),
            ("dp", "seq"),
            scatter_dimension=0,
            tiled=True,
        ),
        lax.psum_scatter(output_weight_full, ("dp", "seq"), scatter_dimension=1, tiled=True),
        lax.psum_scatter(
            product(normed_ff.T, grad_gate), ("dp", "seq"), scatter_dimension=0, tiled=True
        ),
        lax.psum_scatter(
            product(normed_ff.T, grad_up), ("dp", "seq"), scatter_dimension=0, tiled=True
        ),
        lax.psum_scatter(
            product(hidden_units.T, block_cotangent), ("dp", "seq"), scatter_dimension=1, tiled=True
        ),
    )
    summed_small = lax.psum(
        (
            attention_gain_grad,
            feedforward_gain_grad,
            downs_grad,
            query_up_grad,
            key_up_grad,
            value_up_grad,
            output_down_grad,
            output_up_grad,
            query_table_grad,
            key_table_grad,
        ),
        ("dp", "seq"),
    )
    downs_total = summed_small[2]
    return (
        block_output,
        input_grad,
        summed_small[0],
        shards[0],
        shards[1],
        shards[2],
        shards[3],
        downs_total[:, :rank_width],
        summed_small[3],
        downs_total[:, rank_width : 2 * rank_width],
        summed_small[4],
        downs_total[:, 2 * rank_width :],
        summed_small[5],
        summed_small[6],
        summed_small[7],
        summed_small[8].reshape(local_heads, HEAD_SIZE, FEATURE_HALF),
        summed_small[9].reshape(local_heads, HEAD_SIZE, FEATURE_HALF),
        summed_small[1],
        shards[4],
        shards[5],
        shards[6],
    )


def solution(mesh):
    in_specs = (
        P(("dp", "seq"), None),
        P("dp", None),
        P(),
        P(("dp", "seq"), "tensor"),
        P(("dp", "seq"), "tensor"),
        P(("dp", "seq"), "tensor"),
        P("tensor", ("dp", "seq")),
        P(),
        P(None, "tensor"),
        P(),
        P(None, "tensor"),
        P(),
        P(None, "tensor"),
        P("tensor", None),
        P(),
        P("tensor", None, None),
        P("tensor", None, None),
        P(),
        P(("dp", "seq"), "tensor"),
        P(("dp", "seq"), "tensor"),
        P("tensor", ("dp", "seq")),
        P(("dp", "seq"), None),
    )
    out_specs = (
        P(("dp", "seq"), None),
        P(("dp", "seq"), None),
        P(),
        P(("dp", "seq"), "tensor"),
        P(("dp", "seq"), "tensor"),
        P(("dp", "seq"), "tensor"),
        P("tensor", ("dp", "seq")),
        P(),
        P(None, "tensor"),
        P(),
        P(None, "tensor"),
        P(),
        P(None, "tensor"),
        P("tensor", None),
        P(),
        P("tensor", None, None),
        P("tensor", None, None),
        P(),
        P(("dp", "seq"), "tensor"),
        P(("dp", "seq"), "tensor"),
        P("tensor", ("dp", "seq")),
    )
    return jax.shard_map(
        on_device, mesh=mesh, in_specs=in_specs, out_specs=out_specs, check_vma=False
    )
```

profile of v0, /device:TPU:15, one launch (start us, length us, event | category | flops | bytes accessed | tf_op | source)
XLA Modules:
  0.0 2830.5 jit_solution(10453637161343237269)
XLA Ops:
  23.1 22.1 all-gather.16.cloned.1.call-done
  48.9 32.8 %all-gather.14.cloned.1.call-done = bf16[2048,256]{1,0:T(8,128)(2,1)} async-done(((bf16[128,256]{1,0:T(8,128)(2,1)}), bf16[2048,256]{1,0:T(8,128)(2,1)}) %all-gather.14.cloned.1.call-update) | async-done | bytes 1048592 | tf_op jit(solution)/shard_map/all_gather | solution.py:182
  117.7 13.2 all-gather.1
  158.2 19.0 all-gather.28.cloned.1.call-done
  177.2 44.8 %while.36 = (s32[]{:T(128)}, f32[4,4,128,64]{3,2,1,0:T(8,128)}, f32[4,4,128]{2,1,0:T(4,128)S(1)}, s32[]{:T(128)}, f32[8,4,4,128,64]{3,4,2,1,0:T(8,128)}, /*index...) while((s32[]{:T(128)}, f32[4,4,128,64]{3,2,1,0:T(8,128)}, ...), condition=%wide.region_16.17_spmd.clone, body=%wide.region_15.16_spmd.clone.sunk | while | flops 532485 | bytes 3694763 | solution.py:37
  228.2 12.5 all-gather.20.cloned.1.call-done
  257.1 55.2 %all-reduce.10.cloned.1.call-done = f32[256,2048]{1,0:T(8,128)} async-done(((f32[256,2048]{1,0:T(8,128)}), f32[256,2048]{1,0:T(8,128)}) %all-reduce.10.cloned.1.call-update) | async-done | bytes 2097168 | tf_op jit(solution)/shard_map/psum | solution.py:266
  316.4 129.8 %all-gather.22.cloned.1.call-done = bf16[2048,4096]{1,0:T(8,128)(2,1)} async-done(((bf16[128,4096]{1,0:T(8,128)(2,1)}), bf16[2048,4096]{1,0:T(8,128)(2,1)}) %all-gather.22.cloned.1.call-update) | async-done | bytes 16777232 | tf_op jit(solution)/shard_map/all_gather | solution.py:183
  446.2 12.5 fusion.198
  458.7 124.5 %all-gather.24.cloned.1.call-done = bf16[2048,4096]{1,0:T(8,128)(2,1)} async-done(((bf16[128,4096]{1,0:T(8,128)(2,1)}), bf16[2048,4096]{1,0:T(8,128)(2,1)}) %all-gather.24.cloned.1.call-update) | async-done | bytes 16777232 | tf_op jit(solution)/shard_map/all_gather | solution.py:184
  583.2 12.6 fusion.199
  595.8 165.4 %all-gather.26.cloned.1.call-done = bf16[4096,2048]{1,0:T(8,128)(2,1)} async-done(((bf16[4096,128]{1,0:T(8,128)(2,1)}), bf16[4096,2048]{1,0:T(8,128)(2,1)}) %all-gather.26.cloned.1.call-update) | async-done | bytes 16777232 | tf_op jit(solution)/shard_map/all_gather | solution.py:186
  761.2 13.5 multiply_convert_fusion.1
  787.0 12.8 convolution_add_fusion.4
  800.1 69.9 %all-reduce.14.cloned.1.call-done = f32[256,2048]{1,0:T(8,128)} async-done(((f32[256,2048]{1,0:T(8,128)}), f32[256,2048]{1,0:T(8,128)}) %all-reduce.14.cloned.1.call-update) | async-done | bytes 2097168 | tf_op jit(solution)/shard_map/psum | solution.py:296
  923.7 39.8 %while.37 = (s32[]{:T(128)}, f32[4,4,128,64]{3,2,1,0:T(8,128)}, f32[4,4,128]{2,1,0:T(4,128)S(1)}, s32[]{:T(128)}, f32[8,4,4,128,64]{3,4,2,1,0:T(8,128)}, /*index...) while((s32[]{:T(128)}, f32[4,4,128,64]{3,2,1,0:T(8,128)}, ...), condition=%wide.region_28.29_spmd.clone, body=%wide.region_27.28_spmd.clone.sunk | while | flops 532489 | bytes 3694825 | solution.py:37
  972.4 29.1 %fusion.4 = f32[320,4,4,64]{3,0,2,1:T(8,128)} fusion(f32[320,4,4,128]{3,0,2,1:T(8,128)S(1)} %add_bitcast_fusion, f32[320,4,4,64]{3,0,2,1:T(8,128)S(1)} %copy-done.20, f32[320,4,4]{0,2,1:T(4,128)S(1)} %copy-done.77), kind=kOutput, calls=%fused_computation.10 | output fusion | flops 660543 | bytes 5263360 | tf_op jit(solution)/shard_map/sub | solution.py:103
  1001.5 36.0 %fusion.79 = f32[320,4,64]{0,2,1:T(8,128)S(1)} fusion(f32[320,4,64]{0,2,1:T(8,128)} %convolution_bitcast_fusion.5, bf16[4,4,64,64]{3,2,1,0:T(8,128)(2,1)} %bitcast.350, f32[320,4,4,64]{3,0,2,1:T(8,128)} %fusion.4, f32[320,4,4,128]{3,0,2,1:T(8,128)} %copy-done.36, f32[320,4,4,64]{3,0,2,1:T(8,128)} %copy-done.18, f32[320,4,4]{0,2,1:T(4,128)} %copy-done.75, ...), kind=kOutput, calls=%fused_computation.122 | convolution fusion | flops 45306944 | bytes 19402752 | tf_op jit(solution)/shard_map/ekgf,kgdf->ekd/dot_general | solution.py:360
  1062.7 37.3 %fusion.53 = f32[4,4,64,64]{3,2,1,0:T(8,128)S(1)} fusion(f32[320,4,4,64]{3,0,2,1:T(8,128)} %fusion.4, f32[320,4,4,128]{3,0,2,1:T(8,128)} %copy-done.36, bf16[256,4,64]{0,2,1:T(8,128)(2,1)S(1)} %copy-done.35, bf16[64,4,64]{0,2,1:T(8,128)(2,1)} %copy-done.60, f32[320,4,4,64]{3,0,2,1:T(8,128)} %copy-done.18, f32[320,4,4]{0,2,1:T(4,128)} %copy-done.75, ...), kind=kOutput, calls=%fused_computation.90 | convolution fusion | flops 45552704 | bytes 18882560 | tf_op jit(solution)/shard_map/ekd,ekgf->kgdf/dot_general | solution.py:364
  1149.1 14.8 fusion.209
  1164.3 14.9 fusion.210
  1180.4 15.0 fusion.211
  1195.4 57.5 %all-reduce.20.cloned.1.call-done = (f32[2048,24]{0,1:T(8,128)}, f32[8,2048]{1,0:T(8,128)}, f32[16,64,64]{2,1,0:T(8,128)}, f32[16,64,64]{2,1,0:T(8,128)}) async-done(((f32[2048,24]{0,1:T(8,128)}, f32[8,2048]{1,0:T(8,128)}, f32[16,64,64]{2,1,0:T(8,128)}, f32[16,64,64]{2,1,0:T(8,128)}), (f32[2048,24]{0,1:T(8,128)}, f32[8,2048]{1,0:T(8,128)}, f32[16,64,64]{2,1,0:T(8,128)}, ...) | async-done | bytes 786448 | tf_op jit(solution)/shard_map/psum | solution.py:438
  1254.5 41.7 %all-reduce.12.cloned.1.call-done = bf16[256,2048]{1,0:T(8,128)(2,1)} async-done(((bf16[256,2048]{1,0:T(8,128)(2,1)}), bf16[256,2048]{1,0:T(8,128)(2,1)}) %all-reduce.12.cloned.1.call-update) | async-done | bytes 1048592 | tf_op jit(solution)/shard_map/psum | solution.py:277
  1300.7 115.8 %all-reduce.18.cloned.1.call-done = (f32[2048]{0:T(1024)}, f32[8,1024]{1,0:T(8,128)}, f32[8,256]{1,0:T(8,128)}, f32[8,256]{1,0:T(8,128)}, f32[1024,8]{0,1:T(8,128)}, /*index=5*/f32[2048]{0:T(1024)}) async-done(((f32[2048]{0:T(1024)}, f32[8,1024]{1,0:T(8,128)}, f32[8,256]{1,0:T(8,128)}, f32[8,256]{1,0:T(8,128)}, f32[1024,8]{0,1:T(8,128)}, /*index=5*/f32[2048]{0:T(1024)}), (f32[2048]{0:T(1024)}, ...) | async-done | bytes 98320 | tf_op jit(solution)/shard_map/psum | solution.py:438
  1416.5 66.9 %reduce-scatter.10.cloned.1.call-done = f32[128,256]{1,0:T(8,128)} async-done(((f32[2048,256]{1,0:T(8,128)}), f32[128,256]{1,0:T(8,128)}) %reduce-scatter.10.cloned.1.call-update) | async-done | bytes 131088 | tf_op jit(solution)/shard_map/reduce_scatter | solution.py:415
  1483.5 67.9 %reduce-scatter.12.cloned.1.call-done = f32[128,256]{1,0:T(8,128)} async-done(((f32[2048,256]{1,0:T(8,128)}), f32[128,256]{1,0:T(8,128)}) %reduce-scatter.12.cloned.1.call-update) | async-done | bytes 131088 | tf_op jit(solution)/shard_map/reduce_scatter | solution.py:421
  1551.3 98.0 %reduce-scatter.8.cloned.1.call-done = f32[128,1024]{1,0:T(8,128)} async-done(((f32[2048,1024]{1,0:T(8,128)}), f32[128,1024]{1,0:T(8,128)}) %reduce-scatter.8.cloned.1.call-update) | async-done | bytes 524304 | tf_op jit(solution)/shard_map/reduce_scatter | solution.py:409
  1649.3 99.9 %reduce-scatter.14.cloned.1.call-done = f32[1024,128]{1,0:T(8,128)} async-done(((f32[1024,2048]{1,0:T(8,128)}), f32[1024,128]{1,0:T(8,128)}) %reduce-scatter.14.cloned.1.call-update) | async-done | bytes 524304 | tf_op jit(solution)/shard_map/reduce_scatter | solution.py:427
  1749.2 351.4 %reduce-scatter.16.cloned.1.call-done = f32[128,4096]{1,0:T(8,128)} async-done(((f32[2048,4096]{1,0:T(8,128)}), f32[128,4096]{1,0:T(8,128)}) %reduce-scatter.16.cloned.1.call-update) | async-done | bytes 2097168 | tf_op jit(solution)/shard_map/reduce_scatter | solution.py:428
  2100.6 355.1 %reduce-scatter.18.cloned.1.call-done = f32[128,4096]{1,0:T(8,128)} async-done(((f32[2048,4096]{1,0:T(8,128)}), f32[128,4096]{1,0:T(8,128)}) %reduce-scatter.18.cloned.1.call-update) | async-done | bytes 2097168 | tf_op jit(solution)/shard_map/reduce_scatter | solution.py:431
  2455.8 355.1 %reduce-scatter.20.cloned.1.call-done = f32[4096,128]{1,0:T(8,128)} async-done(((f32[4096,2048]{1,0:T(8,128)}), f32[4096,128]{1,0:T(8,128)}) %reduce-scatter.20.cloned.1.call-update) | async-done | bytes 2097168 | tf_op jit(solution)/shard_map/reduce_scatter | solution.py:434
  (524 shorter events, 349.3 us)
Async XLA Ops:
  7.2 137.2 %copy-start = (bf16[16,64,64]{2,1,0:T(8,128)(2,1)S(1)}, bf16[16,64,64]{2,1,0:T(8,128)(2,1)}, u32[]{:S(2)}) copy-start(bf16[16,64,64]{2,1,0:T(8,128)(2,1)} %param.46) | copy-start | bytes 393220
  7.2 38.1 %all-gather.16.cloned.1.call-start = ((), (), s32[]{:S(2)}) async-start(), calls=%async_computation.8 | async-start | bytes 1114112 | tf_op jit(solution)/shard_map/all_gather | solution.py:181
  8.0 73.8 %all-gather.14.cloned.1.call-start = ((), (), s32[]{:S(2)}) async-start(), calls=%async_computation.7 | async-start | bytes 1114112 | tf_op jit(solution)/shard_map/all_gather | solution.py:182
  8.7 126.6 %all-gather.18.cloned.1.call-start = ((), (), s32[]{:S(2)}) async-start(), calls=%async_computation.9 | async-start | bytes 4456448 | tf_op jit(solution)/shard_map/all_gather | solution.py:180
  9.4 167.7 %all-gather.28.cloned.1.call-start = ((), (), s32[]{:S(2)}) async-start(), calls=%async_computation.25 | async-start | bytes 4718592 | tf_op jit(solution)/shard_map/all_gather | solution.py:26
  12.9 211.4 %copy-start.104 = (f32[256]{0:T(256)}, f32[256]{0:T(256)S(1)}, u32[]{:S(2)}) copy-start(f32[256]{0:T(256)S(1)} %get-tuple-element.514) | copy-start | bytes 3076
  17.5 126.5 %copy-start.45 = (f32[256,64]{0,1:T(8,128)}, f32[256,64]{0,1:T(8,128)S(1)}, u32[]{:S(2)}) copy-start(f32[256,64]{0,1:T(8,128)S(1)} %get-tuple-element.535) | copy-start | bytes 196612
  47.6 37.6 %collective-permute-start.1 = (bf16[64,4,64]{0,2,1:T(8,128)(2,1)S(1)}, bf16[64,4,64]{0,2,1:T(8,128)(2,1)S(1)}, u32[]{:S(2)}, u32[]{:S(2)}) collective-permute-start(bf16[64,4,64]{0,2,1:T(8,128)(2,1)S(1)} %slice.161), channel_id=1, source_target_pairs={{0,2},{2,4},{4,6},{6,8},{8,10},{10,12},{12,14},{1,3},{3,5},{5,7},{... | collective-permute-start | bytes 98312 | tf_op jit(solution)/shard_map/ppermute | solution.py:21
  84.0 15.7 collective-permute-start
  101.1 139.6 %all-gather.20.cloned.1.call-start = ((), (), s32[]{:S(2)}) async-start(), calls=%async_computation.10 | async-start | bytes 4456448 | tf_op jit(solution)/shard_map/all_gather | solution.py:185
  101.7 210.7 %all-reduce.10.cloned.1.call-start = ((), (), s32[]{:S(2)}) async-start(), calls=%async_computation.11 | async-start | bytes 4194304 | tf_op jit(solution)/shard_map/psum | solution.py:266
  245.5 200.6 %all-gather.22.cloned.1.call-start = ((), (), s32[]{:S(2)}) async-start(), calls=%async_computation.12 | async-start | bytes 17825792 | tf_op jit(solution)/shard_map/all_gather | solution.py:183
  246.3 336.9 %all-gather.24.cloned.1.call-start = ((), (), s32[]{:S(2)}) async-start(), calls=%async_computation.13 | async-start | bytes 17825792 | tf_op jit(solution)/shard_map/all_gather | solution.py:184
  247.0 514.2 %all-gather.26.cloned.1.call-start = ((), (), s32[]{:S(2)}) async-start(), calls=%async_computation.14 | async-start | bytes 17825792 | tf_op jit(solution)/shard_map/all_gather | solution.py:186
  247.8 622.3 %all-reduce.14.cloned.1.call-start = ((), (), s32[]{:S(2)}) async-start(), calls=%async_computation.16 | async-start | bytes 4194304 | tf_op jit(solution)/shard_map/psum | solution.py:296
  314.6 558.4 %copy-start.3 = (f32[256,2048]{1,0:T(8,128)}, f32[256,2048]{1,0:T(8,128)S(1)}, u32[]{:S(2)}) copy-start(f32[256,2048]{1,0:T(8,128)S(1)} %get-tuple-element.553) | copy-start | bytes 6291460
  799.9 123.9 %all-gather.30.cloned.1.call-start = ((), (), s32[]{:S(2)}) async-start(), calls=%async_computation.26 | async-start | bytes 4718592 | tf_op jit(solution)/shard_map/all_gather | solution.py:26
  881.5 247.9 %all-reduce.16.cloned.1.call-start = ((), (), s32[]{:S(2)}) async-start(), calls=%async_computation.17 | async-start | bytes 4194304 | tf_op jit(solution)/shard_map/psum | solution.py:400
  1038.3 11.5 collective-permute-start.2
  1046.5 4.5 collective-permute-start.3
  1056.4 196.5 %all-reduce.20.cloned.1.call-start = ((), (), s32[]{:S(2)}) async-start(), calls=%async_computation.28 | async-start | bytes 2621440 | tf_op jit(solution)/shard_map/psum | solution.py:438
  1111.6 184.6 %all-reduce.12.cloned.1.call-start = ((), (), s32[]{:S(2)}) async-start(), calls=%async_computation.15 | async-start | bytes 2097152 | tf_op jit(solution)/shard_map/psum | solution.py:277
  1123.8 292.7 %all-reduce.18.cloned.1.call-start = ((), (), s32[]{:S(2)}) async-start(), calls=%async_computation.27 | async-start | bytes 196608 | tf_op jit(solution)/shard_map/psum | solution.py:438
  1134.5 349.0 %reduce-scatter.10.cloned.1.call-start = ((), (), s32[]{:S(2)}) async-start(), calls=%async_computation.19 | async-start | bytes 2228224 | tf_op jit(solution)/shard_map/reduce_scatter | solution.py:415
  1136.5 414.8 %reduce-scatter.12.cloned.1.call-start = ((), (), s32[]{:S(2)}) async-start(), calls=%async_computation.20 | async-start | bytes 2228224 | tf_op jit(solution)/shard_map/reduce_scatter | solution.py:421
  1138.5 510.8 %reduce-scatter.8.cloned.1.call-start = ((), (), s32[]{:S(2)}) async-start(), calls=%async_computation.18 | async-start | bytes 8912896 | tf_op jit(solution)/shard_map/reduce_scatter | solution.py:409
  1143.3 605.9 %reduce-scatter.14.cloned.1.call-start = ((), (), s32[]{:S(2)}) async-start(), calls=%async_computation.21 | async-start | bytes 8912896 | tf_op jit(solution)/shard_map/reduce_scatter | solution.py:427
  1147.9 952.7 %reduce-scatter.16.cloned.1.call-start = ((), (), s32[]{:S(2)}) async-start(), calls=%async_computation.22 | async-start | bytes 35651584 | tf_op jit(solution)/shard_map/reduce_scatter | solution.py:428
  1164.0 1291.8 %reduce-scatter.18.cloned.1.call-start = ((), (), s32[]{:S(2)}) async-start(), calls=%async_computation.23 | async-start | bytes 35651584 | tf_op jit(solution)/shard_map/reduce_scatter | solution.py:431
  1179.2 1631.7 %reduce-scatter.20.cloned.1.call-start = ((), (), s32[]{:S(2)}) async-start(), calls=%async_computation.24 | async-start | bytes 35651584 | tf_op jit(solution)/shard_map/reduce_scatter | solution.py:434
  1296.2 1521.3 %copy-start.87 = (f32[8,2048]{1,0:T(8,128)S(1)}, f32[8,2048]{1,0:T(8,128)}, u32[]{:S(2)}) copy-start(f32[8,2048]{1,0:T(8,128)} %get-tuple-element.727) | copy-start | bytes 196612
  1296.2 1527.0 %copy-start.1 = (bf16[16,64,64]{2,1,0:T(8,128)(2,1)S(1)}, bf16[16,64,64]{2,1,0:T(8,128)(2,1)}, u32[]{:S(2)}) copy-start(bf16[16,64,64]{2,1,0:T(8,128)(2,1)} %param.46) | copy-start | bytes 393220
  (115 other events, 2113.1 us)
Sparse Core Ops, SparseCore 0:
  10.4 34.8 all-gather.15
  47.6 34.1 all-gather.13
  84.1 51.1 all-gather.17
  137.6 39.4 all-gather.27
  179.3 61.4 all-gather.19
  245.7 66.6 all-reduce.9
  314.9 131.1 all-gather.21
  448.7 134.4 all-gather.23
  585.8 175.4 all-gather.25
  800.0 70.0 all-reduce.13
  881.7 37.4 all-gather.29
  1056.5 66.2 all-reduce.15
  1127.4 125.4 all-reduce.19
  1255.8 40.3 all-reduce.11
  1300.5 115.9 all-reduce.17
  1419.3 64.0 reduce-scatter.9
  1486.2 65.0 reduce-scatter.11
  1554.2 95.1 reduce-scatter.7
  1652.3 96.8 reduce-scatter.13
  1752.1 348.4 reduce-scatter.15
  2103.7 352.0 reduce-scatter.17
  2458.8 351.9 reduce-scatter.19
where the time goes:
time: 2850 us; the launch traced here: 2830 us
  waiting for transfers between devices  2250 us (79%)
  matrix products  312 us (11%)
  other arithmetic  107 us (4%)
  local copies, waits for them, and re-layouts  71.8 us (3%)
  blocking collectives  51.5 us (2%)
    reduce_scatter x1, waiting for transfers between devices, on_device(): lax.psum_scatter(product(normed_ff.T, grad_up), ('dp', 'seq'), scatter_di...  355 us
    reduce_scatter x1, waiting for transfers between devices, on_device(): lax.psum_scatter(product(hidden_units.T, block_cotangent), ('dp', 'seq'),...  355 us
    reduce_scatter x1, waiting for transfers between devices, on_device(): lax.psum_scatter(product(normed_ff.T, grad_gate), ('dp', 'seq'), scatter_...  351 us
    psum x2, waiting for transfers between devices, on_device(): lax.psum((attention_gain_grad, feedforward_gain_grad, downs_grad, query_u...  173 us
    dot_general x35, matrix products, product(): return jnp.dot(left, right, preferred_element_type=FLOAT)  168 us
    all_gather x1, waiting for transfers between devices, on_device(): lax.all_gather(down_weight, ('dp', 'seq'), axis=1, tiled=True)  165 us
    all_gather x1, waiting for transfers between devices, on_device(): lax.all_gather(gate_weight, ('dp', 'seq'), axis=0, tiled=True)  130 us
    all_gather x1, waiting for transfers between devices, on_device(): lax.all_gather(up_weight, ('dp', 'seq'), axis=0, tiled=True)  125 us
  transfers between devices with their start and end apart: 26, of which 20 were waited for; matrix products, arithmetic and copies ran while one was open for 11% of the time, Pallas kernels for 0%

commit v1 on v0

v1 whole, which is shorter than its diff:
```python
import functools

import jax
import jax.numpy as jnp
import numpy as np
from jax import lax
from jax.experimental import pallas as pl
from jax.experimental.pallas import tpu as pltpu
from jax.sharding import Mesh
from jax.sharding import PartitionSpec as P

HEAD_SIZE = 64
FEATURE_HALF = 64
SOFTMAX_KEYS = 64
CORES = 2


EPS = 1e-05
FLOAT = jnp.float32
BFLOAT = jnp.bfloat16


def swap(value, axis, mask=1):
    count = lax.axis_size(axis)
    return lax.ppermute(value, axis, [(source, source ^ mask) for source in range(count)])


def bit(axis, mask=1):
    return (lax.axis_index(axis) // mask) % 2


def ordered(which, mine, other, dim):
    return jnp.where(
        which == 0,
        jnp.concatenate([mine, other], axis=dim),
        jnp.concatenate([other, mine], axis=dim),
    )


def take(value, index, dim):
    return lax.dynamic_index_in_dim(value, index, dim, keepdims=True)


def cube_dims():
    chips = lax.axis_size("chip")
    masks = []
    mask = chips // 2
    while mask >= 1:
        masks.append(("chip", mask))
        mask //= 2
    return [("dp", 1)] + masks


def cube_orders():
    count = len(cube_dims())
    inner = list(range(1, count))
    return ([0] + inner, [0] + inner[::-1])


def gather_blocks(block, order):
    dims = cube_dims()
    value = block.reshape((1,) * len(dims) + block.shape)
    for dim in order:
        axis, mask = dims[dim]
        value = ordered(bit(axis, mask), value, swap(value, axis, mask), dim)
    return value.reshape((-1,) + block.shape)


def scatter_blocks(value, order):
    dims = cube_dims()
    block = value.shape[1:]
    value = value.reshape((2,) * len(dims) + block)
    for dim in order:
        axis, mask = dims[dim]
        which = bit(axis, mask)
        send = take(value, 1 - which, dim).astype(BFLOAT)
        value = take(value, which, dim).astype(FLOAT) + swap(send, axis, mask).astype(FLOAT)
    return value.reshape(block)


def token_orders():
    masks = [dim for dim in cube_dims() if dim[0] == "chip"]
    return (masks[::-1], masks)


def gather_tokens(rows, order):
    for axis, mask in order:
        rows = jnp.concatenate([rows, swap(rows, axis, mask)], axis=0)
    return rows, swap(rows, "core")


def scatter_tokens(rows, sibling_rows, order):
    rows = rows.astype(FLOAT) + swap(sibling_rows, "core").astype(FLOAT)
    for axis, mask in order[::-1]:
        half = rows.shape[0] // 2
        send = rows[half:].astype(BFLOAT)
        rows = rows[:half] + swap(send, axis, mask).astype(FLOAT)
    return rows


def pair_sum(value, axis, mask=1):
    sent = value.astype(BFLOAT)
    return sent.astype(FLOAT) + swap(sent, axis, mask).astype(FLOAT)


def frequencies(head_width):
    inverse = 1.0 / 500000.0 ** (np.arange(0, head_width, 2) / head_width)
    wavelen = 2.0 * np.pi / inverse
    smooth = (8192.0 / wavelen - 1.0) / 3.0
    blended = (1.0 - smooth) * inverse / 32.0 + smooth * inverse
    return np.where(wavelen > 8192.0, inverse / 32.0, np.where(wavelen < 2048.0, inverse, blended))


def rotation(positions, head_width):
    freq_table = jnp.asarray(frequencies(head_width), FLOAT)
    turned = positions.astype(FLOAT)[:, None] * freq_table[None, :]
    cosine, sine = jnp.cos(turned), jnp.sin(turned)
    return (
        jnp.concatenate([cosine, cosine], axis=-1),
        jnp.concatenate([-sine, sine], axis=-1),
    )


def turn(values):
    width = values.shape[1]
    half = HEAD_SIZE // 2
    first = (lax.broadcasted_iota(jnp.int32, (1, width), 1) % HEAD_SIZE) < half
    return jnp.where(first, jnp.roll(values, -half, axis=1), jnp.roll(values, half, axis=1))


def spread(table, width):
    return jnp.tile(table, (1, width // table.shape[1]))


def apply_rotary(values, cosine_table, sine_table):
    width = values.shape[1]
    return values * spread(cosine_table, width) + turn(values) * spread(sine_table, width)


def rotate_back(grad_in, cosine_table, sine_table):
    width = grad_in.shape[1]
    return grad_in * spread(cosine_table, width) - turn(grad_in) * spread(sine_table, width)


def locate(places, lengths):
    doc_ends = jnp.cumsum(lengths)
    passed = places[:, None] >= doc_ends[None, :]
    segment = jnp.sum(passed.astype(jnp.int32), axis=1)
    doc_begin = jnp.sum(jnp.where(passed, lengths[None, :], 0), axis=1)
    return (jnp.where(places < 0, -1, segment), places - doc_begin)


def norm_scale(inputs):
    return lax.rsqrt(jnp.mean(inputs * inputs, axis=-1, keepdims=True) + EPS)


def norm_back(inputs, gain_vec, grad_normed):
    scale_vec = norm_scale(inputs)
    weighted = grad_normed * gain_vec
    grad_inputs = scale_vec * weighted - inputs * scale_vec * scale_vec * scale_vec * jnp.mean(
        weighted * inputs, axis=-1, keepdims=True
    )
    return (grad_inputs, jnp.sum(grad_normed * inputs * scale_vec, axis=0))


def product(left, right):
    return jnp.dot(left, right, preferred_element_type=FLOAT)


def product_t(left, right):
    return lax.dot_general(left, right, (((1,), (1,)), ((), ())), preferred_element_type=FLOAT)


def t_product(left, right):
    return lax.dot_general(left, right, (((0,), (0,)), ((), ())), preferred_element_type=FLOAT)


def dot(left, right):
    return lax.dot_general(left, right, (((1,), (0,)), ((), ())), preferred_element_type=FLOAT)


def lanes(shape):
    return lax.broadcasted_iota(jnp.int32, shape, 1)


def half_sums(rows):
    first = lax.broadcasted_iota(jnp.int32, (128, 128), 0) < FEATURE_HALF
    ones = jnp.where(first == (lanes((128, 128)) < FEATURE_HALF), 1.0, 0.0).astype(BFLOAT)
    return dot(rows, ones)


def two_softmax(mixed):
    low = lanes(mixed.shape) < FEATURE_HALF
    top = jnp.max(jnp.where(low, mixed, -jnp.inf), axis=1, keepdims=True)
    top_other = jnp.max(jnp.where(low, -jnp.inf, mixed), axis=1, keepdims=True)
    raised = jnp.exp(mixed - jnp.where(low, top, top_other))
    return (raised / half_sums(raised.astype(BFLOAT))).astype(BFLOAT)


def phi_kernel(group, q_ref, k_ref, vm_ref, fq_ref, fk_ref, phi_q_ref, phi_k_ref, state_ref):
    keys = k_ref[0]
    masked = vm_ref[0]
    for head in range(group):
        rows = q_ref[:, head * HEAD_SIZE : (head + 1) * HEAD_SIZE]
        phi_q_ref[head] = two_softmax(dot(rows, fq_ref[head]))
        phi_k = two_softmax(dot(keys, fk_ref[head]))
        phi_k_ref[head] = phi_k
        state_ref[head] = t_product(masked, phi_k).astype(BFLOAT)


def tile_masks(seg_q, seg_k, at):
    width = at + 256
    same = seg_q == seg_k[:, :width]
    row = lax.broadcasted_iota(jnp.int32, (128, 256), 0)
    col = lanes((128, 256))
    earlier = col <= row + SOFTMAX_KEYS
    window = (col > row + SOFTMAX_KEYS) & (col <= row + 128) & same[:, at:]
    return same[:, :at], window, earlier & same[:, at:]


def tile_weights(rows, phi_rows, k_ref, phi_k, at, masks):
    far, window, earlier = masks
    scale = HEAD_SIZE ** (-0.5)
    raw = product_t(rows, k_ref[0, at : at + 256])
    window_exp = jnp.where(window, jnp.exp(jnp.where(window, scale * raw, 0.0)), 0.0)
    linear = product_t(phi_rows, phi_k[: at + 256])
    near = jnp.where(earlier, linear[:, at:], window_exp)
    if at == 0:
        return window_exp, near.astype(BFLOAT)
    return window_exp, jnp.concatenate(
        [jnp.where(far, linear[:, :at], 0.0), near], axis=1
    ).astype(BFLOAT)


def intra_kernel(group, q_ref, k_ref, v_ref, phi_q_ref, phi_k_ref, seg_q_ref, seg_k_ref, num_ref):
    for at in range(0, q_ref.shape[0], 128):
        masks = tile_masks(seg_q_ref[at : at + 128], seg_k_ref[...], at)
        for head in range(group):
            rows = q_ref[at : at + 128, head * HEAD_SIZE : (head + 1) * HEAD_SIZE]
            weights = tile_weights(
                rows, phi_q_ref[head, at : at + 128], k_ref, phi_k_ref.at[head], at, masks
            )[1]
            num_ref[head, at : at + 128] = dot(weights, v_ref[0, : at + 256])


def finish_kernel(group, num_ref, phi_q_ref, state_ref, cont_ref, att_ref, den_ref):
    cont = cont_ref[...]
    den = jnp.zeros(den_ref.shape[1:], FLOAT)
    for head in range(group):
        total = num_ref[head] + cont * product_t(phi_q_ref[head], state_ref[head])
        below = total[:, HEAD_SIZE : HEAD_SIZE + 1]
        att_ref[:, head * HEAD_SIZE : (head + 1) * HEAD_SIZE] = (
            total[:, :HEAD_SIZE] / below
        ).astype(BFLOAT)
        den = jnp.where(lanes(den.shape) == head, below, den)
    den_ref[0] = den


def grad_numer_kernel(group, da_ref, att_ref, den_ref, phi_q_ref, cont_ref, dn_ref, ds_ref):
    cont = cont_ref[...]
    for head in range(group):
        cols = slice(head * HEAD_SIZE, (head + 1) * HEAD_SIZE)
        numer = da_ref[:, cols] / den_ref[0][:, head : head + 1]
        denom = -jnp.sum(numer * att_ref[:, cols].astype(FLOAT), axis=1, keepdims=True)
        high = denom.astype(BFLOAT).astype(FLOAT)
        wide = jnp.concatenate([numer, jnp.zeros_like(numer)], axis=1)
        lane = lanes(wide.shape)
        wide = jnp.where(lane == HEAD_SIZE, high, wide)
        wide = jnp.where(lane == HEAD_SIZE + 1, denom - high, wide)
        dn_ref[head] = wide.astype(BFLOAT)
        state = t_product((wide * cont).astype(BFLOAT), phi_q_ref[head])
        row = lax.broadcasted_iota(jnp.int32, state.shape, 0)
        both = state[HEAD_SIZE : HEAD_SIZE + 1] + state[HEAD_SIZE + 1 : HEAD_SIZE + 2]
        state = jnp.where(row == HEAD_SIZE, both, jnp.where(row > HEAD_SIZE, 0.0, state))
        ds_ref[head] = state.astype(BFLOAT)


def intra_back_kernel(
    group, q_ref, k_ref, v_ref, phi_q_ref, phi_k_ref, dn_ref, seg_q_ref, seg_k_ref,
    dq_ref, dk_ref, dv_ref, dphi_q_ref, dphi_k_ref,
):
    scale = HEAD_SIZE ** (-0.5)
    dk_ref[...] = jnp.zeros(dk_ref.shape, FLOAT)
    dv_ref[...] = jnp.zeros(dv_ref.shape, FLOAT)
    dphi_k_ref[...] = jnp.zeros(dphi_k_ref.shape, FLOAT)
    for at in range(0, q_ref.shape[0], 128):
        masks = tile_masks(seg_q_ref[at : at + 128], seg_k_ref[...], at)
        tile = slice(at, at + 128)
        width = at + 256
        for head in range(group):
            cols = slice(head * HEAD_SIZE, (head + 1) * HEAD_SIZE)
            rows = q_ref[tile, cols]
            phi_rows = phi_q_ref[head, tile]
            numer = dn_ref[head, tile]
            window_exp, weights = tile_weights(
                rows, phi_rows, k_ref, phi_k_ref.at[head], at, masks
            )
            grad = product_t(numer, v_ref[0, :width])
            near = grad[:, at:]
            grad_raw = (scale * near * window_exp).astype(BFLOAT)
            grad_linear = jnp.where(masks[2], near, 0.0)
            if at > 0:
                grad_linear = jnp.concatenate(
                    [jnp.where(masks[0], grad[:, :at], 0.0), grad_linear], axis=1
                )
            grad_linear = grad_linear.astype(BFLOAT)
            dv_ref[0, :width] += t_product(weights, numer)
            dphi_q_ref[head, tile] = dot(grad_linear, phi_k_ref[head, :width])
            dphi_k_ref[head, :width] += t_product(grad_linear, phi_rows)
            dq_ref[tile, cols] = dot(grad_raw, k_ref[0, at:width])
            dk_ref[0, at:width] += t_product(grad_raw, rows)


def softmax_back(phi, grad):
    wide = phi.astype(FLOAT)
    terms = grad * wide
    high = terms.astype(BFLOAT)
    low = (terms - high.astype(FLOAT)).astype(BFLOAT)
    mean = (half_sums(high) + half_sums(low)) / half_sums(phi)
    return (wide * (grad - mean)).astype(BFLOAT)


def features_back_kernel(
    group, q_ref, k_ref, v_ref, phi_q_ref, phi_k_ref, dn_ref, fq_ref, fk_ref, state_ref, ds_ref,
    cont_ref, carry_ref, dq_in, dk_in, dv_in, dphi_q_ref, dphi_k_ref,
    dq_ref, dk_ref, dv_ref, gq_ref, gk_ref,
):
    cont = cont_ref[...]
    carry = carry_ref[...]
    keys = k_ref[0]
    dk = dk_in[0]
    dv = dv_in[0]
    for head in range(group):
        cols = slice(head * HEAD_SIZE, (head + 1) * HEAD_SIZE)
        grad_state = ds_ref[head]
        phi_k = phi_k_ref[head]
        grad_q = dphi_q_ref[head] + cont * dot(dn_ref[head], state_ref[head])
        grad_k = dphi_k_ref[head] + carry * dot(v_ref[0], grad_state)
        dv = dv + carry * product_t(phi_k, grad_state)
        mixed_q = softmax_back(phi_q_ref[head], grad_q)
        mixed_k = softmax_back(phi_k, grad_k)
        dq_ref[:, cols] = dq_in[:, cols] + product_t(mixed_q, fq_ref[head])
        dk = dk + product_t(mixed_k, fk_ref[head])
        gq_ref[head] = t_product(q_ref[:, cols], mixed_q)
        gk_ref[head] = t_product(keys, mixed_k)
    dk_ref[0] = dk
    dv_ref[0] = dv


def feed_kernel(x_ref, c_ref, gate_ref, up_ref, down_ref, hid_ref, dg_ref, du_ref, out_ref, back_ref):
    rows = x_ref[...]
    gate = dot(rows, gate_ref[...])
    up = dot(rows, up_ref[...])
    grad = product_t(c_ref[...], down_ref[...])
    sigmoid = 1.0 / (1.0 + jnp.exp(-gate))
    silu = gate * sigmoid
    hidden = (silu * up).astype(BFLOAT)
    grad_gate = (grad * up * (sigmoid + silu * (1.0 - sigmoid))).astype(BFLOAT)
    grad_up = (grad * silu).astype(BFLOAT)
    hid_ref[...] = hidden
    dg_ref[...] = grad_gate
    du_ref[...] = grad_up
    back_ref[...] = (product_t(grad_gate, gate_ref[...]) + product_t(grad_up, up_ref[...])).astype(BFLOAT)
    out_ref[...] = dot(hidden, down_ref[...]).astype(BFLOAT)


def feed(rows, cotangent, gate, up, down):
    count, model = rows.shape
    units = gate.shape[1]
    tile = min(256, count)

    def tiled(width):
        return pl.BlockSpec((tile, width), lambda at: (at, 0))

    def whole(shape):
        return pl.BlockSpec(shape, lambda at: (0, 0))

    return pl.pallas_call(
        feed_kernel,
        grid=(count // tile,),
        in_specs=[tiled(model), tiled(model), whole(gate.shape), whole(up.shape), whole(down.shape)],
        out_specs=[tiled(units)] * 3 + [tiled(model)] * 2,
        out_shape=[jax.ShapeDtypeStruct((count, units), BFLOAT)] * 3
        + [jax.ShapeDtypeStruct((count, model), BFLOAT)] * 2,
        compiler_params=pltpu.CompilerParams(vmem_limit_bytes=56 * 1024 * 1024),
        cost_estimate=pl.CostEstimate(
            flops=12 * count * model * units,
            bytes_accessed=8 * count * model + 6 * model * units,
            transcendentals=count * units,
        ),
    )(rows, cotangent, gate, up, down)


def tie(first, second):
    return lax.optimization_barrier((first, second))


def heads_call(kernel, kv_heads, group, args, outs, flops):
    def spec(shape, kind):
        if kind == "cols":
            return pl.BlockSpec((shape[0], shape[1] // kv_heads), lambda at: (0, at))
        if kind == "all":
            return pl.BlockSpec(shape, lambda at: (0,) * len(shape))
        return pl.BlockSpec((shape[0] // kv_heads,) + shape[1:], lambda at: (at, 0, 0))

    moved = sum(np.prod(value.shape) * 2 for value, _ in args) + sum(np.prod(s) * 3 for s, _, _ in outs)
    return pl.pallas_call(
        functools.partial(kernel, group),
        grid=(kv_heads,),
        in_specs=[spec(value.shape, kind) for value, kind in args],
        out_specs=[spec(shape, kind) for shape, _, kind in outs],
        out_shape=[jax.ShapeDtypeStruct(shape, dtype) for shape, dtype, _ in outs],
        compiler_params=pltpu.CompilerParams(vmem_limit_bytes=48 * 1024 * 1024),
        cost_estimate=pl.CostEstimate(flops=int(flops), bytes_accessed=int(moved), transcendentals=0),
    )(*[value for value, _ in args])


def carried(value, coefs):
    count = lax.axis_size("chip")
    me = lax.axis_index("chip")
    sent = value[:, : HEAD_SIZE + 16]
    total = jnp.zeros(sent.shape, FLOAT)
    for step in range(1, count):
        total = total + coefs[me ^ step] * swap(sent, "chip", step).astype(FLOAT)
    return jnp.pad(total.astype(BFLOAT), ((0, 0), (0, value.shape[1] - sent.shape[1]), (0, 0)))


def carry_coefs(lengths, tokens):
    count = lax.axis_size("chip")
    me = lax.axis_index("chip")
    starts = jnp.arange(count, dtype=jnp.int32) * tokens
    open_chip = locate(starts - 1, lengths)[0] == locate(starts + tokens - 1, lengths)[0]
    source = jnp.arange(count)[:, None]
    between = jnp.arange(count)[None, :]
    after = (between > source) & (between < me)
    before = (between < source) & (between > me)
    forward = jnp.all(open_chip[None, :] | ~after, axis=1) & (source[:, 0] < me)
    backward = jnp.all(open_chip[None, :] | ~before, axis=1) & (source[:, 0] > me)
    return forward.astype(FLOAT), backward.astype(FLOAT)


def on_device(
    hidden_in,
    doc_lengths,
    attention_gain,
    query_weight,
    key_projection,
    value_projection,
    output_weight,
    query_down,
    query_up,
    key_down,
    key_adapter_up,
    value_down,
    value_adapter_up,
    output_down,
    output_up,
    query_feature_maps,
    key_feature_maps,
    feedforward_gain,
    gate_weight,
    up_weight,
    down_weight,
    block_cotangent,
):
    own_rows, model = hidden_in.shape
    tokens = own_rows * CORES
    core = lax.axis_index("core")
    chip = lax.axis_index("chip")
    chips = lax.axis_size("chip")
    heads = query_feature_maps.shape[0] // CORES
    kv_heads = key_projection.shape[1] // HEAD_SIZE // CORES
    group = heads // kv_heads
    q_width = heads * HEAD_SIZE
    kv_width = kv_heads * HEAD_SIZE
    rank = query_down.shape[1]
    ff_axes = ("chip", "core")

    def own_cols(value, width, which):
        return lax.dynamic_slice_in_dim(value, which * width, width, 1)

    def own_heads(value, count, which):
        return lax.dynamic_slice_in_dim(value, which * count, count, 0)

    def qkv_cols(which):
        return jnp.concatenate(
            [
                own_cols(query_weight, q_width, which),
                own_cols(key_projection, kv_width, which),
                own_cols(value_projection, kv_width, which),
            ],
            axis=1,
        )

    qkv_block = ordered(core, qkv_cols(core), swap(qkv_cols(1 - core), "core"), 0)
    out_mine = own_heads(output_weight, q_width, core)[None]
    out_block = ordered(core, out_mine, swap(own_heads(output_weight, q_width, 1 - core)[None], "core"), 0)
    orders = cube_orders()
    qkv_width = q_width + 2 * kv_width

    def gather_two(block, dim):
        parts = jnp.split(block, 2, axis=dim)
        return [gather_blocks(part, order) for part, order in zip(parts, orders)]

    qkv_parts = gather_two(qkv_block, 1)
    full_qkv = jnp.concatenate([part.reshape(model, qkv_width // 2) for part in qkv_parts], axis=1)
    out_parts = gather_two(out_block, 1)
    full_out = jnp.concatenate(
        [part.transpose(2, 0, 1, 3).reshape(q_width // 2, model) for part in out_parts], axis=0
    )

    t_orders = token_orders()

    def gather_rows(rows):
        return [gather_tokens(part, order) for part, order in zip(jnp.split(rows, 2, axis=0), t_orders)]

    dp_at = lax.axis_index("dp")

    def ff_weight(weight, split_dim):
        both = ordered(dp_at, weight[None], swap(weight, "dp")[None], 0)
        mine = lax.all_to_all(both, ff_axes, split_dim + 1, 2 - split_dim, tiled=True)
        return mine

    full_gate = ff_weight(gate_weight, 1).reshape(model, -1)
    full_up = ff_weight(up_weight, 1).reshape(model, -1)
    down_both = ff_weight(down_weight, 0)
    full_down = jnp.concatenate([down_both[0], down_both[1]], axis=1)
    cotangents = gather_rows(block_cotangent)

    first_row = chip * tokens
    lengths = doc_lengths[0]
    seg_rows, pos_rows = locate(first_row + jnp.arange(tokens, dtype=jnp.int32), lengths)
    seg_rim = locate(first_row - SOFTMAX_KEYS + jnp.arange(SOFTMAX_KEYS, dtype=jnp.int32), lengths)[
        0
    ]
    seg_first = locate(jnp.reshape(first_row - 1, (1,)), lengths)[0][0]
    gap = 128 - SOFTMAX_KEYS
    seg_ext = jnp.concatenate([jnp.full((gap,), -2, jnp.int32), seg_rim, seg_rows])
    seg_last = seg_rows[tokens - 1]
    continuing = (seg_rows == seg_first).astype(FLOAT)[:, None]
    carry = ((jnp.arange(tokens + 128) < tokens + gap) & (seg_ext == seg_last)).astype(FLOAT)[:, None]
    seg_column, seg_line = seg_rows[:, None], seg_ext[None, :]
    forward_coefs, backward_coefs = carry_coefs(lengths, tokens)
    cosine_table, sine_table = rotation(pos_rows, HEAD_SIZE)
    query_table = own_heads(query_feature_maps, heads, core)
    key_table = own_heads(key_feature_maps, heads, core)
    query_table = jnp.concatenate([query_table, -query_table], axis=2)
    key_table = jnp.concatenate([key_table, -key_table], axis=2)
    downs = jnp.concatenate([query_down, key_down, value_down], axis=1)
    own_query_up = own_cols(query_up, q_width, core)
    own_key_up = own_cols(key_adapter_up, kv_width, core)
    own_value_up = own_cols(value_adapter_up, kv_width, core)
    own_output_down = own_heads(output_down, q_width, core)
    pad = 128 - 3 * rank
    ups = jnp.concatenate(
        [
            jnp.pad(own_query_up, ((0, 0), (0, 2 * kv_width))),
            jnp.pad(own_key_up, ((0, 0), (q_width, kv_width))),
            jnp.pad(own_value_up, ((0, 0), (q_width + kv_width, 0))),
        ],
        axis=0,
    )

    hidden_chip = ordered(core, hidden_in, swap(hidden_in, "core"), 0)
    hidden32 = hidden_chip.astype(FLOAT)
    normed = (hidden32 * norm_scale(hidden32) * attention_gain).astype(BFLOAT)
    low_rank = product(normed, downs).astype(BFLOAT)
    pre = product(normed, full_qkv) + product(low_rank, ups)
    queries = apply_rotary(pre[:, :q_width], cosine_table, sine_table).astype(BFLOAT)
    keys = apply_rotary(pre[:, q_width : q_width + kv_width], cosine_table, sine_table).astype(BFLOAT)
    values = pre[:, q_width + kv_width :].astype(BFLOAT)
    rim = lax.ppermute(
        jnp.concatenate([keys[tokens - SOFTMAX_KEYS :], values[tokens - SOFTMAX_KEYS :]], axis=1),
        "chip",
        [(source, source + 1) for source in range(chips - 1)],
    )
    kv_ext = jnp.concatenate(
        [jnp.zeros((gap, 2 * kv_width), BFLOAT), rim, jnp.concatenate([keys, values], axis=1)], axis=0
    )
    kv_ext = kv_ext.reshape(tokens + 128, 2, kv_heads, HEAD_SIZE).transpose(1, 2, 0, 3)
    key_ext = kv_ext[0]
    tail = jnp.where(jnp.arange(128 - HEAD_SIZE) < 2, 1.0, 0.0).astype(BFLOAT)
    value_ext = jnp.concatenate(
        [kv_ext[1], jnp.broadcast_to(tail, (kv_heads, tokens + 128, 128 - HEAD_SIZE))], axis=2
    )
    masked_values = value_ext * carry.astype(BFLOAT)
    extent = tokens + 128
    call = functools.partial(heads_call, kv_heads=kv_heads, group=group)
    phi_q, phi_k, state_part = call(
        phi_kernel,
        args=[
            (queries, "cols"),
            (key_ext, "heads"),
            (masked_values, "heads"),
            (query_table, "heads"),
            (key_table, "heads"),
        ],
        outs=[
            ((heads, tokens, 128), BFLOAT, "heads"),
            ((heads, extent, 128), BFLOAT, "heads"),
            ((heads, 128, 128), BFLOAT, "heads"),
        ],
        flops=4e9,
    )
    numer_part = call(
        intra_kernel,
        args=[
            (queries, "cols"),
            (key_ext, "heads"),
            (value_ext, "heads"),
            (phi_q, "heads"),
            (phi_k, "heads"),
            (seg_column, "all"),
            (seg_line, "all"),
        ],
        outs=[((heads, tokens, 128), FLOAT, "heads")],
        flops=8e9,
    )[0]
    state = carried(state_part, forward_coefs)
    attended, denominator = call(
        finish_kernel,
        args=[(numer_part, "heads"), (phi_q, "heads"), (state, "heads"), (continuing, "all")],
        outs=[((tokens, q_width), BFLOAT, "cols"), ((kv_heads, tokens, 128), FLOAT, "heads")],
        flops=1e9,
    )

    out_and_down = jnp.concatenate(
        [full_out, own_output_down, jnp.zeros((q_width, 128 - rank), BFLOAT)], axis=1
    )

    def over_heads(part):
        halves = part.reshape(CORES, own_rows, -1)
        mine = take(halves, core, 0)[0].astype(FLOAT) + swap(
            take(halves, 1 - core, 0)[0].astype(BFLOAT), "core"
        ).astype(FLOAT)
        return pair_sum(mine, "tensor")

    branch = over_heads(product(attended, out_and_down).astype(BFLOAT))
    low_mid = branch[:, model : model + rank].astype(BFLOAT)
    hidden_own = hidden_in.astype(FLOAT)
    residual = hidden_own + branch[:, :model] + product(low_mid, output_up)
    normed_ff = (residual * norm_scale(residual) * feedforward_gain).astype(BFLOAT)

    parts = []
    for gathered, cotangent, order in zip(gather_rows(normed_ff), cotangents, t_orders):
        there = feed(gathered[1], cotangent[1], full_gate, full_up, full_down)
        here = feed(gathered[0], cotangent[0], full_gate, full_up, full_down)
        parts.append((here, gathered[0], cotangent[0]))
        parts.append((there, gathered[1], cotangent[1]))

    def halves_sum(which):
        pieces = [
            scatter_tokens(parts[2 * at][0][which], parts[2 * at + 1][0][which], t_orders[at])
            for at in range(2)
        ]
        return pair_sum(jnp.concatenate(pieces, axis=0), "tensor")

    grad_normed_ff = halves_sum(4)

    def rows_sum(pick):
        return sum(t_product(*pick(part)) for part in parts)

    gate_grad = rows_sum(lambda part: (part[1], part[0][1]))
    up_grad = rows_sum(lambda part: (part[1], part[0][2]))
    down_grad = rows_sum(lambda part: (part[0][0], part[2]))
    block_output = (residual + halves_sum(3)).astype(BFLOAT)

    def dp_half(grad, dim):
        half = grad.shape[dim] // 2
        send = lax.dynamic_slice_in_dim(grad, (1 - dp_at) * half, half, dim).astype(BFLOAT)
        keep = lax.dynamic_slice_in_dim(grad, dp_at * half, half, dim).astype(FLOAT)
        return (keep + swap(send, "dp").astype(FLOAT)).astype(BFLOAT)

    down_shard = lax.all_to_all(dp_half(down_grad, 1), ff_axes, 1, 0, tiled=True).astype(FLOAT)
    gate_shard = lax.all_to_all(dp_half(gate_grad, 0), ff_axes, 0, 1, tiled=True).astype(FLOAT)
    up_shard = lax.all_to_all(dp_half(up_grad, 0), ff_axes, 0, 1, tiled=True).astype(FLOAT)

    grad_res_part, feedforward_gain_grad = norm_back(residual, feedforward_gain, grad_normed_ff)
    grad_residual = block_cotangent.astype(FLOAT) + grad_res_part
    grad_branch_own = grad_residual.astype(BFLOAT)
    output_up_grad = t_product(low_mid, grad_branch_own)
    grad_branch = ordered(core, grad_branch_own, swap(grad_branch_own, "core"), 0)
    grad_mid = product_t(grad_branch, output_up).astype(BFLOAT)
    grad_attended = product_t(grad_branch, full_out) + product_t(grad_mid, own_output_down)
    output_down_grad = t_product(grad_mid, attended)
    out_grad = t_product(attended, grad_branch).astype(BFLOAT)
    grad_numer, grad_state_part = call(
        grad_numer_kernel,
        args=[
            (grad_attended, "cols"),
            (attended, "cols"),
            (denominator, "heads"),
            (phi_q, "heads"),
            (continuing, "all"),
        ],
        outs=[((heads, tokens, 128), BFLOAT, "heads"), ((heads, 128, 128), BFLOAT, "heads")],
        flops=2e9,
    )
    intra = call(
        intra_back_kernel,
        args=[
            (queries, "cols"),
            (key_ext, "heads"),
            (value_ext, "heads"),
            (phi_q, "heads"),
            (phi_k, "heads"),
            (grad_numer, "heads"),
            (seg_column, "all"),
            (seg_line, "all"),
        ],
        outs=[
            ((tokens, q_width), FLOAT, "cols"),
            ((kv_heads, extent, HEAD_SIZE), FLOAT, "heads"),
            ((kv_heads, extent, 128), FLOAT, "heads"),
            ((heads, tokens, 128), FLOAT, "heads"),
            ((heads, extent, 128), FLOAT, "heads"),
        ],
        flops=16e9,
    )
    grad_state = carried(grad_state_part, backward_coefs)
    grad_queries, grad_keys, grad_values, query_tables, key_tables = call(
        features_back_kernel,
        args=[
            (queries, "cols"),
            (key_ext, "heads"),
            (value_ext, "heads"),
            (phi_q, "heads"),
            (phi_k, "heads"),
            (grad_numer, "heads"),
            (query_table, "heads"),
            (key_table, "heads"),
            (state, "heads"),
            (grad_state, "heads"),
            (continuing, "all"),
            (carry, "all"),
            (intra[0], "cols"),
            (intra[1], "heads"),
            (intra[2], "heads"),
            (intra[3], "heads"),
            (intra[4], "heads"),
        ],
        outs=[
            ((tokens, q_width), FLOAT, "cols"),
            ((kv_heads, extent, HEAD_SIZE), FLOAT, "heads"),
            ((kv_heads, extent, 128), FLOAT, "heads"),
            ((heads, HEAD_SIZE, 128), FLOAT, "heads"),
            ((heads, HEAD_SIZE, 128), FLOAT, "heads"),
        ],
        flops=6e9,
    )
    query_table_grad = query_tables[:, :, :FEATURE_HALF] - query_tables[:, :, FEATURE_HALF:]
    key_table_grad = key_tables[:, :, :FEATURE_HALF] - key_tables[:, :, FEATURE_HALF:]
    grad_kv_ext = jnp.concatenate(
        [grad_keys[head, gap:] for head in range(kv_heads)]
        + [grad_values[head, gap:, :HEAD_SIZE] for head in range(kv_heads)],
        axis=1,
    )
    rim_grad = lax.ppermute(
        grad_kv_ext[:SOFTMAX_KEYS],
        "chip",
        [(source + 1, source) for source in range(chips - 1)],
    )
    grad_kv = grad_kv_ext[SOFTMAX_KEYS:] + jnp.pad(rim_grad, ((tokens - SOFTMAX_KEYS, 0), (0, 0)))
    grad_pre = jnp.concatenate(
        [
            rotate_back(grad_queries, cosine_table, sine_table),
            rotate_back(grad_kv[:, :kv_width], cosine_table, sine_table),
            grad_kv[:, kv_width:],
        ],
        axis=1,
    ).astype(BFLOAT)
    qkv_grad = t_product(normed, grad_pre).astype(BFLOAT)
    back_weights = jnp.concatenate(
        [full_qkv, ups, jnp.zeros((pad, qkv_width), BFLOAT)], axis=0
    )
    back = over_heads(product_t(grad_pre, back_weights).astype(BFLOAT))
    grad_low = back[:, model : model + 3 * rank].astype(BFLOAT)
    grad_normed = back[:, :model] + product_t(grad_low, downs)
    normed_own = (hidden_own * norm_scale(hidden_own) * attention_gain).astype(BFLOAT)
    downs_grad = t_product(grad_low, normed_own)
    grad_in_part, attention_gain_grad = norm_back(hidden_own, attention_gain, grad_normed)
    input_grad = (grad_residual + grad_in_part).astype(BFLOAT)
    ups_grad = t_product(low_rank, grad_pre)
    value_up_grad = t_product(low_rank[:, 2 * rank :], grad_pre[:, q_width + kv_width :])

    def scatter_two(parts):
        return [scatter_blocks(part, order[::-1]) for part, order in zip(parts, orders)]

    blocks = 2 ** len(cube_dims())
    qkv_blocks = qkv_grad.reshape(blocks, CORES, model // blocks // CORES, qkv_width)
    qkv_sums = jnp.concatenate(scatter_two(jnp.split(qkv_blocks, 2, axis=3)), axis=2)
    qkv_keep = take(qkv_sums, core, 0)[0]
    qkv_other = swap(take(qkv_sums, 1 - core, 0)[0].astype(BFLOAT), "core").astype(FLOAT)
    query_shard = ordered(core, qkv_keep[:, :q_width], qkv_other[:, :q_width], 1)
    key_shard = ordered(
        core,
        qkv_keep[:, q_width : q_width + kv_width],
        qkv_other[:, q_width : q_width + kv_width],
        1,
    )
    value_shard = ordered(
        core, qkv_keep[:, q_width + kv_width :], qkv_other[:, q_width + kv_width :], 1
    )
    out_blocks = out_grad.reshape(q_width, blocks, CORES, model // blocks // CORES).transpose(
        1, 2, 0, 3
    )
    out_sums = jnp.concatenate(scatter_two(jnp.split(out_blocks, 2, axis=2)), axis=1)
    out_keep = take(out_sums, core, 0)[0]
    out_other = swap(take(out_sums, 1 - core, 0)[0].astype(BFLOAT), "core").astype(FLOAT)
    output_shard = ordered(core, out_keep, out_other, 0)

    shared = jnp.concatenate(
        [attention_gain_grad[None], feedforward_gain_grad[None], downs_grad, output_up_grad], axis=0
    )
    headed = jnp.concatenate(
        [
            query_table_grad.reshape(-1, model),
            key_table_grad.reshape(-1, model),
            jnp.concatenate([output_down_grad, ups_grad[:rank, :q_width]], axis=0).reshape(-1, model),
            jnp.concatenate(
                [
                    ups_grad[rank : 2 * rank, q_width : q_width + kv_width],
                    value_up_grad,
                ],
                axis=0,
            ).reshape(-1, model),
        ],
        axis=0,
    )
    shared_rows = shared.shape[0]
    shared = shared + swap(shared, "core")
    small = jnp.concatenate([shared, headed], axis=0)
    for axis, mask in cube_dims()[::-1]:
        small = small + swap(small, axis, mask)
    shared = small[:shared_rows]
    headed = small[shared_rows:]
    both = ordered(core, headed[None], swap(headed, "core")[None], 0)
    table_rows = heads * HEAD_SIZE * FEATURE_HALF // model
    query_features = both[:, :table_rows].reshape(CORES * heads, HEAD_SIZE, FEATURE_HALF)
    key_features = both[:, table_rows : 2 * table_rows].reshape(
        CORES * heads, HEAD_SIZE, FEATURE_HALF
    )
    wide_rows = rank * q_width // model
    at = 2 * table_rows
    down_total = both[:, at : at + wide_rows].reshape(CORES, rank, q_width)
    query_up_total = both[:, at + wide_rows : at + 2 * wide_rows].reshape(CORES, rank, q_width)
    narrow = both[:, at + 2 * wide_rows :].reshape(CORES, 2, rank, kv_width)

    def joined(value):
        return jnp.concatenate([value[0], value[1]], axis=1)

    downs_total = shared[2 : 2 + 3 * rank].T
    return (
        block_output,
        input_grad,
        shared[0],
        query_shard,
        key_shard,
        value_shard,
        output_shard,
        downs_total[:, :rank],
        joined(query_up_total),
        downs_total[:, rank : 2 * rank],
        joined(narrow[:, 0]),
        downs_total[:, 2 * rank :],
        joined(narrow[:, 1]),
        joined(down_total).T,
        shared[2 + 3 * rank :],
        query_features,
        key_features,
        shared[1],
        gate_shard,
        up_shard,
        down_shard,
    )


def solution(mesh):
    dp, seq, tensor = (mesh.shape[name] for name in ("dp", "seq", "tensor"))
    split = Mesh(
        mesh.devices.reshape(dp, seq // CORES, CORES, tensor), ("dp", "chip", "core", "tensor")
    )
    tok = ("dp", "chip", "core")
    in_specs = (
        P(tok, None),
        P("dp", None),
        P(),
        P(tok, "tensor"),
        P(tok, "tensor"),
        P(tok, "tensor"),
        P("tensor", tok),
        P(),
        P(None, "tensor"),
        P(),
        P(None, "tensor"),
        P(),
        P(None, "tensor"),
        P("tensor", None),
        P(),
        P("tensor", None, None),
        P("tensor", None, None),
        P(),
        P(tok, "tensor"),
        P(tok, "tensor"),
        P("tensor", tok),
        P(tok, None),
    )
    out_specs = (
        P(tok, None),
        P(tok, None),
        P(),
        P(tok, "tensor"),
        P(tok, "tensor"),
        P(tok, "tensor"),
        P("tensor", tok),
        P(),
        P(None, "tensor"),
        P(),
        P(None, "tensor"),
        P(),
        P(None, "tensor"),
        P("tensor", None),
        P(),
        P("tensor", None, None),
        P("tensor", None, None),
        P(),
        P(tok, "tensor"),
        P(tok, "tensor"),
        P("tensor", tok),
    )
    return jax.shard_map(
        on_device, mesh=split, in_specs=in_specs, out_specs=out_specs, check_vma=False
    )
```

time: 2850 us -> 882 us (0.31)
  waiting for transfers between devices: 2250 us -> 333 us
  matrix products: 312 us -> 81.5 us
  starting transfers between devices: 9.84 us -> 114 us
  Pallas kernels: 0 us -> 86.9 us
  blocking collectives: 51.5 us -> 0 us
  local copies, waits for them, and re-layouts: 71.8 us -> 123 us
    reduce_scatter x7 -> x0, waiting for transfers between devices: 1390 us -> none  [the longest x1 355 us: on_device(): lax.psum_scatter(product(normed_ff.T, grad_up), ('dp', 'seq'), scatter_di...]
    all_gather x9 -> x0, waiting for transfers between devices: 511 us -> none  [the longest x1 165 us: on_device(): lax.all_gather(down_weight, ('dp', 'seq'), axis=1, tiled=True)]
    psum x6 -> x0, waiting for transfers between devices: 340 us -> none  [the longest x2 173 us: on_device(): lax.psum((attention_gain_grad, feedforward_gain_grad, downs_grad, query_u...]
    ppermute x4 -> x79, waiting for transfers between devices: 0.01 us -> 327 us  [the longest x77 321 us: swap(): lax.ppermute(value, axis, [(source, source ^ mask) for source in range(co...]
    dot_general x35 -> x5, matrix products: 168 us -> 13 us  [product(): return jnp.dot(left, right, preferred_element_type=FLOAT)]
    pallas_call x0 -> x10, Pallas kernels: none -> 86.9 us  [the longest x4 48.9 us: feed(): pl.pallas_call(feed_kernel, grid=(count // tile,), in_specs=[tiled(model)...]
    dot_general x27 -> x24, matrix products: 139 us -> 68.5 us  [the longest x19 57.4 us: t_product(): lax.dot_general(left, right, (((0,), (0,)), ((), ())), preferred_element_...]
    ppermute x4 -> x79, starting transfers between devices: 8.27 us -> 74.1 us  [the longest x77 68.4 us: swap(): lax.ppermute(value, axis, [(source, source ^ mask) for source in range(co...]
  transfers between devices with their start and end apart: 26 -> 85, of which waited for: 20 -> 32; matrix products, arithmetic and copies ran while one was open for 11% -> 34% of each run, Pallas kernels for 0% -> 10%
where the time goes in v1:
time: 882 us; the launch traced here: 866 us
  waiting for transfers between devices  333 us (38%)
  other arithmetic  124 us (14%)
  local copies, waits for them, and re-layouts  123 us (14%)
  starting transfers between devices  114 us (13%)
  Pallas kernels  86.9 us (10%)
  matrix products  81.5 us (9%)
    ppermute x77, waiting for transfers between devices, swap(): lax.ppermute(value, axis, [(source, source ^ mask) for source in range(co...  321 us
    ppermute x77, starting transfers between devices, swap(): lax.ppermute(value, axis, [(source, source ^ mask) for source in range(co...  68.4 us
    dot_general x19, matrix products, t_product(): lax.dot_general(left, right, (((0,), (0,)), ((), ())), preferred_element_...  57.4 us
    pallas_call x4, Pallas kernels, feed(): pl.pallas_call(feed_kernel, grid=(count // tile,), in_specs=[tiled(model)...  48.9 us
    pallas_call x6, Pallas kernels, heads_call(): pl.pallas_call(functools.partial(kernel, group), grid=(kv_heads,), in_spe...  38.1 us
    select_n x4, local copies, waits for them, and re-layouts, ordered(): jnp.where(which == 0, jnp.concatenate([mine, other], axis=dim), jnp.conca...  32.7 us
    select_n x22, other arithmetic, ordered(): jnp.where(which == 0, jnp.concatenate([mine, other], axis=dim), jnp.conca...  26.9 us
    all_to_all x3, starting transfers between devices, ff_weight(): lax.all_to_all(both, ff_axes, split_dim + 1, 2 - split_dim, tiled=True)  21.2 us
  transfers between devices with their start and end apart: 85, of which 32 were waited for; matrix products, arithmetic and copies ran while one was open for 34% of the time, Pallas kernels for 10%

profile of v1, /device:TPU:15, one launch (start us, length us, event | category | flops | bytes accessed | tf_op | source)
XLA Modules:
  0.0 865.9 jit_solution(3920591328107008409)
XLA Ops:
  32.7 38.2 %collective-permute-done.16 = bf16[1,1,1,2,256,128]{5,4,3,2,1,0:T(8,128)(2,1)S(1)} collective-permute-done((bf16[1,1,1,2,256,128]{5,4,3,2,1,0:T(8,128)(2,1)S(1)}, bf16[1,1,1,2,256,128]{5,4,3,2,1,0:T(8,128)(2,1)S(1)}, u32[]{:S(2)}, u32[]{:S(2)}) %collective-permute-start.16) | collective-permute-done | bytes 131104 | tf_op jit(solution)/shard_map/ppermute | solution.py:25
  96.6 7.2 collective-permute-done.18
  116.7 6.2 copy.181
  122.8 8.1 all-to-all-start
  191.9 6.2 copy.183
  200.9 7.1 all-to-all-start.1
  214.4 14.3 %collective-permute-done.27 = bf16[4096,128]{1,0:T(8,128)(2,1)} collective-permute-done((bf16[4096,128]{1,0:T(8,128)(2,1)}, bf16[4096,128]{1,0:T(8,128)(2,1)}, u32[]{:S(2)}, u32[]{:S(2)}) %collective-permute-start.27) | collective-permute-done | bytes 1048608 | tf_op jit(solution)/shard_map/ppermute | solution.py:25
  231.5 18.1 %copy.185 = bf16[2,4096,128]{2,0,1:T(2,128)(2,1)} copy(bf16[2,4096,128]{2,1,0:T(8,128)(2,1)S(1)} %maximum_select_fusion.3) | data formatting | bytes 4194304 | tf_op jit(solution)/shard_map/jit(_where)/select_n | solution.py:33
  270.3 6.2 copy.182
  285.7 8.3 collective-permute-done.33
  300.1 19.5 %collective-permute-done.34 = bf16[256,2048]{1,0:T(8,128)(2,1)S(1)} collective-permute-done((bf16[256,2048]{1,0:T(8,128)(2,1)S(1)}, bf16[256,2048]{1,0:T(8,128)(2,1)S(1)}, u32[]{:S(2)}, u32[]{:S(2)}) %collective-permute-start.34) | collective-permute-done | bytes 1048608 | tf_op jit(solution)/shard_map/ppermute | solution.py:25
  327.5 12.0 %shard_map.387 = (bf16[512,512]{1,0:T(8,128)(2,1)}, bf16[512,512]{1,0:T(8,128)(2,1)}, bf16[512,512]{1,0:T(8,128)(2,1)}, bf16[512,2048]{1,0:T(8,128)(2,1)}, bf16[512,2048]{1,0:T(8,128)(2,1)}) custom-call(bf16[512,2048]{1,0:T(8,128)(2,1)} %pad_maximum_fusion.3.x_ref, bf16[512,2048]{1,0:T(8,128)(2,1)} %pad_maximum_fusion.4.c_ref, bf16[2048,512]{1,0:T(8,128)(2,1)} %bitcast.244, ...), custom_call_target="tpu_custom_call" | custom-call | flops 6442450944 | bytes 14680064 | tf_op jit(solution)/shard_map/pallas_call | solution.py:378
  339.5 12.3 %shard_map.385 = (bf16[512,512]{1,0:T(8,128)(2,1)}, bf16[512,512]{1,0:T(8,128)(2,1)}, bf16[512,512]{1,0:T(8,128)(2,1)}, bf16[512,2048]{1,0:T(8,128)(2,1)}, bf16[512,2048]{1,0:T(8,128)(2,1)}) custom-call(bf16[512,2048]{1,0:T(8,128)(2,1)} %pad_maximum_fusion.1.x_ref, bf16[512,2048]{1,0:T(8,128)(2,1)} %pad_maximum_fusion.2.c_ref, bf16[2048,512]{1,0:T(8,128)(2,1)} %bitcast.245, ...), custom_call_target="tpu_custom_call" | custom-call | flops 6442450944 | bytes 14680064 | tf_op jit(solution)/shard_map/pallas_call | solution.py:378
  381.3 12.0 %shard_map.388 = (bf16[512,512]{1,0:T(8,128)(2,1)}, bf16[512,512]{1,0:T(8,128)(2,1)}, bf16[512,512]{1,0:T(8,128)(2,1)}, bf16[512,2048]{1,0:T(8,128)(2,1)}, bf16[512,2048]{1,0:T(8,128)(2,1)}) custom-call(bf16[512,2048]{1,0:T(8,128)(2,1)} %copy-done.28, bf16[512,2048]{1,0:T(8,128)(2,1)} %collective-permute-done.38.c_ref, bf16[2048,512]{1,0:T(8,128)(2,1)} %bitcast.246, ...), custom_call_target="tpu_custom_call" | custom-call | flops 6442450944 | bytes 14680064 | tf_op jit(solution)/shard_map/pallas_call | solution.py:378
  395.2 12.5 %shard_map.386 = (bf16[512,512]{1,0:T(8,128)(2,1)}, bf16[512,512]{1,0:T(8,128)(2,1)}, bf16[512,512]{1,0:T(8,128)(2,1)}, bf16[512,2048]{1,0:T(8,128)(2,1)}, bf16[512,2048]{1,0:T(8,128)(2,1)}) custom-call(bf16[512,2048]{1,0:T(8,128)(2,1)} %copy-done.18, bf16[512,2048]{1,0:T(8,128)(2,1)} %collective-permute-done.29.c_ref, bf16[2048,512]{1,0:T(8,128)(2,1)} %bitcast.247, ...), custom_call_target="tpu_custom_call" | custom-call | flops 6442450944 | bytes 14680064 | tf_op jit(solution)/shard_map/pallas_call | solution.py:378
  435.4 30.3 %collective-permute-done.76 = bf16[1024,512]{1,0:T(8,128)(2,1)S(1)} collective-permute-done((bf16[1024,512]{1,0:T(8,128)(2,1)}, bf16[1024,512]{1,0:T(8,128)(2,1)S(1)}, u32[]{:S(2)}, u32[]{:S(2)}) %collective-permute-start.76) | collective-permute-done | bytes 1048608 | tf_op jit(solution)/shard_map/ppermute | solution.py:25
  470.0 6.2 all-to-all-start.3
  491.3 19.9 %collective-permute-done.47 = bf16[256,2048]{1,0:T(8,128)(2,1)S(1)} collective-permute-done((bf16[256,2048]{1,0:T(8,128)(2,1)S(1)}, bf16[256,2048]{1,0:T(8,128)(2,1)S(1)}, u32[]{:S(2)}, u32[]{:S(2)}) %collective-permute-start.47) | collective-permute-done | bytes 1048608 | tf_op jit(solution)/shard_map/ppermute | solution.py:25
  513.4 20.3 %collective-permute-done.40 = bf16[256,2048]{1,0:T(8,128)(2,1)S(1)} collective-permute-done((bf16[256,2048]{1,0:T(8,128)(2,1)S(1)}, bf16[256,2048]{1,0:T(8,128)(2,1)S(1)}, u32[]{:S(2)}, u32[]{:S(2)}) %collective-permute-start.40) | collective-permute-done | bytes 1048608 | tf_op jit(solution)/shard_map/ppermute | solution.py:25
  535.9 9.9 %collective-permute-done.48 = bf16[128,2048]{1,0:T(8,128)(2,1)S(1)} collective-permute-done((bf16[128,2048]{1,0:T(8,128)(2,1)S(1)}, bf16[128,2048]{1,0:T(8,128)(2,1)S(1)}, u32[]{:S(2)}, u32[]{:S(2)}) %collective-permute-start.48) | collective-permute-done | bytes 524320 | tf_op jit(solution)/shard_map/ppermute | solution.py:25
  548.4 8.7 %collective-permute-done.41 = bf16[128,2048]{1,0:T(8,128)(2,1)S(1)} collective-permute-done((bf16[128,2048]{1,0:T(8,128)(2,1)S(1)}, bf16[128,2048]{1,0:T(8,128)(2,1)S(1)}, u32[]{:S(2)}, u32[]{:S(2)}) %collective-permute-start.41) | collective-permute-done | bytes 524320 | tf_op jit(solution)/shard_map/ppermute | solution.py:25
  564.2 7.2 all-to-all-start.4
  571.5 10.0 %collective-permute-done.49 = bf16[256,2048]{1,0:T(8,128)(2,1)} collective-permute-done((bf16[256,2048]{1,0:T(8,128)(2,1)}, bf16[256,2048]{1,0:T(8,128)(2,1)}, u32[]{:S(2)}, u32[]{:S(2)}) %collective-permute-start.49) | collective-permute-done | bytes 1048608 | tf_op jit(solution)/shard_map/ppermute | solution.py:25
  584.4 19.6 %collective-permute-done.42 = bf16[256,2048]{1,0:T(8,128)(2,1)} collective-permute-done((bf16[256,2048]{1,0:T(8,128)(2,1)}, bf16[256,2048]{1,0:T(8,128)(2,1)}, u32[]{:S(2)}, u32[]{:S(2)}) %collective-permute-start.42) | collective-permute-done | bytes 1048608 | tf_op jit(solution)/shard_map/ppermute | solution.py:25
  645.9 13.4 %shard_map.390 = (f32[512,512]{1,0:T(8,128)S(1)}, f32[2,640,64]{2,1,0:T(8,128)S(1)}, f32[2,640,128]{2,1,0:T(8,128)S(1)}, f32[8,512,128]{2,1,0:T(8,128)}, f32[8,640,128]{2,1,0:T(8,128)}) custom-call(bf16[512,512]{1,0:T(8,128)(2,1)S(1)} %fusion.44.q_ref, bf16[2,640,64]{2,1,0:T(8,128)(2,1)S(1)} %get-tuple-element.149.k_ref, ...), custom_call_target="tpu_custom_call" | custom-call | flops 16000000000 | bytes 9488640 | tf_op jit(solution)/shard_map/pallas_call | solution.py:407
  681.3 8.2 shard_map.391
  727.8 18.3 %collective-permute-done.72 = bf16[2,1,1,2,256,128]{5,4,3,2,1,0:T(8,128)(2,1)S(1)} collective-permute-done((bf16[2,1,1,2,256,128]{5,4,3,2,1,0:T(8,128)(2,1)S(1)}, bf16[2,1,1,2,256,128]{5,4,3,2,1,0:T(8,128)(2,1)S(1)}, u32[]{:S(2)}, u32[]{:S(2)}) %collective-permute-start.72) | collective-permute-done | bytes 262176 | tf_op jit(solution)/shard_map/ppermute | solution.py:25
  748.8 8.2 collective-permute-done.73
  776.8 17.4 %collective-permute-done.56 = bf16[256,2176]{1,0:T(8,128)(2,1)S(1)} collective-permute-done((bf16[256,2176]{1,0:T(8,128)(2,1)S(1)}, bf16[256,2176]{1,0:T(8,128)(2,1)S(1)}, u32[]{:S(2)}, u32[]{:S(2)}) %collective-permute-start.56) | collective-permute-done | bytes 1114144 | tf_op jit(solution)/shard_map/ppermute | solution.py:25
  811.3 6.4 collective-permute-done.58
  821.3 10.3 %collective-permute-done.59 = f32[71,2048]{1,0:T(8,128)S(1)} collective-permute-done((f32[71,2048]{1,0:T(8,128)S(1)}, f32[71,2048]{1,0:T(8,128)S(1)}, u32[]{:S(2)}, u32[]{:S(2)}) %collective-permute-start.59) | collective-permute-done | bytes 581664 | tf_op jit(solution)/shard_map/ppermute | solution.py:25
  833.9 22.8 %collective-permute-done.60 = f32[71,2048]{1,0:T(8,128)S(1)} collective-permute-done((f32[71,2048]{1,0:T(8,128)S(1)}, f32[71,2048]{1,0:T(8,128)S(1)}, u32[]{:S(2)}, u32[]{:S(2)}) %collective-permute-start.60) | collective-permute-done | bytes 581664 | tf_op jit(solution)/shard_map/ppermute | solution.py:25
  (690 shorter events, 436.5 us)
Async XLA Ops:
  6.3 106.3 %collective-permute-start.25 = (bf16[128,4096]{1,0:T(8,128)(2,1)}, bf16[128,4096]{1,0:T(8,128)(2,1)}, u32[]{:S(2)}, u32[]{:S(2)}) collective-permute-start(bf16[128,4096]{1,0:T(8,128)(2,1)} %param.41), channel_id=1, source_target_pairs={{0,16},{16,0},{1,17},{17,1},{2,18},{18,2},{3,19},{19,3},{4,20},{20... | collective-permute-start | bytes 3145736 | tf_op jit(solution)/shard_map/ppermute | solution.py:25
  26.6 44.3 %collective-permute-start.16 = (bf16[1,1,1,2,256,128]{5,4,3,2,1,0:T(8,128)(2,1)S(1)}, bf16[1,1,1,2,256,128]{5,4,3,2,1,0:T(8,128)(2,1)S(1)}, u32[]{:S(2)}, u32[]{:S(2)}) collective-permute-start(bf16[1,1,1,2,256,128]{5,4,3,2,1,0:T(8,128)(2,1)S(1)} %get-tuple-element.166), channel_id=1, source_target_pairs={{0,16},{16,0},{1,17},{17,1},{2,18},{18,2},{3,19},{19,3},{4,20},{20... | collective-permute-start | bytes 393224 | tf_op jit(solution)/shard_map/ppermute | solution.py:25
  26.7 47.0 %collective-permute-start.13 = (bf16[1,1,1,2,256,128]{5,4,3,2,1,0:T(8,128)(2,1)S(1)}, bf16[1,1,1,2,256,128]{5,4,3,2,1,0:T(8,128)(2,1)S(1)}, u32[]{:S(2)}, u32[]{:S(2)}) collective-permute-start(bf16[1,1,1,2,256,128]{5,4,3,2,1,0:T(8,128)(2,1)S(1)} %get-tuple-element.165), channel_id=1, source_target_pairs={{0,16},{16,0},{1,17},{17,1},{2,18},{18,2},{3,19},{19,3},{4,20},{20... | collective-permute-start | bytes 393224 | tf_op jit(solution)/shard_map/ppermute | solution.py:25
  30.3 47.7 %collective-permute-start.5 = (bf16[1,1,1,256,384]{4,3,2,1,0:T(8,128)(2,1)S(1)}, bf16[1,1,1,256,384]{4,3,2,1,0:T(8,128)(2,1)S(1)}, u32[]{:S(2)}, u32[]{:S(2)}) collective-permute-start(bf16[1,1,1,256,384]{4,3,2,1,0:T(8,128)(2,1)S(1)} %get-tuple-element.162), channel_id=1, source_target_pairs={{0,16},{16,0},{1,17},{17,1},{2,18},{18,2},{3,19},{19,3},{4,20},{20... | collective-permute-start | bytes 589832 | tf_op jit(solution)/shard_map/ppermute | solution.py:25
  30.4 51.8 %collective-permute-start.2 = (bf16[1,1,1,256,384]{4,3,2,1,0:T(8,128)(2,1)S(1)}, bf16[1,1,1,256,384]{4,3,2,1,0:T(8,128)(2,1)S(1)}, u32[]{:S(2)}, u32[]{:S(2)}) collective-permute-start(bf16[1,1,1,256,384]{4,3,2,1,0:T(8,128)(2,1)S(1)} %get-tuple-element.161), channel_id=1, source_target_pairs={{0,16},{16,0},{1,17},{17,1},{2,18},{18,2},{3,19},{19,3},{4,20},{20... | collective-permute-start | bytes 589832 | tf_op jit(solution)/shard_map/ppermute | solution.py:25
  84.0 47.0 %collective-permute-start = (bf16[256,2048]{1,0:T(8,128)(2,1)S(1)}, bf16[256,2048]{1,0:T(8,128)(2,1)}, u32[]{:S(2)}, u32[]{:S(2)}) collective-permute-start(bf16[256,2048]{1,0:T(8,128)(2,1)S(1)} %copy-done.16), channel_id=1, source_target_pairs={{0,2},{2,0},{1,3},{3,1},{4,6},{6,4},{5,7},{7,5},{8,10},{10,8},{9,1... | collective-permute-start | bytes 3145736 | tf_op jit(solution)/shard_map/ppermute | solution.py:25
  92.5 95.5 %collective-permute-start.26 = (bf16[128,4096]{1,0:T(8,128)(2,1)}, bf16[128,4096]{1,0:T(8,128)(2,1)}, u32[]{:S(2)}, u32[]{:S(2)}) collective-permute-start(bf16[128,4096]{1,0:T(8,128)(2,1)} %param.42), channel_id=1, source_target_pairs={{0,16},{16,0},{1,17},{17,1},{2,18},{18,2},{3,19},{19,3},{4,20},{20... | collective-permute-start | bytes 3145736 | tf_op jit(solution)/shard_map/ppermute | solution.py:25
  122.8 78.1 %all-to-all-start = ((bf16[2,128,4096]{1,0,2:T(2,128)(2,1)}), bf16[2,128,4096]{1,0,2:T(2,128)(2,1)}, u32[]{:S(2)}, u32[]{:S(2)}) async-start(bf16[2,128,4096]{1,0,2:T(2,128)(2,1)} %copy.181), calls=%async_computation | async-start | bytes 4194304 | tf_op jit(solution)/shard_map/all_to_all | solution.py:521
  183.1 45.6 %collective-permute-start.27 = (bf16[4096,128]{1,0:T(8,128)(2,1)}, bf16[4096,128]{1,0:T(8,128)(2,1)}, u32[]{:S(2)}, u32[]{:S(2)}) collective-permute-start(bf16[4096,128]{1,0:T(8,128)(2,1)} %param.43), channel_id=1, source_target_pairs={{0,16},{16,0},{1,17},{17,1},{2,18},{18,2},{3,19},{19,3},{4,20},{20... | collective-permute-start | bytes 3145736 | tf_op jit(solution)/shard_map/ppermute | solution.py:25
  200.9 48.7 %collective-permute-start.20 = (bf16[256,2176]{1,0:T(8,128)(2,1)}, bf16[256,2176]{1,0:T(8,128)(2,1)}, u32[]{:S(2)}, u32[]{:S(2)}) collective-permute-start(bf16[256,2176]{1,0:T(8,128)(2,1)} %fusion.12), channel_id=1, source_target_pairs={{0,1},{1,0},{2,3},{3,2},{4,5},{5,4},{6,7},{7,6},{8,9},{9,8},{10,11... | collective-permute-start | bytes 3342344 | tf_op jit(solution)/shard_map/ppermute | solution.py:25
  200.9 51.9 %all-to-all-start.1 = ((bf16[2,128,4096]{1,0,2:T(2,128)(2,1)}), bf16[2,128,4096]{1,0,2:T(2,128)(2,1)}, u32[]{:S(2)}, u32[]{:S(2)}) async-start(bf16[2,128,4096]{1,0,2:T(2,128)(2,1)} %copy.183), calls=%async_computation.1 | async-start | bytes 4194304 | tf_op jit(solution)/shard_map/all_to_all | solution.py:521
  211.8 51.4 %collective-permute-start.36 = (bf16[256,2048]{1,0:T(8,128)(2,1)}, bf16[256,2048]{1,0:T(8,128)(2,1)}, u32[]{:S(2)}, u32[]{:S(2)}) collective-permute-start(bf16[256,2048]{1,0:T(8,128)(2,1)} %pad_maximum_fusion.11), channel_id=1, source_target_pairs={{0,4},{4,0},{8,12},{12,8},{1,5},{5,1},{9,13},{13,9},{2,6},{6,2},{1... | collective-permute-start | bytes 3145736 | tf_op jit(solution)/shard_map/ppermute | solution.py:25
  214.3 52.6 %collective-permute-start.24 = (bf16[256,2048]{1,0:T(8,128)(2,1)}, bf16[256,2048]{1,0:T(8,128)(2,1)}, u32[]{:S(2)}, u32[]{:S(2)}) collective-permute-start(bf16[256,2048]{1,0:T(8,128)(2,1)} %pad_maximum_fusion.9), channel_id=1, source_target_pairs={{0,8},{4,12},{8,0},{12,4},{1,9},{5,13},{9,1},{13,5},{2,10},{6,14},... | collective-permute-start | bytes 3145736 | tf_op jit(solution)/shard_map/ppermute | solution.py:25
  266.3 113.7 %collective-permute-start.38 = (bf16[512,2048]{1,0:T(8,128)(2,1)}, bf16[512,2048]{1,0:T(8,128)(2,1)}, u32[]{:S(2)}, u32[]{:S(2)}) collective-permute-start(bf16[512,2048]{1,0:T(8,128)(2,1)} %pad_maximum_fusion.4.c_ref), channel_id=1, source_target_pairs={{0,2},{2,0},{1,3},{3,1},{4,6},{6,4},{5,7},{7,5},{8,10},{10,8},{9,1... | collective-permute-start | bytes 6291464 | tf_op jit(solution)/shard_map/ppermute | solution.py:25
  270.0 123.8 %collective-permute-start.29 = (bf16[512,2048]{1,0:T(8,128)(2,1)}, bf16[512,2048]{1,0:T(8,128)(2,1)}, u32[]{:S(2)}, u32[]{:S(2)}) collective-permute-start(bf16[512,2048]{1,0:T(8,128)(2,1)} %pad_maximum_fusion.2.c_ref), channel_id=1, source_target_pairs={{0,2},{2,0},{1,3},{3,1},{4,6},{6,4},{5,7},{7,5},{8,10},{10,8},{9,1... | collective-permute-start | bytes 6291464 | tf_op jit(solution)/shard_map/ppermute | solution.py:25
  322.9 57.1 %collective-permute-start.37 = (bf16[512,2048]{1,0:T(8,128)(2,1)}, bf16[512,2048]{1,0:T(8,128)(2,1)S(1)}, u32[]{:S(2)}, u32[]{:S(2)}) collective-permute-start(bf16[512,2048]{1,0:T(8,128)(2,1)} %pad_maximum_fusion.3.x_ref), channel_id=1, source_target_pairs={{0,2},{2,0},{1,3},{3,1},{4,6},{6,4},{5,7},{7,5},{8,10},{10,8},{9,1... | collective-permute-start | bytes 6291464 | tf_op jit(solution)/shard_map/ppermute | solution.py:25
  327.5 66.4 %collective-permute-start.28 = (bf16[512,2048]{1,0:T(8,128)(2,1)}, bf16[512,2048]{1,0:T(8,128)(2,1)S(1)}, u32[]{:S(2)}, u32[]{:S(2)}) collective-permute-start(bf16[512,2048]{1,0:T(8,128)(2,1)} %pad_maximum_fusion.1.x_ref), channel_id=1, source_target_pairs={{0,2},{2,0},{1,3},{3,1},{4,6},{6,4},{5,7},{7,5},{8,10},{10,8},{9,1... | collective-permute-start | bytes 6291464 | tf_op jit(solution)/shard_map/ppermute | solution.py:25
  393.4 82.8 %collective-permute-start.46 = (bf16[512,2048]{1,0:T(8,128)(2,1)}, bf16[512,2048]{1,0:T(8,128)(2,1)}, u32[]{:S(2)}, u32[]{:S(2)}) collective-permute-start(bf16[512,2048]{1,0:T(8,128)(2,1)} %get-tuple-element.69), channel_id=1, source_target_pairs={{0,2},{2,0},{1,3},{3,1},{4,6},{6,4},{5,7},{7,5},{8,10},{10,8},{9,1... | collective-permute-start | bytes 6291464 | tf_op jit(solution)/shard_map/ppermute | solution.py:25
  407.7 71.8 %collective-permute-start.43 = (bf16[512,2048]{1,0:T(8,128)(2,1)}, bf16[512,2048]{1,0:T(8,128)(2,1)}, u32[]{:S(2)}, u32[]{:S(2)}) collective-permute-start(bf16[512,2048]{1,0:T(8,128)(2,1)} %get-tuple-element.67), channel_id=1, source_target_pairs={{0,2},{2,0},{1,3},{3,1},{4,6},{6,4},{5,7},{7,5},{8,10},{10,8},{9,1... | collective-permute-start | bytes 6291464 | tf_op jit(solution)/shard_map/ppermute | solution.py:25
  407.7 75.7 %collective-permute-start.39 = (bf16[512,2048]{1,0:T(8,128)(2,1)}, bf16[512,2048]{1,0:T(8,128)(2,1)}, u32[]{:S(2)}, u32[]{:S(2)}) collective-permute-start(bf16[512,2048]{1,0:T(8,128)(2,1)} %get-tuple-element.65), channel_id=1, source_target_pairs={{0,2},{2,0},{1,3},{3,1},{4,6},{6,4},{5,7},{7,5},{8,10},{10,8},{9,1... | collective-permute-start | bytes 6291464 | tf_op jit(solution)/shard_map/ppermute | solution.py:25
  408.2 79.2 %collective-permute-start.30 = (bf16[512,2048]{1,0:T(8,128)(2,1)}, bf16[512,2048]{1,0:T(8,128)(2,1)}, u32[]{:S(2)}, u32[]{:S(2)}) collective-permute-start(bf16[512,2048]{1,0:T(8,128)(2,1)} %get-tuple-element.63), channel_id=1, source_target_pairs={{0,2},{2,0},{1,3},{3,1},{4,6},{6,4},{5,7},{7,5},{8,10},{10,8},{9,1... | collective-permute-start | bytes 6291464 | tf_op jit(solution)/shard_map/ppermute | solution.py:25
  416.8 48.8 %collective-permute-start.76 = (bf16[1024,512]{1,0:T(8,128)(2,1)}, bf16[1024,512]{1,0:T(8,128)(2,1)S(1)}, u32[]{:S(2)}, u32[]{:S(2)}) collective-permute-start(bf16[1024,512]{1,0:T(8,128)(2,1)} %dynamic-slice_convert_fusion.2), channel_id=1, source_target_pairs={{0,16},{16,0},{1,17},{17,1},{2,18},{18,2},{3,19},{19,3},{4,20},{20... | collective-permute-start | bytes 3145736 | tf_op jit(solution)/shard_map/ppermute | solution.py:25
  465.7 93.7 %collective-permute-start.77 = (bf16[1024,512]{1,0:T(8,128)(2,1)}, bf16[1024,512]{1,0:T(8,128)(2,1)}, u32[]{:S(2)}, u32[]{:S(2)}) collective-permute-start(bf16[1024,512]{1,0:T(8,128)(2,1)} %dynamic-slice_convert_fusion.1), channel_id=1, source_target_pairs={{0,16},{16,0},{1,17},{17,1},{2,18},{18,2},{3,19},{19,3},{4,20},{20... | collective-permute-start | bytes 3145736 | tf_op jit(solution)/shard_map/ppermute | solution.py:25
  470.0 94.2 %all-to-all-start.3 = ((bf16[8,128,512]{2,1,0:T(8,128)(2,1)}), bf16[8,128,512]{2,1,0:T(8,128)(2,1)}, u32[]{:S(2)}, u32[]{:S(2)}) async-start(bf16[8,128,512]{2,1,0:T(8,128)(2,1)} %bitcast.223), calls=%async_computation.3 | async-start | bytes 2097152 | tf_op jit(solution)/shard_map/all_to_all | solution.py:675
  476.2 86.8 %collective-permute-start.78 = (bf16[512,1024]{1,0:T(8,128)(2,1)}, bf16[512,1024]{1,0:T(8,128)(2,1)S(1)}, u32[]{:S(2)}, u32[]{:S(2)}) collective-permute-start(bf16[512,1024]{1,0:T(8,128)(2,1)} %dynamic-slice_convert_fusion), channel_id=1, source_target_pairs={{0,16},{16,0},{1,17},{17,1},{2,18},{18,2},{3,19},{19,3},{4,20},{20... | collective-permute-start | bytes 3145736 | tf_op jit(solution)/shard_map/ppermute | solution.py:25
  487.4 46.3 %collective-permute-start.40 = (bf16[256,2048]{1,0:T(8,128)(2,1)S(1)}, bf16[256,2048]{1,0:T(8,128)(2,1)S(1)}, u32[]{:S(2)}, u32[]{:S(2)}) collective-permute-start(bf16[256,2048]{1,0:T(8,128)(2,1)S(1)} %slice.558), channel_id=1, source_target_pairs={{0,4},{4,0},{8,12},{12,8},{1,5},{5,1},{9,13},{13,9},{2,6},{6,2},{1... | collective-permute-start | bytes 3145736 | tf_op jit(solution)/shard_map/ppermute | solution.py:25
  559.3 44.6 %collective-permute-start.42 = (bf16[256,2048]{1,0:T(8,128)(2,1)}, bf16[256,2048]{1,0:T(8,128)(2,1)}, u32[]{:S(2)}, u32[]{:S(2)}) collective-permute-start(bf16[256,2048]{1,0:T(8,128)(2,1)} %pad_maximum_fusion.12), channel_id=1, source_target_pairs={{0,1},{1,0},{2,3},{3,2},{4,5},{5,4},{6,7},{7,6},{8,9},{9,8},{10,11... | collective-permute-start | bytes 3145736 | tf_op jit(solution)/shard_map/ppermute | solution.py:25
  564.2 45.3 %all-to-all-start.4 = ((bf16[8,128,512]{2,1,0:T(8,128)(2,1)}), bf16[8,128,512]{2,1,0:T(8,128)(2,1)}, u32[]{:S(2)}, u32[]{:S(2)}) async-start(bf16[8,128,512]{2,1,0:T(8,128)(2,1)} %bitcast.224), calls=%async_computation.4 | async-start | bytes 2097152 | tf_op jit(solution)/shard_map/all_to_all | solution.py:676
  674.8 48.1 %collective-permute-start.71 = (bf16[2,1,2,2,256,128]{5,4,3,2,1,0:T(8,128)(2,1)}, bf16[2,1,2,2,256,128]{5,4,3,2,1,0:T(8,128)(2,1)}, u32[]{:S(2)}, u32[]{:S(2)}) collective-permute-start(bf16[2,1,2,2,256,128]{5,4,3,2,1,0:T(8,128)(2,1)} %constant_dynamic-slice_fusion), channel_id=1, source_target_pairs={{0,8},{4,12},{8,0},{12,4},{1,9},{5,13},{9,1},{13,5},{2,10},{6,14},... | collective-permute-start | bytes 1572872 | tf_op jit(solution)/shard_map/ppermute | solution.py:25
  677.3 47.7 %collective-permute-start.68 = (bf16[2,2,1,2,256,128]{5,4,3,2,1,0:T(8,128)(2,1)}, bf16[2,2,1,2,256,128]{5,4,3,2,1,0:T(8,128)(2,1)}, u32[]{:S(2)}, u32[]{:S(2)}) collective-permute-start(bf16[2,2,1,2,256,128]{5,4,3,2,1,0:T(8,128)(2,1)} %constant_dynamic-slice_fusion.1), channel_id=1, source_target_pairs={{0,4},{4,0},{8,12},{12,8},{1,5},{5,1},{9,13},{13,9},{2,6},{6,2},{1... | collective-permute-start | bytes 1572872 | tf_op jit(solution)/shard_map/ppermute | solution.py:25
  712.6 48.8 %collective-permute-start.55 = (bf16[256,2176]{1,0:T(8,128)(2,1)}, bf16[256,2176]{1,0:T(8,128)(2,1)}, u32[]{:S(2)}, u32[]{:S(2)}) collective-permute-start(bf16[256,2176]{1,0:T(8,128)(2,1)} %dynamic-slice_bitcast_fusion), channel_id=1, source_target_pairs={{0,2},{2,0},{1,3},{3,1},{4,6},{6,4},{5,7},{7,5},{8,10},{10,8},{9,1... | collective-permute-start | bytes 3342344 | tf_op jit(solution)/shard_map/ppermute | solution.py:25
  721.6 44.5 %collective-permute-start.61 = (bf16[2,2,1,2,128,384]{5,4,3,2,1,0:T(8,128)(2,1)S(1)}, bf16[2,2,1,2,128,384]{5,4,3,2,1,0:T(8,128)(2,1)S(1)}, u32[]{:S(2)}, u32[]{:S(2)}) collective-permute-start(bf16[2,2,1,2,128,384]{5,4,3,2,1,0:T(8,128)(2,1)S(1)} %constant_dynamic-slice_fusion.3), channel_id=1, source_target_pairs={{0,4},{4,0},{8,12},{12,8},{1,5},{5,1},{9,13},{13,9},{2,6},{6,2},{1... | collective-permute-start | bytes 2359304 | tf_op jit(solution)/shard_map/ppermute | solution.py:25
  (175 other events, 2610.9 us)

commit v2 on v1

v2 whole, which is shorter than its diff:
```python
import functools

import jax
import jax.numpy as jnp
import numpy as np
from jax import lax
from jax.experimental import pallas as pl
from jax.experimental.pallas import tpu as pltpu
from jax.sharding import Mesh
from jax.sharding import PartitionSpec as P

HEAD_SIZE = 64
FEATURE_HALF = 64
SOFTMAX_KEYS = 64
CORES = 2


EPS = 1e-05
FLOAT = jnp.float32
BFLOAT = jnp.bfloat16


def ordered(which, mine, other, dim):
    return jnp.where(
        which == 0,
        jnp.concatenate([mine, other], axis=dim),
        jnp.concatenate([other, mine], axis=dim),
    )


def frequencies(head_width):
    inverse = 1.0 / 500000.0 ** (np.arange(0, head_width, 2) / head_width)
    wavelen = 2.0 * np.pi / inverse
    smooth = (8192.0 / wavelen - 1.0) / 3.0
    blended = (1.0 - smooth) * inverse / 32.0 + smooth * inverse
    return np.where(wavelen > 8192.0, inverse / 32.0, np.where(wavelen < 2048.0, inverse, blended))


def rotation(positions, head_width):
    freq_table = jnp.asarray(frequencies(head_width), FLOAT)
    turned = positions.astype(FLOAT)[:, None] * freq_table[None, :]
    cosine, sine = jnp.cos(turned), jnp.sin(turned)
    return (
        jnp.concatenate([cosine, cosine], axis=-1),
        jnp.concatenate([-sine, sine], axis=-1),
    )


def spread(table, width):
    return jnp.tile(table, (1, width // table.shape[1]))


def locate(places, lengths):
    doc_ends = jnp.cumsum(lengths)
    passed = places[:, None] >= doc_ends[None, :]
    segment = jnp.sum(passed.astype(jnp.int32), axis=1)
    doc_begin = jnp.sum(jnp.where(passed, lengths[None, :], 0), axis=1)
    return (jnp.where(places < 0, -1, segment), places - doc_begin)


def product(left, right):
    return jnp.dot(left, right, preferred_element_type=FLOAT)


def product_t(left, right):
    return lax.dot_general(left, right, (((1,), (1,)), ((), ())), preferred_element_type=FLOAT)


def t_product(left, right):
    return lax.dot_general(left, right, (((0,), (0,)), ((), ())), preferred_element_type=FLOAT)


def dot(left, right):
    return lax.dot_general(left, right, (((1,), (0,)), ((), ())), preferred_element_type=FLOAT)


def lanes(shape):
    return lax.broadcasted_iota(jnp.int32, shape, 1)


def half_sums(rows):
    first = lax.broadcasted_iota(jnp.int32, (128, 128), 0) < FEATURE_HALF
    ones = jnp.where(first == (lanes((128, 128)) < FEATURE_HALF), 1.0, 0.0).astype(BFLOAT)
    return dot(rows, ones)


def two_softmax(mixed):
    low = lanes(mixed.shape) < FEATURE_HALF
    top = jnp.max(jnp.where(low, mixed, -jnp.inf), axis=1, keepdims=True)
    top_other = jnp.max(jnp.where(low, -jnp.inf, mixed), axis=1, keepdims=True)
    raised = jnp.exp(mixed - jnp.where(low, top, top_other))
    return (raised / half_sums(raised.astype(BFLOAT))).astype(BFLOAT)


def phi_kernel(group, q_ref, k_ref, vm_ref, fq_ref, fk_ref, phi_q_ref, phi_k_ref, state_ref):
    keys = k_ref[0]
    masked = vm_ref[0]
    for head in range(group):
        rows = q_ref[:, head * HEAD_SIZE : (head + 1) * HEAD_SIZE]
        phi_q_ref[head] = two_softmax(dot(rows, fq_ref[head]))
        phi_k = two_softmax(dot(keys, fk_ref[head]))
        phi_k_ref[head] = phi_k
        state_ref[head] = t_product(masked, phi_k).astype(BFLOAT)


def tile_masks(seg_q, seg_k, at):
    width = at + 256
    same = seg_q == seg_k[:, :width]
    row = lax.broadcasted_iota(jnp.int32, (128, 256), 0)
    col = lanes((128, 256))
    earlier = col <= row + SOFTMAX_KEYS
    window = (col > row + SOFTMAX_KEYS) & (col <= row + 128) & same[:, at:]
    return same[:, :at], window, earlier & same[:, at:]


def tile_weights(rows, phi_rows, k_ref, phi_k, at, masks):
    far, window, earlier = masks
    scale = HEAD_SIZE ** (-0.5)
    raw = product_t(rows, k_ref[0, at : at + 256])
    window_exp = jnp.where(window, jnp.exp(jnp.where(window, scale * raw, 0.0)), 0.0)
    linear = product_t(phi_rows, phi_k[: at + 256])
    near = jnp.where(earlier, linear[:, at:], window_exp)
    if at == 0:
        return window_exp, near.astype(BFLOAT)
    return window_exp, jnp.concatenate(
        [jnp.where(far, linear[:, :at], 0.0), near], axis=1
    ).astype(BFLOAT)


def intra_kernel(group, q_ref, k_ref, v_ref, phi_q_ref, phi_k_ref, seg_q_ref, seg_k_ref, num_ref):
    for at in range(0, q_ref.shape[0], 128):
        masks = tile_masks(seg_q_ref[at : at + 128], seg_k_ref[...], at)
        for head in range(group):
            rows = q_ref[at : at + 128, head * HEAD_SIZE : (head + 1) * HEAD_SIZE]
            weights = tile_weights(
                rows, phi_q_ref[head, at : at + 128], k_ref, phi_k_ref.at[head], at, masks
            )[1]
            num_ref[head, at : at + 128] = dot(weights, v_ref[0, : at + 256])


def finish_kernel(group, num_ref, phi_q_ref, state_ref, cont_ref, att_ref, den_ref):
    cont = cont_ref[...]
    den = jnp.zeros(den_ref.shape[1:], FLOAT)
    for head in range(group):
        total = num_ref[head] + cont * product_t(phi_q_ref[head], state_ref[head])
        below = total[:, HEAD_SIZE : HEAD_SIZE + 1]
        att_ref[:, head * HEAD_SIZE : (head + 1) * HEAD_SIZE] = (
            total[:, :HEAD_SIZE] / below
        ).astype(BFLOAT)
        den = jnp.where(lanes(den.shape) == head, below, den)
    den_ref[0] = den


def grad_numer_kernel(group, da_ref, att_ref, den_ref, phi_q_ref, cont_ref, dn_ref, ds_ref):
    cont = cont_ref[...]
    for head in range(group):
        cols = slice(head * HEAD_SIZE, (head + 1) * HEAD_SIZE)
        numer = da_ref[:, cols] / den_ref[0][:, head : head + 1]
        denom = -jnp.sum(numer * att_ref[:, cols].astype(FLOAT), axis=1, keepdims=True)
        high = denom.astype(BFLOAT).astype(FLOAT)
        wide = jnp.concatenate([numer, jnp.zeros_like(numer)], axis=1)
        lane = lanes(wide.shape)
        wide = jnp.where(lane == HEAD_SIZE, high, wide)
        wide = jnp.where(lane == HEAD_SIZE + 1, denom - high, wide)
        dn_ref[head] = wide.astype(BFLOAT)
        state = t_product((wide * cont).astype(BFLOAT), phi_q_ref[head])
        row = lax.broadcasted_iota(jnp.int32, state.shape, 0)
        both = state[HEAD_SIZE : HEAD_SIZE + 1] + state[HEAD_SIZE + 1 : HEAD_SIZE + 2]
        state = jnp.where(row == HEAD_SIZE, both, jnp.where(row > HEAD_SIZE, 0.0, state))
        ds_ref[head] = state.astype(BFLOAT)


def intra_back_kernel(
    group, q_ref, k_ref, v_ref, phi_q_ref, phi_k_ref, dn_ref, seg_q_ref, seg_k_ref,
    dq_ref, dk_ref, dv_ref, dphi_q_ref, dphi_k_ref,
):
    scale = HEAD_SIZE ** (-0.5)
    dk_ref[...] = jnp.zeros(dk_ref.shape, FLOAT)
    dv_ref[...] = jnp.zeros(dv_ref.shape, FLOAT)
    dphi_k_ref[...] = jnp.zeros(dphi_k_ref.shape, FLOAT)
    for at in range(0, q_ref.shape[0], 128):
        masks = tile_masks(seg_q_ref[at : at + 128], seg_k_ref[...], at)
        tile = slice(at, at + 128)
        width = at + 256
        for head in range(group):
            cols = slice(head * HEAD_SIZE, (head + 1) * HEAD_SIZE)
            rows = q_ref[tile, cols]
            phi_rows = phi_q_ref[head, tile]
            numer = dn_ref[head, tile]
            window_exp, weights = tile_weights(
                rows, phi_rows, k_ref, phi_k_ref.at[head], at, masks
            )
            grad = product_t(numer, v_ref[0, :width])
            near = grad[:, at:]
            grad_raw = (scale * near * window_exp).astype(BFLOAT)
            grad_linear = jnp.where(masks[2], near, 0.0)
            if at > 0:
                grad_linear = jnp.concatenate(
                    [jnp.where(masks[0], grad[:, :at], 0.0), grad_linear], axis=1
                )
            grad_linear = grad_linear.astype(BFLOAT)
            dv_ref[0, :width] += t_product(weights, numer)
            dphi_q_ref[head, tile] = dot(grad_linear, phi_k_ref[head, :width])
            dphi_k_ref[head, :width] += t_product(grad_linear, phi_rows)
            dq_ref[tile, cols] = dot(grad_raw, k_ref[0, at:width])
            dk_ref[0, at:width] += t_product(grad_raw, rows)


def softmax_back(phi, grad):
    wide = phi.astype(FLOAT)
    terms = grad * wide
    high = terms.astype(BFLOAT)
    low = (terms - high.astype(FLOAT)).astype(BFLOAT)
    mean = (half_sums(high) + half_sums(low)) / half_sums(phi)
    return (wide * (grad - mean)).astype(BFLOAT)


def features_back_kernel(
    group, q_ref, k_ref, v_ref, phi_q_ref, phi_k_ref, dn_ref, fq_ref, fk_ref, state_ref, ds_ref,
    cont_ref, carry_ref, dq_in, dk_in, dv_in, dphi_q_ref, dphi_k_ref,
    dq_ref, dk_ref, dv_ref, gq_ref, gk_ref,
):
    cont = cont_ref[...]
    carry = carry_ref[...]
    keys = k_ref[0]
    dk = dk_in[0]
    dv = dv_in[0]
    for head in range(group):
        cols = slice(head * HEAD_SIZE, (head + 1) * HEAD_SIZE)
        grad_state = ds_ref[head]
        phi_k = phi_k_ref[head]
        grad_q = dphi_q_ref[head] + cont * dot(dn_ref[head], state_ref[head])
        grad_k = dphi_k_ref[head] + carry * dot(v_ref[0], grad_state)
        dv = dv + carry * product_t(phi_k, grad_state)
        mixed_q = softmax_back(phi_q_ref[head], grad_q)
        mixed_k = softmax_back(phi_k, grad_k)
        dq_ref[:, cols] = dq_in[:, cols] + product_t(mixed_q, fq_ref[head])
        dk = dk + product_t(mixed_k, fk_ref[head])
        gq_ref[head] = t_product(q_ref[:, cols], mixed_q)
        gk_ref[head] = t_product(keys, mixed_k)
    dk_ref[0] = dk
    dv_ref[0] = dv


def remote(source, target, send_sem, recv_sem, **where):
    return pltpu.make_async_remote_copy(
        src_ref=source,
        dst_ref=target,
        send_sem=send_sem,
        recv_sem=recv_sem,
        device_id=where,
        device_id_type=pl.DeviceIdType.MESH,
    )


def greet(peers):
    barrier = pltpu.get_barrier_semaphore()
    for where in peers:
        pl.semaphore_signal(barrier, inc=1, device_id=where, device_id_type=pl.DeviceIdType.MESH)
    pl.semaphore_wait(barrier, len(peers))


def feed_kernel(
    chips, x_ref, c_ref, ff_ref,
    grad_ref, out_ref, ffg_ref, got_ref,
    x_buf, c_buf, gg_ref, gu_ref, gd_ref, keep, sib_out, sib_in, part, stage, wide,
    load_sems, stage_sems, sib_send, sib_recv, part_send, part_recv, cross_sems, ffg_sems, free_sem,
):
    core, chip, tensor = (lax.axis_index(name) for name in ("core", "chip", "tensor"))
    rows = keep.shape[2]
    count, model = x_buf.shape[1:]
    units = ff_ref.shape[2]
    gate_ref, up_ref, down_ref = (ff_ref.at[which] for which in range(3))
    sibling = {"core": 1 - core}
    greet(
        [sibling, {"tensor": 1 - tensor}]
        + [{"chip": lax.rem(chip + step, chips)} for step in range(1, chips)]
    )

    def place(step):
        return lax.rem(step + 1, chips)

    def loads(step):
        slot = lax.rem(step, 2)
        return [
            pltpu.make_async_copy(ref.at[place(step)], buf.at[slot], load_sems.at[at, slot])
            for at, (ref, buf) in enumerate(((x_ref, x_buf), (c_ref, c_buf)))
        ]

    def to_sibling(step):
        slot = lax.rem(step, 2)
        return remote(
            sib_out.at[slot], sib_in.at[slot], sib_send.at[slot], sib_recv.at[slot], **sibling
        )

    def stage_copy(step):
        slot = lax.rem(step, 2)
        return pltpu.make_async_copy(stage.at[slot], out_ref.at[place(step)], stage_sems.at[slot])

    def to_chip(step):
        return remote(
            part.at[step],
            got_ref.at[step],
            part_send.at[step],
            part_recv.at[step],
            chip=lax.rem(chip + step + 1, chips),
        )

    def total(step, which):
        slot = lax.rem(step, 2)
        return keep[slot, which].astype(FLOAT) + sib_in[slot, which].astype(FLOAT)

    for copy in loads(0):
        copy.start()
    gg_ref[...] = jnp.zeros(gg_ref.shape, FLOAT)
    gu_ref[...] = jnp.zeros(gu_ref.shape, FLOAT)
    gd_ref[...] = jnp.zeros(gd_ref.shape, FLOAT)

    def body(step, nothing):
        slot = lax.rem(step, 2)
        for copy in loads(step):
            copy.wait()

        @pl.when(step < chips - 1)
        def _():
            for copy in loads(step + 1):
                copy.start()

        tokens = x_buf[slot]
        cotangent = c_buf[slot]
        gate = dot(tokens, gate_ref[...])
        up = dot(tokens, up_ref[...])
        grad = dot(cotangent, down_ref[...])
        sigmoid = 1.0 / (1.0 + jnp.exp(-gate))
        silu = gate * sigmoid
        hidden = (silu * up).astype(BFLOAT)
        grad_gate = (grad * up * (sigmoid + silu * (1.0 - sigmoid))).astype(BFLOAT)
        grad_up = (grad * silu).astype(BFLOAT)

        @pl.when(step >= 2)
        def _():
            to_sibling(step).wait_send()
            pl.semaphore_wait(free_sem, 1)

        def back(part_of):
            return (
                product_t(grad_gate[part_of], gate_ref[...])
                + product_t(grad_up[part_of], up_ref[...])
            ).astype(BFLOAT)

        def out(part_of):
            return product_t(hidden[part_of], down_ref[...]).astype(BFLOAT)

        mine, theirs = slice(0, rows), slice(rows, 2 * rows)
        sib_out[slot, 0] = back(theirs)
        sib_out[slot, 1] = out(theirs)
        to_sibling(step).start()
        keep[slot, 0] = back(mine)
        keep[slot, 1] = out(mine)

        @pl.when(step > 0)
        def _():
            before = step - 1
            to_sibling(before).wait_recv()
            part[before] = total(before, 0).astype(BFLOAT)
            to_chip(before).start()

            @pl.when(step > 2)
            def _():
                stage_copy(before).wait()

            stage[lax.rem(before, 2)] = total(before, 1).astype(BFLOAT)
            stage_copy(before).start()
            pl.semaphore_signal(free_sem, inc=1, device_id=sibling, device_id_type=pl.DeviceIdType.MESH)

        gg_ref[...] += t_product(tokens, grad_gate)
        gu_ref[...] += t_product(tokens, grad_up)
        gd_ref[...] += t_product(cotangent, hidden)
        return nothing

    lax.fori_loop(0, chips, body, 0)
    last = chips - 1
    to_sibling(last).wait_recv()
    grad_ref[...] = total(last, 0)
    if chips > 2:
        stage_copy(last).wait()
    stage[last % 2] = total(last, 1).astype(BFLOAT)
    stage_copy(last).start()
    per = model // units
    ffg_copies = []
    for which, ref in enumerate((gg_ref, gu_ref, gd_ref)):
        for at in range(model // count):
            place_at = which * (model // count) + at
            buf = (x_buf, c_buf)[place_at // (2 * per)]
            spot = buf.at[(place_at // per) % 2, :, pl.ds((place_at % per) * units, units)]
            piece = pl.ds(at * count, count)
            spot[...] = ref[piece].astype(BFLOAT)
            copy = pltpu.make_async_copy(spot, ffg_ref.at[which, piece], ffg_sems.at[place_at])
            copy.start()
            ffg_copies.append(copy)

    def finish(step, nothing):
        to_chip(step).wait_recv()
        load = pltpu.make_async_copy(got_ref.at[step], wide.at[0], load_sems.at[0, 0])
        load.start()
        load.wait()
        grad_ref[...] += wide[0].astype(FLOAT)
        return nothing

    lax.fori_loop(0, chips - 1, finish, 0)
    wide[0] = grad_ref[...].astype(BFLOAT)
    across = remote(wide.at[0], wide.at[1], cross_sems.at[0], cross_sems.at[1], tensor=1 - tensor)
    across.start()

    def drain(step, nothing):
        to_chip(step).wait_send()
        return nothing

    lax.fori_loop(0, chips - 1, drain, 0)
    for copy in ffg_copies:
        copy.wait()
    for step in range(max(0, chips - 2), chips):
        to_sibling(step).wait_send()
        stage_copy(step).wait()
    pl.semaphore_wait(free_sem, min(1, chips - 1))
    across.wait()
    grad_ref[...] = wide[0].astype(FLOAT) + wide[1].astype(FLOAT)


def feed(tokens, cotangent, weights):
    chips, count, model = tokens.shape
    rows = count // CORES
    units = weights.shape[2]
    near = pl.BlockSpec(memory_space=pltpu.VMEM)
    far = pl.BlockSpec(memory_space=pl.ANY)
    return pl.pallas_call(
        functools.partial(feed_kernel, chips),
        in_specs=[far, far, near],
        out_specs=[near, far, far, far],
        out_shape=[
            jax.ShapeDtypeStruct((rows, model), FLOAT),
            jax.ShapeDtypeStruct((chips, rows, model), BFLOAT),
            jax.ShapeDtypeStruct(weights.shape, BFLOAT),
            jax.ShapeDtypeStruct((chips - 1, rows, model), BFLOAT),
        ],
        scratch_shapes=[
            pltpu.VMEM((2, count, model), BFLOAT),
            pltpu.VMEM((2, count, model), BFLOAT),
            pltpu.VMEM((model, units), FLOAT),
            pltpu.VMEM((model, units), FLOAT),
            pltpu.VMEM((model, units), FLOAT),
            pltpu.VMEM((2, 2, rows, model), BFLOAT),
            pltpu.VMEM((2, 2, rows, model), BFLOAT),
            pltpu.VMEM((2, 2, rows, model), BFLOAT),
            pltpu.VMEM((chips - 1, rows, model), BFLOAT),
            pltpu.VMEM((2, rows, model), BFLOAT),
            pltpu.VMEM((2, rows, model), BFLOAT),
            pltpu.SemaphoreType.DMA((2, 2)),
            dma_row(2),
            dma_row(2),
            dma_row(2),
            dma_row(chips - 1),
            dma_row(chips - 1),
            dma_row(2),
            dma_row(3 * model // count),
            pltpu.SemaphoreType.REGULAR,
        ],
        compiler_params=pltpu.CompilerParams(
            vmem_limit_bytes=62 * 1024 * 1024, collective_id=1, has_side_effects=True
        ),
        cost_estimate=pl.CostEstimate(
            flops=18 * chips * count * model * units,
            bytes_accessed=8 * chips * count * model,
            transcendentals=0,
        ),
    )(tokens, cotangent, weights)


def dma_row(count):
    return pltpu.SemaphoreType.DMA((count,))


def front_kernel(
    chips, kv_heads, group,
    hid_ref, again_ref, fgain_ref, downs_ref, ups_ref, cos_ref, sin_ref, fq_ref, fk_ref,
    seg_q_ref, seg_k_ref, cont_ref, carry_ref, coef_ref, odown_ref, oup_ref,
    wqkv_ref, wo_ref, gate_ref, up_ref, down_ref, cot_ref,
    qkv_ref, wof_ref, normed_ref, low_ref, mid_ref, res_ref, q_ref, k_ref, v_ref,
    phi_q_ref, phi_k_ref, att_ref, den_ref, state_ref,
    ff_ref, call_ref, xall_ref,
    hid_sib, vm, rim_out, rim_in, st_out, st_in, num, br_out, br_in, tz_out, tz_in, xn,
    hid_sem, q1_send, q1_recv, q2_send, q2_recv, o1_send, o1_recv, o2_send, o2_recv,
    ff_send, ff_recv, local_sems, c_send, c_recv, cf_send, cf_recv, x_send, x_recv, xf_send, xf_recv,
    rim_sem, st_send, st_recv, br_sem, tz_sem,
):
    dp, chip, core, tensor = (lax.axis_index(name) for name in ("dp", "chip", "core", "tensor"))
    own = hid_ref.shape[0]
    tokens = CORES * own
    model = hid_ref.shape[1]
    shard = wqkv_ref.shape[1]
    q_width = q_ref.shape[1]
    pairs = CORES * chips
    units = ff_ref.shape[2]
    other = 1 - core
    there = 1 - dp
    sibling = {"core": other}
    at_chip = [lax.rem(chip + step, chips) for step in range(1, chips)]
    behind = [lax.rem(chip + chips - step, chips) for step in range(1, chips)]
    greet(
        [sibling, {"tensor": 1 - tensor}]
        + [{"dp": there, "core": core}, {"dp": there, "core": other}]
        + [{"chip": to, "core": which} for to in at_chip for which in (core, other)]
        + [{"dp": there, "chip": to, "core": which} for to in at_chip for which in (core, other)]
    )

    def first(source, target, send, recv):
        rows = pl.ds(((dp * chips + chip) * CORES + core) * shard, shard)
        return [
            remote(source.at[other], target.at[rows], send.at[0], recv.at[0], core=other),
            remote(source.at[core], target.at[rows], send.at[1], recv.at[1], dp=there),
            remote(source.at[other], target.at[rows], send.at[2], recv.at[2], dp=there, core=other),
        ]

    def local(source, target, at):
        rows = pl.ds(((dp * chips + chip) * CORES + core) * shard, shard)
        return pltpu.make_async_copy(source.at[core], target.at[rows], local_sems.at[at])

    def second(target, send, recv, side):
        group_at = dp if side == 0 else there
        rows = pl.ds((group_at * chips + chip) * CORES * shard, CORES * shard)
        return [
            remote(target.at[rows], target.at[rows], send.at[side, at], recv.at[side, at], chip=to)
            for at, to in enumerate(at_chip)
        ]

    q_first = first(wqkv_ref, qkv_ref, q1_send, q1_recv)
    o_first = first(wo_ref, wof_ref, o1_send, o1_recv)
    q_local, o_local = local(wqkv_ref, qkv_ref, 0), local(wo_ref, wof_ref, 1)
    q_second = [second(qkv_ref, q2_send, q2_recv, side) for side in range(2)]
    o_second = [second(wof_ref, o2_send, o2_recv, side) for side in range(2)]
    hid_copy = remote(hid_ref, hid_sib, hid_sem.at[0], hid_sem.at[1], **sibling)
    q_local.start()
    hid_copy.start()
    for copy in q_first:
        copy.start()

    ff_rows = pl.ds(((dp * chips + chip) * CORES + core) * shard, shard)
    ff_sources = (gate_ref, up_ref, down_ref)

    def ff_copy(which, step, side):
        to = lax.rem(chip * CORES + core + step, pairs)
        return remote(
            ff_sources[which].at[:, pl.ds(pl.multiple_of(to * units, units), units)],
            ff_ref.at[which, ff_rows],
            ff_send.at[which],
            ff_recv.at[which],
            dp=dp if side == 0 else there,
            chip=to // CORES,
            core=lax.rem(to, CORES),
        )

    def ff_local(which):
        return pltpu.make_async_copy(
            ff_sources[which].at[:, pl.ds(pl.multiple_of((chip * CORES + core) * units, units), units)],
            ff_ref.at[which, ff_rows],
            local_sems.at[2 + which],
        )

    def ff_start(which, side):
        def one(step, nothing):
            ff_copy(which, step, side).start()
            return nothing

        lax.fori_loop(1 - side, pairs, one, 0)

    def row_copies(source, target, send, recv):
        return [
            remote(source, target.at[step + 1, pl.ds(0, own)], send.at[step], recv.at[step], chip=to)
            for step, to in enumerate(behind)
        ]

    def forward_copy(source, target, send, recv, step):
        return remote(source, target.at[step, pl.ds(own, own)], send.at[step], recv.at[step], **sibling)

    c_copies = row_copies(cot_ref, call_ref, c_send, c_recv)
    x_copies = row_copies(xn, xall_ref, x_send, x_recv)
    c_forward = [
        forward_copy(cot_ref if step == 0 else call_ref.at[step, pl.ds(0, own)], call_ref, cf_send, cf_recv, step)
        for step in range(chips)
    ]
    x_forward = [
        forward_copy(xn if step == 0 else xall_ref.at[step, pl.ds(0, own)], xall_ref, xf_send, xf_recv, step)
        for step in range(chips)
    ]
    c_local = pltpu.make_async_copy(cot_ref, call_ref.at[0, pl.ds(0, own)], local_sems.at[5])
    x_local = pltpu.make_async_copy(xn, xall_ref.at[0, pl.ds(0, own)], local_sems.at[6])

    def normalized(rows, gain):
        return (rows * lax.rsqrt(jnp.mean(rows * rows, axis=1, keepdims=True) + EPS) * gain).astype(BFLOAT)

    hidden = hid_ref[...].astype(FLOAT)
    normed_ref[pl.ds(pl.multiple_of(core * own, own), own)] = normalized(hidden, again_ref[...])
    q_first[0].wait_recv()
    q_local.wait()
    for copy in q_second[0]:
        copy.start()
    hid_copy.wait()
    normed_ref[pl.ds(pl.multiple_of(other * own, own), own)] = normalized(
        hid_sib[...].astype(FLOAT), again_ref[...]
    )
    low_ref[...] = dot(normed_ref[...], downs_ref[...]).astype(BFLOAT)
    q_first[1].wait_recv()
    q_first[2].wait_recv()
    for copy in q_second[1]:
        copy.start()
    o_local.start()
    for copy in o_first:
        copy.start()
    for which in range(3):
        ff_local(which).start()
    c_local.start()
    ff_start(0, 1)
    o_first[0].wait_recv()
    o_local.wait()
    for copy in o_second[0]:
        copy.start()
    for side in range(2):
        for copy in q_second[side]:
            copy.wait_recv()
    o_first[1].wait_recv()
    o_first[2].wait_recv()
    for copy in o_second[1]:
        copy.start()
    ff_start(1, 1)
    ff_start(0, 0)

    pre = dot(normed_ref[...], qkv_ref[...]) + dot(low_ref[...], ups_ref[...])
    half = HEAD_SIZE // 2
    first_half = lax.rem(lanes((tokens, 128)), HEAD_SIZE) < half

    def rotated(block):
        turned = jnp.where(first_half, pltpu.roll(block, 128 - half, 1), pltpu.roll(block, half, 1))
        return (block * cos_ref[...] + turned * sin_ref[...]).astype(BFLOAT)

    for at in range(0, q_width, 128):
        q_ref[:, at : at + 128] = rotated(pre[:, at : at + 128])
    keys = rotated(pre[:, q_width : q_width + 128])
    values = pre[:, q_width + 128 :].astype(BFLOAT)
    rim_out[:, :128] = keys[tokens - SOFTMAX_KEYS :]
    rim_out[:, 128:] = values[tokens - SOFTMAX_KEYS :]
    rim_copy = remote(rim_out, rim_in, rim_sem.at[0], rim_sem.at[1], chip=lax.rem(chip + 1, chips))

    @pl.when(chip < chips - 1)
    def _():
        rim_copy.start()

    def tailed(rows):
        tail = jnp.where(lanes((rows.shape[0], 128 - HEAD_SIZE)) < 2, 1.0, 0.0).astype(BFLOAT)
        return jnp.concatenate([rows, tail], axis=1)

    gap = 128 - SOFTMAX_KEYS
    for head in range(kv_heads):
        cols = slice(head * HEAD_SIZE, (head + 1) * HEAD_SIZE)
        k_ref[head, 128:] = keys[:, cols]
        v_ref[head, 128:] = tailed(values[:, cols])
        k_ref[head, :gap] = jnp.zeros((gap, HEAD_SIZE), BFLOAT)
        v_ref[head, :gap] = tailed(jnp.zeros((gap, HEAD_SIZE), BFLOAT))

    @pl.when(chip == 0)
    def _():
        rim_in[...] = jnp.zeros(rim_in.shape, BFLOAT)

    @pl.when(chip > 0)
    def _():
        rim_copy.wait_recv()

    carry = carry_ref[...]
    for head in range(kv_heads):
        cols = slice(head * HEAD_SIZE, (head + 1) * HEAD_SIZE)
        k_ref[head, gap:128] = rim_in[:, cols]
        v_ref[head, gap:128] = tailed(rim_in[:, 128 + head * HEAD_SIZE : 128 + (head + 1) * HEAD_SIZE])
        vm[head] = (v_ref[head].astype(FLOAT) * carry).astype(BFLOAT)

    def views(at):
        heads = pl.ds(at * group, group)
        one = pl.ds(at, 1)
        wide = pl.ds(at * group * HEAD_SIZE, group * HEAD_SIZE)
        return heads, one, wide

    for at in range(kv_heads):
        heads, one, wide = views(at)
        phi_kernel(
            group, q_ref.at[:, wide], k_ref.at[one], vm.at[one], fq_ref.at[heads], fk_ref.at[heads],
            phi_q_ref.at[heads], phi_k_ref.at[heads], st_out.at[heads],
        )
    kept = HEAD_SIZE + 16
    st_copies = [
        remote(st_out.at[:, pl.ds(0, kept)], st_in.at[at], st_send.at[at], st_recv.at[at], chip=to)
        for at, to in enumerate(at_chip)
    ]
    for copy in st_copies:
        copy.start()
    ff_start(2, 1)
    ff_start(1, 0)
    for at in range(kv_heads):
        heads, one, wide = views(at)
        intra_kernel(
            group, q_ref.at[:, wide], k_ref.at[one], v_ref.at[one], phi_q_ref.at[heads],
            phi_k_ref.at[heads], seg_q_ref, seg_k_ref, num.at[heads],
        )
    total = jnp.zeros(st_in.shape[1:], FLOAT)
    for at, copy in enumerate(st_copies):
        copy.wait_recv()
        total = total + coef_ref[at] * st_in[at].astype(FLOAT)
    state_ref[:, :kept] = total.astype(BFLOAT)
    state_ref[:, kept:] = jnp.zeros((state_ref.shape[0], 128 - kept, 128), BFLOAT)
    for at in range(kv_heads):
        heads, one, wide = views(at)
        finish_kernel(
            group, num.at[heads], phi_q_ref.at[heads], state_ref.at[heads], cont_ref,
            att_ref.at[:, wide], den_ref.at[one],
        )

    for side in range(2):
        for copy in o_second[side]:
            copy.wait_recv()

    def branch(which, target):
        rows = att_ref[pl.ds(pl.multiple_of(which * own, own), own)]
        return product_t(rows, wof_ref[...]), dot(rows, odown_ref[...])

    wide_part, low_part = branch(other, None)
    br_out[:, :model] = wide_part.astype(BFLOAT)
    br_out[:, model:] = low_part.astype(BFLOAT)
    br_copy = remote(br_out, br_in, br_sem.at[0], br_sem.at[1], **sibling)
    br_copy.start()
    wide_part, low_part = branch(core, None)
    br_copy.wait_recv()
    tz_out[:, :model] = (wide_part + br_in[:, :model].astype(FLOAT)).astype(BFLOAT)
    tz_out[:, model:] = (low_part + br_in[:, model:].astype(FLOAT)).astype(BFLOAT)
    tz_copy = remote(tz_out, tz_in, tz_sem.at[0], tz_sem.at[1], tensor=1 - tensor)
    tz_copy.start()
    ff_start(2, 0)
    c_forward[0].start()
    for copy in c_copies:
        copy.start()
    tz_copy.wait_recv()
    mid = (tz_out[:, model:].astype(FLOAT) + tz_in[:, model:].astype(FLOAT)).astype(BFLOAT)
    mid_ref[...] = mid
    residual = (
        hid_ref[...].astype(FLOAT)
        + (tz_out[:, :model].astype(FLOAT) + tz_in[:, :model].astype(FLOAT))
        + dot(mid, oup_ref[...])
    )
    res_ref[...] = residual
    xn[...] = normalized(residual, fgain_ref[...])
    x_local.start()
    x_forward[0].start()
    for copy in x_copies:
        copy.start()
    for step in range(1, chips):
        c_copies[step - 1].wait_recv()
        c_forward[step].start()
    for step in range(1, chips):
        x_copies[step - 1].wait_recv()
        x_forward[step].start()

    hid_done = [br_copy, tz_copy] + q_first + o_first + q_second[0] + q_second[1]
    for copy in hid_done + o_second[0] + o_second[1] + st_copies + c_copies + x_copies:
        copy.wait_send()

    @pl.when(chip < chips - 1)
    def _():
        rim_copy.wait_send()

    for copy in c_forward + x_forward:
        copy.wait()
    c_local.wait()
    x_local.wait()
    moved = (2 * pairs - 1) * shard
    for which in range(3):
        ff_local(which).wait()
        every = ff_ref.at[which, pl.ds(0, moved)]
        remote(every, every, ff_send.at[which], ff_recv.at[which], **sibling).wait()


def front(
    chips, kv_heads, group, tokens, near_args, far_args
):
    own, model = near_args[0].shape
    heads = kv_heads * group
    q_width = heads * HEAD_SIZE
    qkv_width = q_width + 2 * kv_heads * HEAD_SIZE
    extent = tokens + 128
    units = far_args[2].shape[1] // (chips * CORES)
    near = pl.BlockSpec(memory_space=pltpu.VMEM)
    far = pl.BlockSpec(memory_space=pl.ANY)
    kept = HEAD_SIZE + 16
    near_outs = [
        ((model, qkv_width), BFLOAT),
        ((model, q_width), BFLOAT),
        ((tokens, model), BFLOAT),
        ((tokens, 128), BFLOAT),
        ((own, 128), BFLOAT),
        ((own, model), FLOAT),
        ((tokens, q_width), BFLOAT),
        ((kv_heads, extent, HEAD_SIZE), BFLOAT),
        ((kv_heads, extent, 128), BFLOAT),
        ((heads, tokens, 128), BFLOAT),
        ((heads, extent, 128), BFLOAT),
        ((tokens, q_width), BFLOAT),
        ((kv_heads, tokens, 128), FLOAT),
        ((heads, 128, 128), BFLOAT),
    ]
    far_outs = [
        ((3, model, units), BFLOAT),
        ((chips, tokens, model), BFLOAT),
        ((chips, tokens, model), BFLOAT),
    ]
    pair = dma_row(2)
    return pl.pallas_call(
        functools.partial(front_kernel, chips, kv_heads, group),
        in_specs=[near] * len(near_args) + [far] * len(far_args),
        out_specs=[near] * len(near_outs) + [far] * len(far_outs),
        out_shape=[jax.ShapeDtypeStruct(*out) for out in near_outs + far_outs],
        scratch_shapes=[
            pltpu.VMEM((own, model), BFLOAT),
            pltpu.VMEM((kv_heads, extent, 128), BFLOAT),
            pltpu.VMEM((SOFTMAX_KEYS, 256), BFLOAT),
            pltpu.VMEM((SOFTMAX_KEYS, 256), BFLOAT),
            pltpu.VMEM((heads, 128, 128), BFLOAT),
            pltpu.VMEM((chips - 1, heads, kept, 128), BFLOAT),
            pltpu.VMEM((heads, tokens, 128), FLOAT),
            pltpu.VMEM((own, model + 128), BFLOAT),
            pltpu.VMEM((own, model + 128), BFLOAT),
            pltpu.VMEM((own, model + 128), BFLOAT),
            pltpu.VMEM((own, model + 128), BFLOAT),
            pltpu.VMEM((own, model), BFLOAT),
            pair,
            dma_row(3),
            dma_row(3),
            pltpu.SemaphoreType.DMA((2, chips - 1)),
            pltpu.SemaphoreType.DMA((2, chips - 1)),
            dma_row(3),
            dma_row(3),
            pltpu.SemaphoreType.DMA((2, chips - 1)),
            pltpu.SemaphoreType.DMA((2, chips - 1)),
            dma_row(3),
            dma_row(3),
            dma_row(7),
            dma_row(chips - 1),
            dma_row(chips - 1),
            dma_row(chips),
            dma_row(chips),
            dma_row(chips - 1),
            dma_row(chips - 1),
            dma_row(chips),
            dma_row(chips),
            pair,
            dma_row(chips - 1),
            dma_row(chips - 1),
            pair,
            pair,
        ],
        compiler_params=pltpu.CompilerParams(
            vmem_limit_bytes=60 * 1024 * 1024, collective_id=2, has_side_effects=True
        ),
        cost_estimate=pl.CostEstimate(
            flops=int(1e10), bytes_accessed=int(1e8), transcendentals=0
        ),
    )(*near_args, *far_args)


def rear_kernel(
    chips, kv_heads, group, rank,
    gnf_ref, res_ref, cot_ref, hid_ref, again_ref, fgain_ref, wof_ref, odown_ref, oup_ref, mid_ref,
    att_ref, den_ref, q_ref, k_ref, v_ref, phi_q_ref, phi_k_ref, fq_ref, fk_ref, state_ref,
    seg_q_ref, seg_k_ref, cont_ref, carry_ref, coef_ref, cos_ref, sin_ref,
    normed_ref, low_ref, qkv_ref, ups_ref, downs_ref,
    out_ref, ffg_ref,
    block_ref, igrad_ref, qkv_own, qkv_sib, o_own, o_sib,
    tab_own, early_own, ups_own, late_own, tab_sib, early_sib, ups_sib, late_sib,
    ffin_ref, oin_ref,
    db, dq, dn, ds_out, ds_in, gstate, dk, dv, dphi_q, dphi_k, gq, gk, dres,
    rim_out, rim_in, gp, br_out, br_in, tz_in,
    qg, q_in, q_dp_out, q_dp_in, q_core, og, o_in, o_dp_out, o_dp_in, o_core,
    tab_slots, early_slots, ups_slots, late_slots,
    tab_dp, early_dp, ups_dp, late_dp,
    db_sem, ds_send, ds_recv, rim_sem, br_sem, tz_sem, oz_sem, o_load, os_send, os_recv,
    q_send, q_recv, q_dp_sem, q_core_sem, o_send, o_recv, o_dp_sem, o_core_sem,
    small_send, small_recv, small_dp, small_core,
    ff_send, ff_recv, local_sems,
):
    dp, chip, core, tensor = (lax.axis_index(name) for name in ("dp", "chip", "core", "tensor"))
    own, model = gnf_ref.shape
    tokens = CORES * own
    q_width = q_ref.shape[1]
    pairs = CORES * chips
    shard = model // (2 * pairs)
    units = ffg_ref.shape[2]
    other = 1 - core
    there = 1 - dp
    sibling = {"core": other}
    at_chip = [lax.rem(chip + step, chips) for step in range(1, chips)]
    greet(
        [sibling, {"tensor": 1 - tensor}]
        + [{"dp": there, "core": core}, {"dp": there, "core": other}]
        + [{"chip": to, "core": which} for to in at_chip for which in (core, other)]
        + [{"dp": there, "chip": to, "core": which} for to in at_chip for which in (core, other)]
    )
    mine = pl.ds(pl.multiple_of(core * own, own), own)
    theirs = pl.ds(pl.multiple_of(other * own, own), own)

    def ff_start(which, side):
        def one(step, nothing):
            to = lax.rem(chip * CORES + core + step, pairs)
            group_to = dp if side == 0 else there
            remote(
                ffg_ref.at[which, pl.ds((group_to * pairs + to) * shard, shard)],
                ffin_ref.at[which, dp, :, pl.ds(pl.multiple_of((chip * CORES + core) * units, units), units)],
                ff_send.at[which, side],
                ff_recv.at[which, side],
                dp=group_to,
                chip=to // CORES,
                core=lax.rem(to, CORES),
            ).start()
            return nothing

        lax.fori_loop(1 - side, pairs, one, 0)

    def ff_local(which):
        at = chip * CORES + core
        return pltpu.make_async_copy(
            ffg_ref.at[which, pl.ds((dp * pairs + at) * shard, shard)],
            ffin_ref.at[which, dp, :, pl.ds(pl.multiple_of(at * units, units), units)],
            local_sems.at[which],
        )

    os_copies = [
        remote(out_ref.at[at + 1], oin_ref.at[at], os_send.at[at], os_recv.at[at], chip=to)
        for at, to in enumerate(at_chip)
    ]

    def norm_back_rows(inputs, gain, grad):
        scale = lax.rsqrt(jnp.mean(inputs * inputs, axis=1, keepdims=True) + EPS)
        weighted = grad * gain
        back = scale * weighted - inputs * (
            scale * scale * scale * jnp.mean(weighted * inputs, axis=1, keepdims=True)
        )
        return back, jnp.sum(grad * inputs * scale, axis=0, keepdims=True)

    slots = (tab_slots, early_slots, ups_slots, late_slots)
    dp_bufs = (tab_dp, early_dp, ups_dp, late_dp)
    owns = (tab_own, early_own, ups_own, late_own)
    sibs = (tab_sib, early_sib, ups_sib, late_sib)

    def small_copies(which):
        return [
            remote(
                slots[which].at[chip], slots[which].at[chip],
                small_send.at[which, at], small_recv.at[which, at], chip=to,
            )
            for at, to in enumerate(at_chip)
        ]

    def small_start(which, value):
        slots[which][chip] = value.astype(BFLOAT)
        for copy in small_copies(which):
            copy.start()

    def small_across(which):
        return remote(
            dp_bufs[which].at[0], dp_bufs[which].at[1],
            small_dp.at[which, 0], small_dp.at[which, 1], dp=there,
        )

    def small_over(which):
        return remote(owns[which], sibs[which], small_core.at[which, 0], small_core.at[which, 1], **sibling)

    def small_middle(which):
        for copy in small_copies(which):
            copy.wait()
        total = slots[which][0].astype(FLOAT)
        for at in range(1, chips):
            total = total + slots[which][at].astype(FLOAT)
        dp_bufs[which][0] = total.astype(BFLOAT)
        small_across(which).start()

    def small_end(which):
        small_across(which).wait()
        owns[which][...] = dp_bufs[which][0].astype(FLOAT) + dp_bufs[which][1].astype(FLOAT)
        small_over(which).start()

    def grad_copies(source, target, send, recv):
        return [
            remote(
                source.at[pl.ds(((dp if side == 0 else there) * chips + to) * CORES * shard, CORES * shard)],
                target.at[at, side],
                send.at[side, at],
                recv.at[side, at],
                chip=to,
            )
            for at, to in enumerate(at_chip)
            for side in range(2)
        ]

    q_copies = grad_copies(qg, q_in, q_send, q_recv)
    o_copies = grad_copies(og, o_in, o_send, o_recv)
    q_across = remote(q_dp_out, q_dp_in, q_dp_sem.at[0], q_dp_sem.at[1], dp=there)
    o_across = remote(o_dp_out, o_dp_in, o_dp_sem.at[0], o_dp_sem.at[1], dp=there)
    q_over = remote(q_core, qkv_sib, q_core_sem.at[0], q_core_sem.at[1], **sibling)
    o_over = remote(o_core, o_sib, o_core_sem.at[0], o_core_sem.at[1], **sibling)

    def chip_sum(source, target, side):
        group_at = dp if side == 0 else there
        total = source[pl.ds((group_at * chips + chip) * CORES * shard, CORES * shard)].astype(FLOAT)
        for at in range(chips - 1):
            total = total + target[at, side].astype(FLOAT)
        return total

    def grads_middle(copies, source, target, dp_out, across):
        for copy in copies:
            copy.wait_recv()
        dp_out[...] = chip_sum(source, target, 1).astype(BFLOAT)
        across.start()

    def grads_end(source, target, dp_in, across, result, core_out, over):
        across.wait()
        total = chip_sum(source, target, 0) + dp_in[...].astype(FLOAT)
        upper, lower = total[shard:], total[:shard]
        result[...] = jnp.where(core == 0, lower, upper)
        core_out[...] = jnp.where(core == 0, upper, lower).astype(BFLOAT)
        over.start()

    back_rows, gain_row = norm_back_rows(res_ref[...], fgain_ref[...], gnf_ref[...])
    grad_residual = cot_ref[...].astype(FLOAT) + back_rows
    dres[...] = grad_residual
    db[mine] = grad_residual.astype(BFLOAT)
    db_copy = remote(db.at[mine], db.at[mine], db_sem.at[0], db_sem.at[1], **sibling)
    db_copy.start()
    ff_start(0, 1)
    for copy in os_copies:
        copy.start()
    for which in range(3):
        ff_local(which).start()
    up_rows = t_product(mid_ref[...], db[mine])[:rank]
    filler = jnp.zeros((16 - 1 - rank, model), FLOAT)
    small_start(1, jnp.concatenate([up_rows, gain_row, filler], axis=0))
    db_copy.wait_recv()
    dmid = product_t(db[...], oup_ref[...]).astype(BFLOAT)
    dq[...] = dot(db[...], wof_ref[...]) + product_t(dmid, odown_ref[...])

    def views(at):
        return (
            pl.ds(at * group, group),
            pl.ds(at, 1),
            pl.ds(at * group * HEAD_SIZE, group * HEAD_SIZE),
        )

    for at in range(kv_heads):
        heads, one, wide = views(at)
        grad_numer_kernel(
            group, dq.at[:, wide], att_ref.at[:, wide], den_ref.at[one], phi_q_ref.at[heads], cont_ref,
            dn.at[heads], ds_out.at[heads],
        )
    kept = HEAD_SIZE + 16
    ds_copies = [
        remote(ds_out.at[:, pl.ds(0, kept)], ds_in.at[at], ds_send.at[at], ds_recv.at[at], chip=to)
        for at, to in enumerate([lax.rem(chip + chips - step, chips) for step in range(1, chips)])
    ]
    for copy in ds_copies:
        copy.start()
    ff_start(1, 1)
    og[...] = t_product(db[...], att_ref[...]).astype(BFLOAT)
    for copy in o_copies:
        copy.start()
    down_rows = t_product(dmid, att_ref[...])[:rank]
    for at in range(kv_heads):
        heads, one, wide = views(at)
        intra_back_kernel(
            group, q_ref.at[:, wide], k_ref.at[one], v_ref.at[one], phi_q_ref.at[heads],
            phi_k_ref.at[heads], dn.at[heads], seg_q_ref, seg_k_ref,
            dq.at[:, wide], dk.at[one], dv.at[one], dphi_q.at[heads], dphi_k.at[heads],
        )
    total = jnp.zeros(ds_in.shape[1:], FLOAT)
    for at, copy in enumerate(ds_copies):
        copy.wait_recv()
        total = total + coef_ref[at] * ds_in[at].astype(FLOAT)
    gstate[:, :kept] = total.astype(BFLOAT)
    gstate[:, kept:] = jnp.zeros((gstate.shape[0], 128 - kept, 128), BFLOAT)
    for at in range(kv_heads):
        heads, one, wide = views(at)
        features_back_kernel(
            group, q_ref.at[:, wide], k_ref.at[one], v_ref.at[one], phi_q_ref.at[heads],
            phi_k_ref.at[heads], dn.at[heads], fq_ref.at[heads], fk_ref.at[heads],
            state_ref.at[heads], gstate.at[heads], cont_ref, carry_ref,
            dq.at[:, wide], dk.at[one], dv.at[one], dphi_q.at[heads], dphi_k.at[heads],
            dq.at[:, wide], dk.at[one], dv.at[one], gq.at[heads], gk.at[heads],
        )

    gap = 128 - SOFTMAX_KEYS

    def joined(rows):
        return jnp.concatenate(
            [dk[head, rows] for head in range(kv_heads)]
            + [dv[head, rows, :HEAD_SIZE] for head in range(kv_heads)],
            axis=1,
        )

    rim_out[...] = joined(slice(gap, 128))
    rim_copy = remote(rim_out, rim_in, rim_sem.at[0], rim_sem.at[1], chip=lax.rem(chip + chips - 1, chips))

    @pl.when(chip > 0)
    def _():
        rim_copy.start()

    tables = []
    for head in range(kv_heads * group):
        pieces = [table[head, :, :FEATURE_HALF] - table[head, :, FEATURE_HALF:] for table in (gq, gk)]
        tables.append(jnp.concatenate(pieces, axis=1))
    small_start(0, jnp.concatenate(tables, axis=0))
    half = HEAD_SIZE // 2
    first_half = lax.rem(lanes((tokens, 128)), HEAD_SIZE) < half

    def unrotated(block):
        turned = jnp.where(first_half, pltpu.roll(block, 128 - half, 1), pltpu.roll(block, half, 1))
        return (block * cos_ref[...] - turned * sin_ref[...]).astype(BFLOAT)

    for at in range(0, q_width, 128):
        gp[:, at : at + 128] = unrotated(dq[:, at : at + 128])

    @pl.when(chip == chips - 1)
    def _():
        rim_in[...] = jnp.zeros(rim_in.shape, FLOAT)

    @pl.when(chip < chips - 1)
    def _():
        rim_copy.wait_recv()

    kv = joined(slice(128, 128 + tokens))
    kv = jnp.concatenate(
        [kv[: tokens - SOFTMAX_KEYS], kv[tokens - SOFTMAX_KEYS :] + rim_in[...]], axis=0
    )
    gp[:, q_width : q_width + 128] = unrotated(kv[:, :128])
    gp[:, q_width + 128 :] = kv[:, 128:].astype(BFLOAT)

    def partial(rows):
        grads = gp[rows]
        return product_t(grads, qkv_ref[...]), product_t(grads, ups_ref[...])

    wide_part, low_part = partial(theirs)
    br_out[:, :model] = wide_part.astype(BFLOAT)
    br_out[:, model:] = low_part.astype(BFLOAT)
    br_copy = remote(br_out, br_in, br_sem.at[0], br_sem.at[1], **sibling)
    br_copy.start()
    wide_part, low_part = partial(mine)
    br_copy.wait()
    tz_out = br_out
    tz_out[:, :model] = (wide_part + br_in[:, :model].astype(FLOAT)).astype(BFLOAT)
    tz_out[:, model:] = (low_part + br_in[:, model:].astype(FLOAT)).astype(BFLOAT)
    tz_copy = remote(tz_out, tz_in, tz_sem.at[0], tz_sem.at[1], tensor=1 - tensor)
    tz_copy.start()
    qg[...] = t_product(normed_ref[...], gp[...]).astype(BFLOAT)
    for copy in q_copies:
        copy.start()
    grads_middle(o_copies, og, o_in, o_dp_out, o_across)
    ff_start(2, 1)
    ff_start(0, 0)
    ff_start(1, 0)
    ff_start(2, 0)
    ups_rows = t_product(low_ref[...], gp[...])[: 3 * rank]
    wide_down = jnp.concatenate(
        [down_rows, jnp.zeros((rank, gp.shape[1] - q_width), FLOAT)], axis=1
    )
    small_start(2, jnp.concatenate([ups_rows, wide_down], axis=0))
    small_middle(1)
    small_middle(0)
    tz_copy.wait_recv()
    low = (tz_out[:, model:].astype(FLOAT) + tz_in[:, model:].astype(FLOAT)).astype(BFLOAT)
    grad_normed = (
        tz_out[:, :model].astype(FLOAT) + tz_in[:, :model].astype(FLOAT)
    ) + product_t(low, downs_ref[...])
    low_rows = t_product(low, normed_ref[mine])[: 3 * rank]
    back_rows, gain_row = norm_back_rows(hid_ref[...].astype(FLOAT), again_ref[...], grad_normed)
    igrad_ref[...] = (dres[...] + back_rows).astype(BFLOAT)
    filler = jnp.zeros((rank - 1, model), FLOAT)
    small_start(3, jnp.concatenate([low_rows, gain_row, filler], axis=0))
    small_end(1)
    small_end(0)
    small_middle(2)
    grads_end(og, o_in, o_dp_in, o_across, o_own, o_core, o_over)

    os_buf = tz_in.at[:, pl.ds(0, model)]
    load = pltpu.make_async_copy(out_ref.at[0], os_buf, o_load.at[0])
    load.start()
    load.wait()
    dres[...] = os_buf[...].astype(FLOAT)
    for at in range(chips - 1):
        os_copies[at].wait_recv()
        load = pltpu.make_async_copy(oin_ref.at[at], os_buf, o_load.at[0])
        load.start()
        load.wait()
        dres[...] += os_buf[...].astype(FLOAT)
    tz_copy.wait_send()
    oz_out, oz_in = (ref.at[:, pl.ds(0, model)] for ref in (br_out, br_in))
    oz_out[...] = dres[...].astype(BFLOAT)
    oz_copy = remote(oz_out, oz_in, oz_sem.at[0], oz_sem.at[1], tensor=1 - tensor)
    oz_copy.start()
    grads_middle(q_copies, qg, q_in, q_dp_out, q_across)
    small_end(2)
    small_middle(3)
    oz_copy.wait()
    block_ref[...] = (
        res_ref[...] + (oz_out[...].astype(FLOAT) + oz_in[...].astype(FLOAT))
    ).astype(BFLOAT)
    grads_end(qg, q_in, q_dp_in, q_across, qkv_own, q_core, q_over)
    small_end(3)

    for copy in [db_copy] + ds_copies + os_copies + q_copies + o_copies:
        copy.wait_send()

    @pl.when(chip > 0)
    def _():
        rim_copy.wait_send()

    for which in range(4):
        small_over(which).wait()
    q_over.wait()
    o_over.wait()
    for which in range(3):
        ff_local(which).wait()
        for side in range(2):
            count = pairs - 1 + side
            group_from = dp if side == 0 else there
            sent = ffg_ref.at[which, pl.ds(0, count * shard)]
            came = ffin_ref.at[which, group_from, :, pl.ds(0, count * units)]
            remote(sent, sent, ff_send.at[which, side], ff_recv.at[which, side], **sibling).wait_send()
            remote(came, came, ff_send.at[which, side], ff_recv.at[which, side], **sibling).wait_recv()


def rear(chips, kv_heads, group, rank, near_args, far_args):
    own, model = near_args[0].shape
    tokens = CORES * own
    heads = kv_heads * group
    q_width = heads * HEAD_SIZE
    qkv_width = q_width + 2 * kv_heads * HEAD_SIZE
    extent = tokens + 128
    pairs = chips * CORES
    shard = model // (2 * pairs)
    units = far_args[1].shape[2]
    near = pl.BlockSpec(memory_space=pltpu.VMEM)
    far = pl.BlockSpec(memory_space=pl.ANY)
    kept = HEAD_SIZE + 16
    smalls = [
        (heads * HEAD_SIZE, 128),
        (16, model),
        (4 * rank, qkv_width),
        (4 * rank, model),
    ]
    near_outs = [
        ((own, model), BFLOAT),
        ((own, model), BFLOAT),
        ((shard, qkv_width), FLOAT),
        ((shard, qkv_width), BFLOAT),
        ((shard, q_width), FLOAT),
        ((shard, q_width), BFLOAT),
    ]
    near_outs += [(shape, FLOAT) for shape in smalls] * 2
    far_outs = [
        ((3, 2, shard, pairs * units), BFLOAT),
        ((chips - 1, own, model), BFLOAT),
    ]
    pair = dma_row(2)
    step_pair = pltpu.SemaphoreType.DMA((2, chips - 1))

    def grads(width):
        return [
            pltpu.VMEM((model, width), BFLOAT),
            pltpu.VMEM((chips - 1, 2, CORES * shard, width), BFLOAT),
            pltpu.VMEM((CORES * shard, width), BFLOAT),
            pltpu.VMEM((CORES * shard, width), BFLOAT),
            pltpu.VMEM((shard, width), BFLOAT),
        ]

    wide = pltpu.VMEM((own, model + 128), BFLOAT)
    return pl.pallas_call(
        functools.partial(rear_kernel, chips, kv_heads, group, rank),
        in_specs=[near] * len(near_args) + [far] * len(far_args),
        out_specs=[near] * len(near_outs) + [far] * len(far_outs),
        out_shape=[jax.ShapeDtypeStruct(*out) for out in near_outs + far_outs],
        scratch_shapes=[
            pltpu.VMEM((tokens, model), BFLOAT),
            pltpu.VMEM((tokens, q_width), FLOAT),
            pltpu.VMEM((heads, tokens, 128), BFLOAT),
            pltpu.VMEM((heads, 128, 128), BFLOAT),
            pltpu.VMEM((chips - 1, heads, kept, 128), BFLOAT),
            pltpu.VMEM((heads, 128, 128), BFLOAT),
            pltpu.VMEM((kv_heads, extent, HEAD_SIZE), FLOAT),
            pltpu.VMEM((kv_heads, extent, 128), FLOAT),
            pltpu.VMEM((heads, tokens, 128), FLOAT),
            pltpu.VMEM((heads, extent, 128), FLOAT),
            pltpu.VMEM((heads, HEAD_SIZE, 128), FLOAT),
            pltpu.VMEM((heads, HEAD_SIZE, 128), FLOAT),
            pltpu.VMEM((own, model), FLOAT),
            pltpu.VMEM((SOFTMAX_KEYS, 256), FLOAT),
            pltpu.VMEM((SOFTMAX_KEYS, 256), FLOAT),
            pltpu.VMEM((tokens, qkv_width), BFLOAT),
            wide,
            wide,
            wide,
        ]
        + grads(qkv_width)
        + grads(q_width)
        + [pltpu.VMEM((chips,) + shape, BFLOAT) for shape in smalls]
        + [pltpu.VMEM((2,) + shape, BFLOAT) for shape in smalls]
        + [
            pair,
            dma_row(chips - 1),
            dma_row(chips - 1),
            pair,
            pair,
            pair,
            pair,
            dma_row(1),
            dma_row(chips - 1),
            dma_row(chips - 1),
            step_pair,
            step_pair,
            pair,
            pair,
            step_pair,
            step_pair,
            pair,
            pair,
            pltpu.SemaphoreType.DMA((4, chips - 1)),
            pltpu.SemaphoreType.DMA((4, chips - 1)),
            pltpu.SemaphoreType.DMA((4, 2)),
            pltpu.SemaphoreType.DMA((4, 2)),
            pltpu.SemaphoreType.DMA((3, 2)),
            pltpu.SemaphoreType.DMA((3, 2)),
            dma_row(3),
        ],
        compiler_params=pltpu.CompilerParams(
            vmem_limit_bytes=63 * 1024 * 1024, collective_id=3, has_side_effects=True
        ),
        cost_estimate=pl.CostEstimate(
            flops=int(4e10), bytes_accessed=int(1e8), transcendentals=0
        ),
    )(*near_args, *far_args)


def carry_coefs(lengths, tokens):
    count = lax.axis_size("chip")
    me = lax.axis_index("chip")
    starts = jnp.arange(count, dtype=jnp.int32) * tokens
    open_chip = locate(starts - 1, lengths)[0] == locate(starts + tokens - 1, lengths)[0]
    source = jnp.arange(count)[:, None]
    between = jnp.arange(count)[None, :]
    after = (between > source) & (between < me)
    before = (between < source) & (between > me)
    forward = jnp.all(open_chip[None, :] | ~after, axis=1) & (source[:, 0] < me)
    backward = jnp.all(open_chip[None, :] | ~before, axis=1) & (source[:, 0] > me)
    return forward.astype(FLOAT), backward.astype(FLOAT)


def on_device(
    hidden_in,
    doc_lengths,
    attention_gain,
    query_weight,
    key_projection,
    value_projection,
    output_weight,
    query_down,
    query_up,
    key_down,
    key_adapter_up,
    value_down,
    value_adapter_up,
    output_down,
    output_up,
    query_feature_maps,
    key_feature_maps,
    feedforward_gain,
    gate_weight,
    up_weight,
    down_weight,
    block_cotangent,
):
    own_rows, model = hidden_in.shape
    tokens = own_rows * CORES
    core = lax.axis_index("core")
    chip = lax.axis_index("chip")
    chips = lax.axis_size("chip")
    heads = query_feature_maps.shape[0] // CORES
    kv_heads = key_projection.shape[1] // HEAD_SIZE // CORES
    group = heads // kv_heads
    q_width = heads * HEAD_SIZE
    kv_width = kv_heads * HEAD_SIZE
    rank = query_down.shape[1]

    def own_cols(value, width, which):
        return lax.dynamic_slice_in_dim(value, which * width, width, 1)

    def own_heads(value, count, which):
        return lax.dynamic_slice_in_dim(value, which * count, count, 0)

    wqkv = jnp.stack(
        [
            jnp.concatenate(
                [
                    own_cols(query_weight, q_width, which),
                    own_cols(key_projection, kv_width, which),
                    own_cols(value_projection, kv_width, which),
                ],
                axis=1,
            )
            for which in range(CORES)
        ]
    )
    wout = output_weight.reshape(CORES, q_width, -1).transpose(0, 2, 1)
    qkv_width = q_width + 2 * kv_width

    first_row = chip * tokens
    lengths = doc_lengths[0]
    seg_rows, pos_rows = locate(first_row + jnp.arange(tokens, dtype=jnp.int32), lengths)
    seg_rim = locate(first_row - SOFTMAX_KEYS + jnp.arange(SOFTMAX_KEYS, dtype=jnp.int32), lengths)[
        0
    ]
    seg_first = locate(jnp.reshape(first_row - 1, (1,)), lengths)[0][0]
    gap = 128 - SOFTMAX_KEYS
    seg_ext = jnp.concatenate([jnp.full((gap,), -2, jnp.int32), seg_rim, seg_rows])
    seg_last = seg_rows[tokens - 1]
    continuing = (seg_rows == seg_first).astype(FLOAT)[:, None]
    carry = ((jnp.arange(tokens + 128) < tokens + gap) & (seg_ext == seg_last)).astype(FLOAT)[:, None]
    seg_column, seg_line = seg_rows[:, None], seg_ext[None, :]
    forward_coefs, backward_coefs = carry_coefs(lengths, tokens)
    cosine_table, sine_table = rotation(pos_rows, HEAD_SIZE)
    query_table = own_heads(query_feature_maps, heads, core)
    key_table = own_heads(key_feature_maps, heads, core)
    query_table = jnp.concatenate([query_table, -query_table], axis=2)
    key_table = jnp.concatenate([key_table, -key_table], axis=2)
    downs = jnp.concatenate([query_down, key_down, value_down], axis=1)
    own_query_up = own_cols(query_up, q_width, core)
    own_key_up = own_cols(key_adapter_up, kv_width, core)
    own_value_up = own_cols(value_adapter_up, kv_width, core)
    own_output_down = own_heads(output_down, q_width, core)
    pad = 128 - 3 * rank
    ups = jnp.concatenate(
        [
            jnp.pad(own_query_up, ((0, 0), (0, 2 * kv_width))),
            jnp.pad(own_key_up, ((0, 0), (q_width, kv_width))),
            jnp.pad(own_value_up, ((0, 0), (q_width + kv_width, 0))),
            jnp.zeros((pad, qkv_width), BFLOAT),
        ],
        axis=0,
    )
    extent = tokens + 128
    behind = [lax.rem(chip + chips - step, chips) for step in range(1, chips)]
    ahead = [lax.rem(chip + step, chips) for step in range(1, chips)]

    def coef_rows(coefs, places):
        rows = jnp.stack([coefs[at] for at in places])
        return jnp.broadcast_to(rows[:, None, None], (chips - 1, 1, 128))

    wide_cosine, wide_sine = spread(cosine_table, 128), spread(sine_table, 128)
    wide_downs = jnp.pad(downs, ((0, 0), (0, pad)))
    wide_output_down = jnp.pad(own_output_down, ((0, 0), (0, 128 - rank)))
    wide_output_up = jnp.pad(output_up, ((0, 128 - rank), (0, 0)))
    (
        full_qkv, full_out, normed, low_rank, low_mid, residual, queries, key_ext, value_ext,
        phi_q, phi_k, attended, denominator, state, full_ff, cotangents, gathered,
    ) = front(
        chips,
        kv_heads,
        group,
        tokens,
        [
            hidden_in,
            attention_gain[None],
            feedforward_gain[None],
            wide_downs,
            ups,
            wide_cosine,
            wide_sine,
            query_table,
            key_table,
            seg_column,
            seg_line,
            continuing,
            carry,
            coef_rows(forward_coefs, behind),
            wide_output_down,
            wide_output_up,
        ],
        [wqkv, wout, gate_weight, up_weight, down_weight.T, block_cotangent],
    )
    grad_normed_ff, out_sums, ff_grads, _ = feed(gathered, cotangents, full_ff)
    rear_outs = rear(
        chips,
        kv_heads,
        group,
        rank,
        [
            grad_normed_ff,
            residual,
            block_cotangent,
            hidden_in,
            attention_gain[None],
            feedforward_gain[None],
            full_out,
            wide_output_down[:, :16],
            wide_output_up[:16],
            low_mid,
            attended,
            denominator,
            queries,
            key_ext,
            value_ext,
            phi_q,
            phi_k,
            query_table,
            key_table,
            state,
            seg_column,
            seg_line,
            continuing,
            carry,
            coef_rows(backward_coefs, ahead),
            wide_cosine,
            wide_sine,
            normed,
            low_rank,
            full_qkv,
            ups,
            wide_downs,
        ],
        [out_sums, ff_grads],
    )
    block_output, input_grad, qkv_keep, qkv_other, out_keep, out_other = rear_outs[:6]
    own_small, sib_small = rear_outs[6:10], rear_outs[10:14]
    qkv_other, out_other = qkv_other.astype(FLOAT), out_other.astype(FLOAT)

    def by_core(dim, mine, other):
        return ordered(core, mine, other, dim)

    at_key, at_value = q_width, q_width + kv_width
    query_shard = by_core(1, qkv_keep[:, :at_key], qkv_other[:, :at_key])
    key_shard = by_core(1, qkv_keep[:, at_key:at_value], qkv_other[:, at_key:at_value])
    value_shard = by_core(1, qkv_keep[:, at_value:], qkv_other[:, at_value:])
    output_shard = by_core(1, out_keep, out_other).T
    ff_shards = rear_outs[14].astype(FLOAT)
    ff_shards = ff_shards[:, 0] + ff_shards[:, 1]

    tables = by_core(0, own_small[0], sib_small[0]).reshape(CORES * heads, HEAD_SIZE, 128)
    early = own_small[1] + sib_small[1]
    late = own_small[3] + sib_small[3]
    ups_mine, ups_other = own_small[2], sib_small[2]

    def ups_part(row, start, stop):
        rows = slice(row * rank, (row + 1) * rank)
        return by_core(1, ups_mine[rows, start:stop], ups_other[rows, start:stop])

    downs_total = late[: 3 * rank].T
    return (
        block_output,
        input_grad,
        late[3 * rank],
        query_shard,
        key_shard,
        value_shard,
        output_shard,
        downs_total[:, :rank],
        ups_part(0, 0, at_key),
        downs_total[:, rank : 2 * rank],
        ups_part(1, at_key, at_value),
        downs_total[:, 2 * rank :],
        ups_part(2, at_value, qkv_width),
        ups_part(3, 0, at_key).T,
        early[:rank],
        tables[:, :, :FEATURE_HALF],
        tables[:, :, FEATURE_HALF:],
        early[rank],
        ff_shards[0],
        ff_shards[1],
        ff_shards[2].T,
    )


def solution(mesh):
    dp, seq, tensor = (mesh.shape[name] for name in ("dp", "seq", "tensor"))
    split = Mesh(
        mesh.devices.reshape(dp, seq // CORES, CORES, tensor), ("dp", "chip", "core", "tensor")
    )
    tok = ("dp", "chip", "core")
    in_specs = (
        P(tok, None),
        P("dp", None),
        P(),
        P(tok, "tensor"),
        P(tok, "tensor"),
        P(tok, "tensor"),
        P("tensor", tok),
        P(),
        P(None, "tensor"),
        P(),
        P(None, "tensor"),
        P(),
        P(None, "tensor"),
        P("tensor", None),
        P(),
        P("tensor", None, None),
        P("tensor", None, None),
        P(),
        P(tok, "tensor"),
        P(tok, "tensor"),
        P("tensor", tok),
        P(tok, None),
    )
    out_specs = (
        P(tok, None),
        P(tok, None),
        P(),
        P(tok, "tensor"),
        P(tok, "tensor"),
        P(tok, "tensor"),
        P("tensor", tok),
        P(),
        P(None, "tensor"),
        P(),
        P(None, "tensor"),
        P(),
        P(None, "tensor"),
        P("tensor", None),
        P(),
        P("tensor", None, None),
        P("tensor", None, None),
        P(),
        P(tok, "tensor"),
        P(tok, "tensor"),
        P("tensor", tok),
    )
    return jax.shard_map(
        on_device, mesh=split, in_specs=in_specs, out_specs=out_specs, check_vma=False
    )
```

time: 882 us -> 729 us (0.83)
  Pallas kernels: 86.9 us -> 666 us
  waiting for transfers between devices: 333 us -> 0 us
  starting transfers between devices: 114 us -> 0 us
  other arithmetic: 124 us -> 23.9 us
  local copies, waits for them, and re-layouts: 123 us -> 28.3 us
  matrix products: 81.5 us -> 0 us
    pallas_call x10 -> x3, Pallas kernels: 86.9 us -> 666 us  [the longest x1 304 us: rear(): pl.pallas_call(functools.partial(rear_kernel, chips, kv_heads, group, ran...]
    ppermute x79 -> x0, waiting for transfers between devices: 327 us -> none  [the longest x77 321 us: swap(): lax.ppermute(value, axis, [(source, source ^ mask) for source in range(co...]
    dot_general x29 -> x0, matrix products: 81.5 us -> none  [the longest x19 57.4 us: t_product(): lax.dot_general(left, right, (((0,), (0,)), ((), ())), preferred_element_...]
    ppermute x79 -> x0, starting transfers between devices: 74.1 us -> none  [the longest x77 68.4 us: swap(): lax.ppermute(value, axis, [(source, source ^ mask) for source in range(co...]
    all_to_all x6 -> x0, starting transfers between devices: 40 us -> none  [the longest x3 21.2 us: ff_weight(): lax.all_to_all(both, ff_axes, split_dim + 1, 2 - split_dim, tiled=True)]
    select_n x4 -> x0, local copies, waits for them, and re-layouts: 32.7 us -> none  [ordered(): jnp.where(which == 0, jnp.concatenate([mine, other], axis=dim), jnp.conca...]
    concatenate x24 -> x2, other arithmetic: 25.9 us -> 0.76 us  [the longest x1 0.76 us: on_device(): jnp.concatenate([jnp.pad(own_query_up, ((0, 0), (0, 2 * kv_width))), jnp....]
    select_n x22 -> x7, other arithmetic: 26.9 us -> 4.04 us  [ordered(): jnp.where(which == 0, jnp.concatenate([mine, other], axis=dim), jnp.conca...]
  transfers between devices with their start and end apart: 85 -> 0, of which waited for: 32 -> 0; matrix products, arithmetic and copies ran while one was open for 34% -> 0% of each run, Pallas kernels for 10% -> 0%
where the time goes in v2:
time: 729 us; the launch traced here: 721 us
  Pallas kernels  666 us (91%)
  local copies, waits for them, and re-layouts  28.3 us (4%)
  other arithmetic  23.9 us (3%)
    pallas_call x1, Pallas kernels, rear(): pl.pallas_call(functools.partial(rear_kernel, chips, kv_heads, group, ran...  304 us
    pallas_call x1, Pallas kernels, front(): pl.pallas_call(functools.partial(front_kernel, chips, kv_heads, group), i...  251 us
    pallas_call x1, Pallas kernels, feed(): pl.pallas_call(functools.partial(feed_kernel, chips), in_specs=[far, far,...  112 us

profile of v2, /device:TPU:15, one launch (start us, length us, event | category | flops | bytes accessed | tf_op | source)
XLA Modules:
  0.0 720.6 jit_solution(10074204650990565243)
XLA Ops:
  0.7 0.9 reduce-window.4
  2.5 2.0 pad_maximum_fusion.6
  5.2 0.7 fusion.15
  6.7 0.7 fusion.17
  7.7 0.8 fusion.7.carry_ref
  8.4 1.0 fusion.13
  9.5 0.8 copy.101.sin_ref
  11.7 0.8 fusion.10.ups_ref
  13.9 0.8 compare_convert_fusion
  14.8 0.8 copy.100.cos_ref
  15.7 0.8 pad_maximum_fusion.3.fq_ref
  16.5 0.8 pad_maximum_fusion.4.fk_ref
  18.2 0.8 pad_maximum_fusion.wqkv_ref
  19.3 0.9 pad.24.downs_ref
  20.2 1.3 copy.99
  21.5 0.8 pad.29.oup_ref
  22.3 0.9 copy.98
  23.2 250.6 %shard_map.382 = (bf16[2048,768]{1,0:T(8,128)(2,1)}, bf16[2048,512]{1,0:T(8,128)(2,1)}, bf16[512,2048]{1,0:T(8,128)(2,1)}, bf16[512,128]{1,0:T(8,128)(2,1)}, bf1...) custom-call(bf16[256,2048]{1,0:T(8,128)(2,1)} %hid_ref.3, ...), custom_call_target="tpu_custom_call" | custom-call | flops 10000000000 | bytes 100000000 | tf_op jit(solution)/shard_map/pallas_call | solution.py:821
  273.8 112.1 %shard_map.383 = (f32[256,2048]{1,0:T(8,128)}, bf16[4,256,2048]{2,1,0:T(8,128)(2,1)}, bf16[3,2048,512]{2,1,0:T(8,128)(2,1)}, bf16[3,256,2048]{2,1,0:T(8,128)(2,1)}) custom-call(bf16[4,512,2048]{2,1,0:T(8,128)(2,1)} %get-tuple-element.56.x_ref, bf16[4,512,2048]{2,1,0:T(8,128)(2,1)} %get-tuple-element.57.c_ref, bf16[3,2048,512]{2,1,0:T(8,128)(2,1)} %get-tuple-element.58.ff_ref), custom_call_target="tpu_custom_call" | custom-call | flops 38654705664 | bytes 33554432 | tf_op jit(solution)/shard_map/pallas_call | solution.py:436
  386.5 2.0 pad_maximum_fusion.7
  390.5 303.8 %shard_map.384 = (bf16[256,2048]{1,0:T(8,128)(2,1)}, bf16[256,2048]{1,0:T(8,128)(2,1)}, f32[128,768]{1,0:T(8,128)}, bf16[128,768]{1,0:T(8,128)(2,1)}, f32[128,51...) custom-call(f32[256,2048]{1,0:T(8,128)} %get-tuple-element.59.gnf_re, ...), custom_call_target="tpu_custom_call" | custom-call | flops 40000000000 | bytes 100000000 | tf_op jit(solution)/shard_map/pallas_call | solution.py:1286
  694.2 4.5 convert_element_type.90
  698.8 1.3 slice_add_fusion
  700.1 2.9 slice_bitcast_fusion
  703.0 3.0 copy.105
  706.0 1.1 fusion.36
  708.4 0.7 fusion.41
  709.2 0.7 fusion.42
  713.8 1.0 copy.104
  716.3 0.8 maximum_select_fusion
  718.5 1.0 copy.109
  719.4 1.0 copy.110
  (119 shorter events, 16.5 us)
Async XLA Ops:
  0.7 10.2 %copy-start = (bf16[8,1024]{1,0:T(8,128)(2,1)S(1)}, bf16[8,1024]{1,0:T(8,128)(2,1)}, u32[]{:S(2)}) copy-start(bf16[8,1024]{1,0:T(8,128)(2,1)} %param.31) | copy-start | bytes 49156
  0.7 15.0 %copy-start.21 = (bf16[16,64,64]{2,1,0:T(8,128)(2,1)S(1)}, bf16[16,64,64]{2,1,0:T(8,128)(2,1)}, u32[]{:S(2)}) copy-start(bf16[16,64,64]{2,1,0:T(8,128)(2,1)} %param.38) | copy-start | bytes 393220
  0.7 14.9 %copy-start.20 = (bf16[16,64,64]{2,1,0:T(8,128)(2,1)S(1)}, bf16[16,64,64]{2,1,0:T(8,128)(2,1)}, u32[]{:S(2)}) copy-start(bf16[16,64,64]{2,1,0:T(8,128)(2,1)} %param.39) | copy-start | bytes 393220
  0.7 16.5 %copy-start.25 = (bf16[1024,8]{0,1:T(8,128)(2,1)S(1)}, bf16[1024,8]{0,1:T(8,128)(2,1)}, u32[]{:S(2)}) copy-start(bf16[1024,8]{0,1:T(8,128)(2,1)} %param.36) | copy-start | bytes 49156
  7.6 10.4 %copy-start.9 = (bf16[128,1024]{1,0:T(8,128)(2,1)S(1)}, bf16[128,1024]{1,0:T(8,128)(2,1)}, u32[]{:S(2)}) copy-start(bf16[128,1024]{1,0:T(8,128)(2,1)} %param.26) | copy-start | bytes 786436
  8.4 9.7 %copy-start.18 = (bf16[128,256]{1,0:T(8,128)(2,1)S(1)}, bf16[128,256]{1,0:T(8,128)(2,1)}, u32[]{:S(2)}) copy-start(bf16[128,256]{1,0:T(8,128)(2,1)} %param.27) | copy-start | bytes 196612
  9.4 8.7 %copy-start.19 = (bf16[128,256]{1,0:T(8,128)(2,1)S(1)}, bf16[128,256]{1,0:T(8,128)(2,1)}, u32[]{:S(2)}) copy-start(bf16[128,256]{1,0:T(8,128)(2,1)} %param.28) | copy-start | bytes 196612
  13.9 5.1 copy-start.22
  13.9 5.1 copy-start.23
  13.9 5.1 copy-start.24
  15.6 4.6 copy-start.2
  18.1 3.4 copy-start.17
  18.1 4.2 copy-start.10
  703.0 3.0 copy-start.12
  703.0 3.0 copy-start.13
  703.0 4.2 copy-start.15
  703.0 4.2 copy-start.16
  703.0 10.7 %copy-start.14 = (bf16[128,512]{1,0:T(8,128)(2,1)S(1)}, bf16[128,512]{1,0:T(8,128)(2,1)}, u32[]{:S(2)}) copy-start(bf16[128,512]{1,0:T(8,128)(2,1)} %get-tuple-element.83) | copy-start | bytes 393220
  706.0 7.8 %copy-start.11 = (f32[128,512]{1,0:T(8,128)S(1)}, f32[128,512]{1,0:T(8,128)}, u32[]{:S(2)}) copy-start(f32[128,512]{1,0:T(8,128)} %get-tuple-element.82) | copy-start | bytes 786436
  706.0 8.9 %copy-start.6 = (f32[128,768]{1,0:T(8,128)S(1)}, f32[128,768]{1,0:T(8,128)}, u32[]{:S(2)}) copy-start(f32[128,768]{1,0:T(8,128)} %get-tuple-element.80) | copy-start | bytes 1179652
  706.0 8.9 %copy-start.5 = (bf16[128,768]{1,0:T(8,128)(2,1)S(1)}, bf16[128,768]{1,0:T(8,128)(2,1)}, u32[]{:S(2)}) copy-start(bf16[128,768]{1,0:T(8,128)(2,1)} %get-tuple-element.81) | copy-start | bytes 589828
  707.2 9.9 %copy-start.7 = (f32[32,2048]{1,0:T(8,128)S(1)}, f32[32,2048]{1,0:T(8,128)}, u32[]{:S(2)}) copy-start(f32[32,2048]{1,0:T(8,128)} %get-tuple-element.78) | copy-start | bytes 786436
  707.2 9.9 %copy-start.8 = (f32[32,2048]{1,0:T(8,128)S(1)}, f32[32,2048]{1,0:T(8,128)}, u32[]{:S(2)}) copy-start(f32[32,2048]{1,0:T(8,128)} %get-tuple-element.79) | copy-start | bytes 786436
  713.8 4.7 copy-start.4
  714.9 4.6 copy-start.3
  716.3 4.1 copy-start.1

commit v3 on v2

--- a/solution.py
+++ b/solution.py
@@ -37,25 +37,19 @@
 
 
 def rotation(positions, head_width):
-    freq_table = jnp.asarray(frequencies(head_width), FLOAT)
-    turned = positions.astype(FLOAT)[:, None] * freq_table[None, :]
-    cosine, sine = jnp.cos(turned), jnp.sin(turned)
-    return (
-        jnp.concatenate([cosine, cosine], axis=-1),
-        jnp.concatenate([-sine, sine], axis=-1),
-    )
-
-
-def spread(table, width):
-    return jnp.tile(table, (1, width // table.shape[1]))
+    table = np.tile(frequencies(head_width), 4)[None].astype(np.float32)
+    sign = np.tile(np.repeat([-1.0, 1.0], head_width // 2), 2)[None].astype(np.float32)
+    turned = positions.astype(FLOAT)[:, None] * table
+    return jnp.cos(turned), jnp.sin(turned) * sign
 
 
 def locate(places, lengths):
-    doc_ends = jnp.cumsum(lengths)
-    passed = places[:, None] >= doc_ends[None, :]
-    segment = jnp.sum(passed.astype(jnp.int32), axis=1)
-    doc_begin = jnp.sum(jnp.where(passed, lengths[None, :], 0), axis=1)
-    return (jnp.where(places < 0, -1, segment), places - doc_begin)
+    segment, begin, end = jnp.zeros_like(places), jnp.zeros_like(places), 0
+    for at in range(lengths.shape[0]):
+        end = end + lengths[at]
+        segment = segment + (places >= end).astype(jnp.int32)
+        begin = jnp.where(places >= end, end, begin)
+    return (jnp.where(places < 0, -1, segment), places - begin)
 
 
 def product(left, right):
@@ -260,11 +254,78 @@
     pl.semaphore_wait(barrier, len(peers))
 
 
+def even_chip(chip):
+    return 1 - lax.rem(chip, 2)
+
+
+def slot_of(chips, chip, step):
+    if chips != 4:
+        return step
+    even = even_chip(chip)
+    return lax.rem(even * step + (1 - even) * (chips - step), chips)
+
+
+def row_copies(chips, chip, source, target, send, recv):
+    own = source.shape[0]
+
+    def one(piece, step, rows, at, to):
+        return remote(piece, target.at[step, rows], send.at[at], recv.at[at], chip=to)
+
+    every = pl.ds(0, own)
+    if chips != 4:
+        to = [lax.rem(chip + chips - step, chips) for step in range(1, chips)]
+        return [one(source, step + 1, every, step, at) for step, at in enumerate(to)], []
+    even = even_chip(chip)
+    beside = 3 - 2 * even
+    across = chip - 1 + 2 * even
+    along = chip + 2 - 4 * (chip // 2)
+    upper, lower = pl.ds(0, own // 2), pl.ds(own // 2, own // 2)
+    return [
+        one(source, chips - beside, every, 0, across),
+        one(source, 2, every, 1, along),
+    ], [
+        one(target.at[beside, upper], chips - beside, upper, 2, along),
+        one(target.at[2, lower], beside, lower, 3, across),
+    ]
+
+
+def relay(copies):
+    for at, copy in enumerate(copies[1]):
+        copies[0][at].wait_recv()
+        copy.start()
+
+
+def forward_copies(chips, chip, core, source, target, send, recv):
+    own = source.shape[0]
+    copies = []
+    for at in range(chips):
+        slot = slot_of(chips, chip, at) if at > 0 else 0
+        piece = target.at[slot, pl.ds(0, own)] if at > 0 else source
+        copies.append(
+            remote(piece, target.at[slot, pl.ds(own, own)], send.at[at], recv.at[at], core=1 - core)
+        )
+    return copies
+
+
+def hand_over(copies, forwards):
+    if copies[1]:
+        forwards[1].start()
+        forwards[2].start()
+        for copy in copies[1]:
+            copy.wait_recv()
+        forwards[3].start()
+    else:
+        for copy, forward in zip(copies[0], forwards[1:]):
+            copy.wait_recv()
+            forward.start()
+
+
 def feed_kernel(
     chips, x_ref, c_ref, ff_ref,
-    grad_ref, out_ref, ffg_ref, got_ref,
+    grad_ref, out_ref, ffg_ref, got_ref, xall_ref,
     x_buf, c_buf, gg_ref, gu_ref, gd_ref, keep, sib_out, sib_in, part, stage, wide,
     load_sems, stage_sems, sib_send, sib_recv, part_send, part_recv, cross_sems, ffg_sems, free_sem,
+    x_send, x_recv, xf_send, xf_recv, x_sem,
 ):
     core, chip, tensor = (lax.axis_index(name) for name in ("core", "chip", "tensor"))
     rows = keep.shape[2]
@@ -278,14 +339,43 @@
     )
 
     def place(step):
-        return lax.rem(step + 1, chips)
-
-    def loads(step):
+        return slot_of(chips, chip, step)
+
+    def load(step, which):
         slot = lax.rem(step, 2)
-        return [
-            pltpu.make_async_copy(ref.at[place(step)], buf.at[slot], load_sems.at[at, slot])
-            for at, (ref, buf) in enumerate(((x_ref, x_buf), (c_ref, c_buf)))
-        ]
+        ref, buf = ((xall_ref, x_buf), (c_ref, c_buf))[which]
+        return pltpu.make_async_copy(ref.at[place(step)], buf.at[slot], load_sems.at[which, slot])
+
+    x_copies = row_copies(chips, chip, x_ref, xall_ref, x_send, x_recv)
+    x_forward = forward_copies(chips, chip, core, x_ref, xall_ref, xf_send, xf_recv)
+    x_local = pltpu.make_async_copy(x_ref, xall_ref.at[0, pl.ds(0, rows)], x_sem)
+
+    def came(step):
+        half = xall_ref.at[place(step), pl.ds(rows, rows)]
+        remote(half, half, xf_send.at[step], xf_recv.at[step], **sibling).wait_recv()
+
+    def advance(step):
+        if chips == 4:
+
+            @pl.when(step == 0)
+            def _():
+                relay(x_copies)
+                x_forward[1].start()
+                x_forward[2].start()
+
+            @pl.when(step == 2)
+            def _():
+                for copy in x_copies[1]:
+                    copy.wait_recv()
+                x_forward[3].start()
+
+        else:
+            for at, copy in enumerate(x_copies[0]):
+
+                @pl.when(step == at)
+                def _(at=at, copy=copy):
+                    copy.wait_recv()
+                    x_forward[at + 1].start()
 
     def to_sibling(step):
         slot = lax.rem(step, 2)
@@ -298,34 +388,39 @@
         return pltpu.make_async_copy(stage.at[slot], out_ref.at[place(step)], stage_sems.at[slot])
 
     def to_chip(step):
+        slot = place(step)
         return remote(
-            part.at[step],
-            got_ref.at[step],
-            part_send.at[step],
-            part_recv.at[step],
-            chip=lax.rem(chip + step + 1, chips),
+            part.at[step - 1],
+            got_ref.at[slot - 1],
+            part_send.at[step - 1],
+            part_recv.at[slot - 1],
+            chip=lax.rem(chip + slot, chips),
         )
 
     def total(step, which):
         slot = lax.rem(step, 2)
         return keep[slot, which].astype(FLOAT) + sib_in[slot, which].astype(FLOAT)
 
-    for copy in loads(0):
+    x_local.start()
+    x_forward[0].start()
+    for copy in x_copies[0]:
         copy.start()
+    load(0, 1).start()
     gg_ref[...] = jnp.zeros(gg_ref.shape, FLOAT)
     gu_ref[...] = jnp.zeros(gu_ref.shape, FLOAT)
     gd_ref[...] = jnp.zeros(gd_ref.shape, FLOAT)
 
     def body(step, nothing):
         slot = lax.rem(step, 2)
-        for copy in loads(step):
-            copy.wait()
+        came(step)
+        load(step, 0).start()
+        load(step, 1).wait()
 
         @pl.when(step < chips - 1)
         def _():
-            for copy in loads(step + 1):
-                copy.start()
-
+            load(step + 1, 1).start()
+
+        load(step, 0).wait()
         tokens = x_buf[slot]
         cotangent = c_buf[slot]
         gate = dot(tokens, gate_ref[...])
@@ -342,6 +437,10 @@
             to_sibling(step).wait_send()
             pl.semaphore_wait(free_sem, 1)
 
+        @pl.when(step > 0)
+        def _():
+            advance(step)
+
         def back(part_of):
             return (
                 product_t(grad_gate[part_of], gate_ref[...])
@@ -362,8 +461,15 @@
         def _():
             before = step - 1
             to_sibling(before).wait_recv()
-            part[before] = total(before, 0).astype(BFLOAT)
-            to_chip(before).start()
+
+            @pl.when(before == 0)
+            def _():
+                grad_ref[...] = total(before, 0)
+
+            @pl.when(before > 0)
+            def _():
+                part[before - 1] = total(before, 0).astype(BFLOAT)
+                to_chip(before).start()
 
             @pl.when(step > 2)
             def _():
@@ -376,12 +482,19 @@
         gg_ref[...] += t_product(tokens, grad_gate)
         gu_ref[...] += t_product(tokens, grad_up)
         gd_ref[...] += t_product(cotangent, hidden)
+
+        @pl.when(step == 0)
+        def _():
+            advance(step)
+
         return nothing
 
+    x_local.wait()
     lax.fori_loop(0, chips, body, 0)
     last = chips - 1
     to_sibling(last).wait_recv()
-    grad_ref[...] = total(last, 0)
+    part[last - 1] = total(last, 0).astype(BFLOAT)
+    to_chip(last).start()
     if chips > 2:
         stage_copy(last).wait()
     stage[last % 2] = total(last, 1).astype(BFLOAT)
@@ -401,13 +514,13 @@
 
     def finish(step, nothing):
         to_chip(step).wait_recv()
-        load = pltpu.make_async_copy(got_ref.at[step], wide.at[0], load_sems.at[0, 0])
-        load.start()
-        load.wait()
+        fetch = pltpu.make_async_copy(got_ref.at[place(step) - 1], wide.at[0], load_sems.at[0, 0])
+        fetch.start()
+        fetch.wait()
         grad_ref[...] += wide[0].astype(FLOAT)
         return nothing
 
-    lax.fori_loop(0, chips - 1, finish, 0)
+    lax.fori_loop(1, chips, finish, 0)
     wide[0] = grad_ref[...].astype(BFLOAT)
     across = remote(wide.at[0], wide.at[1], cross_sems.at[0], cross_sems.at[1], tensor=1 - tensor)
     across.start()
@@ -416,7 +529,9 @@
         to_chip(step).wait_send()
         return nothing
 
-    lax.fori_loop(0, chips - 1, drain, 0)
+    lax.fori_loop(1, chips, drain, 0)
+    for copy in x_copies[0] + x_copies[1] + x_forward:
+        copy.wait_send()
     for copy in ffg_copies:
         copy.wait()
     for step in range(max(0, chips - 2), chips):
@@ -428,7 +543,7 @@
 
 
 def feed(tokens, cotangent, weights):
-    chips, count, model = tokens.shape
+    chips, count, model = cotangent.shape
     rows = count // CORES
     units = weights.shape[2]
     near = pl.BlockSpec(memory_space=pltpu.VMEM)
@@ -436,12 +551,13 @@
     return pl.pallas_call(
         functools.partial(feed_kernel, chips),
         in_specs=[far, far, near],
-        out_specs=[near, far, far, far],
+        out_specs=[near, far, far, far, far],
         out_shape=[
             jax.ShapeDtypeStruct((rows, model), FLOAT),
             jax.ShapeDtypeStruct((chips, rows, model), BFLOAT),
             jax.ShapeDtypeStruct(weights.shape, BFLOAT),
             jax.ShapeDtypeStruct((chips - 1, rows, model), BFLOAT),
+            jax.ShapeDtypeStruct((chips, count, model), BFLOAT),
         ],
         scratch_shapes=[
             pltpu.VMEM((2, count, model), BFLOAT),
@@ -464,6 +580,11 @@
             dma_row(2),
             dma_row(3 * model // count),
             pltpu.SemaphoreType.REGULAR,
+            dma_row(chips),
+            dma_row(chips),
+            dma_row(chips),
+            dma_row(chips),
+            pltpu.SemaphoreType.DMA,
         ],
         compiler_params=pltpu.CompilerParams(
             vmem_limit_bytes=62 * 1024 * 1024, collective_id=1, has_side_effects=True
@@ -487,10 +608,10 @@
     wqkv_ref, wo_ref, gate_ref, up_ref, down_ref, cot_ref,
     qkv_ref, wof_ref, normed_ref, low_ref, mid_ref, res_ref, q_ref, k_ref, v_ref,
     phi_q_ref, phi_k_ref, att_ref, den_ref, state_ref,
-    ff_ref, call_ref, xall_ref,
-    hid_sib, vm, rim_out, rim_in, st_out, st_in, num, br_out, br_in, tz_out, tz_in, xn,
+    xn, ff_ref, call_ref,
+    hid_sib, vm, rim_out, rim_in, st_out, st_in, num, br_out, br_in, tz_out, tz_in,
     hid_sem, q1_send, q1_recv, q2_send, q2_recv, o1_send, o1_recv, o2_send, o2_recv,
-    ff_send, ff_recv, local_sems, c_send, c_recv, cf_send, cf_recv, x_send, x_recv, xf_send, xf_recv,
+    ff_send, ff_recv, local_sems, c_send, c_recv, cf_send, cf_recv,
     rim_sem, st_send, st_recv, br_sem, tz_sem,
 ):
     dp, chip, core, tensor = (lax.axis_index(name) for name in ("dp", "chip", "core", "tensor"))
@@ -543,6 +664,9 @@
     hid_copy.start()
     for copy in q_first:
         copy.start()
+    o_local.start()
+    for copy in o_first:
+        copy.start()
 
     ff_rows = pl.ds(((dp * chips + chip) * CORES + core) * shard, shard)
     ff_sources = (gate_ref, up_ref, down_ref)
@@ -573,31 +697,17 @@
 
         lax.fori_loop(1 - side, pairs, one, 0)
 
-    def row_copies(source, target, send, recv):
-        return [
-            remote(source, target.at[step + 1, pl.ds(0, own)], send.at[step], recv.at[step], chip=to)
-            for step, to in enumerate(behind)
-        ]
-
-    def forward_copy(source, target, send, recv, step):
-        return remote(source, target.at[step, pl.ds(own, own)], send.at[step], recv.at[step], **sibling)
-
-    c_copies = row_copies(cot_ref, call_ref, c_send, c_recv)
-    x_copies = row_copies(xn, xall_ref, x_send, x_recv)
-    c_forward = [
-        forward_copy(cot_ref if step == 0 else call_ref.at[step, pl.ds(0, own)], call_ref, cf_send, cf_recv, step)
-        for step in range(chips)
-    ]
-    x_forward = [
-        forward_copy(xn if step == 0 else xall_ref.at[step, pl.ds(0, own)], xall_ref, xf_send, xf_recv, step)
-        for step in range(chips)
-    ]
+    c_copies = row_copies(chips, chip, cot_ref, call_ref, c_send, c_recv)
+    c_forward = forward_copies(chips, chip, core, cot_ref, call_ref, cf_send, cf_recv)
     c_local = pltpu.make_async_copy(cot_ref, call_ref.at[0, pl.ds(0, own)], local_sems.at[5])
-    x_local = pltpu.make_async_copy(xn, xall_ref.at[0, pl.ds(0, own)], local_sems.at[6])
 
     def normalized(rows, gain):
         return (rows * lax.rsqrt(jnp.mean(rows * rows, axis=1, keepdims=True) + EPS) * gain).astype(BFLOAT)
 
+    ff_start(0, 1)
+    for which in range(3):
+        ff_local(which).start()
+    c_local.start()
     hidden = hid_ref[...].astype(FLOAT)
     normed_ref[pl.ds(pl.multiple_of(core * own, own), own)] = normalized(hidden, again_ref[...])
     q_first[0].wait_recv()
@@ -613,13 +723,6 @@
     q_first[2].wait_recv()
     for copy in q_second[1]:
         copy.start()
-    o_local.start()
-    for copy in o_first:
-        copy.start()
-    for which in range(3):
-        ff_local(which).start()
-    c_local.start()
-    ff_start(0, 1)
     o_first[0].wait_recv()
     o_local.wait()
     for copy in o_second[0]:
@@ -627,12 +730,8 @@
     for side in range(2):
         for copy in q_second[side]:
             copy.wait_recv()
-    o_first[1].wait_recv()
-    o_first[2].wait_recv()
-    for copy in o_second[1]:
-        copy.start()
+    ff_start(0, 0)
     ff_start(1, 1)
-    ff_start(0, 0)
 
     pre = dot(normed_ref[...], qkv_ref[...]) + dot(low_ref[...], ups_ref[...])
     half = HEAD_SIZE // 2
@@ -700,8 +799,14 @@
     ]
     for copy in st_copies:
         copy.start()
-    ff_start(2, 1)
+    o_first[1].wait_recv()
+    o_first[2].wait_recv()
+    for copy in o_second[1]:
+        copy.start()
     ff_start(1, 0)
+    c_forward[0].start()
+    for copy in c_copies[0]:
+        copy.start()
     for at in range(kv_heads):
         heads, one, wide = views(at)
         intra_kernel(
@@ -740,11 +845,10 @@
     tz_out[:, model:] = (low_part + br_in[:, model:].astype(FLOAT)).astype(BFLOAT)
     tz_copy = remote(tz_out, tz_in, tz_sem.at[0], tz_sem.at[1], tensor=1 - tensor)
     tz_copy.start()
+    ff_start(2, 1)
+    tz_copy.wait_recv()
+    relay(c_copies)
     ff_start(2, 0)
-    c_forward[0].start()
-    for copy in c_copies:
-        copy.start()
-    tz_copy.wait_recv()
     mid = (tz_out[:, model:].astype(FLOAT) + tz_in[:, model:].astype(FLOAT)).astype(BFLOAT)
     mid_ref[...] = mid
     residual = (
@@ -754,29 +858,19 @@
     )
     res_ref[...] = residual
     xn[...] = normalized(residual, fgain_ref[...])
-    x_local.start()
-    x_forward[0].start()
-    for copy in x_copies:
-        copy.start()
-    for step in range(1, chips):
-        c_copies[step - 1].wait_recv()
-        c_forward[step].start()
-    for step in range(1, chips):
-        x_copies[step - 1].wait_recv()
-        x_forward[step].start()
+    hand_over(c_copies, c_forward)
 
     hid_done = [br_copy, tz_copy] + q_first + o_first + q_second[0] + q_second[1]
-    for copy in hid_done + o_second[0] + o_second[1] + st_copies + c_copies + x_copies:
+    for copy in hid_done + o_second[0] + o_second[1] + st_copies + c_copies[0] + c_copies[1]:
         copy.wait_send()
 
     @pl.when(chip < chips - 1)
     def _():
         rim_copy.wait_send()
 
-    for copy in c_forward + x_forward:
+    for copy in c_forward:
         copy.wait()
     c_local.wait()
-    x_local.wait()
     moved = (2 * pairs - 1) * shard
     for which in range(3):
         ff_local(which).wait()
@@ -811,10 +905,10 @@
         ((tokens, q_width), BFLOAT),
         ((kv_heads, tokens, 128), FLOAT),
         ((heads, 128, 128), BFLOAT),
+        ((own, model), BFLOAT),
     ]
     far_outs = [
         ((3, model, units), BFLOAT),
-        ((chips, tokens, model), BFLOAT),
         ((chips, tokens, model), BFLOAT),
     ]
     pair = dma_row(2)
@@ -835,7 +929,6 @@
             pltpu.VMEM((own, model + 128), BFLOAT),
             pltpu.VMEM((own, model + 128), BFLOAT),
             pltpu.VMEM((own, model + 128), BFLOAT),
-            pltpu.VMEM((own, model), BFLOAT),
             pair,
             dma_row(3),
             dma_row(3),
@@ -848,12 +941,8 @@
             dma_row(3),
             dma_row(3),
             dma_row(7),
-            dma_row(chips - 1),
-            dma_row(chips - 1),
             dma_row(chips),
             dma_row(chips),
-            dma_row(chips - 1),
-            dma_row(chips - 1),
             dma_row(chips),
             dma_row(chips),
             pair,
@@ -1039,13 +1128,12 @@
     db_copy = remote(db.at[mine], db.at[mine], db_sem.at[0], db_sem.at[1], **sibling)
     db_copy.start()
     ff_start(0, 1)
-    for copy in os_copies:
-        copy.start()
+    os_copies[0].start()
     for which in range(3):
         ff_local(which).start()
     up_rows = t_product(mid_ref[...], db[mine])[:rank]
     filler = jnp.zeros((16 - 1 - rank, model), FLOAT)
-    small_start(1, jnp.concatenate([up_rows, gain_row, filler], axis=0))
+    early_rows = jnp.concatenate([up_rows, gain_row, filler], axis=0)
     db_copy.wait_recv()
     dmid = product_t(db[...], oup_ref[...]).astype(BFLOAT)
     dq[...] = dot(db[...], wof_ref[...]) + product_t(dmid, odown_ref[...])
@@ -1070,10 +1158,9 @@
     ]
     for copy in ds_copies:
         copy.start()
-    ff_start(1, 1)
+    small_start(1, early_rows)
+    ff_start(0, 0)
     og[...] = t_product(db[...], att_ref[...]).astype(BFLOAT)
-    for copy in o_copies:
-        copy.start()
     down_rows = t_product(dmid, att_ref[...])[:rank]
     for at in range(kv_heads):
         heads, one, wide = views(at)
@@ -1119,6 +1206,8 @@
         pieces = [table[head, :, :FEATURE_HALF] - table[head, :, FEATURE_HALF:] for table in (gq, gk)]
         tables.append(jnp.concatenate(pieces, axis=1))
     small_start(0, jnp.concatenate(tables, axis=0))
+    for copy in o_copies:
+        copy.start()
     half = HEAD_SIZE // 2
     first_half = lax.rem(lanes((tokens, 128)), HEAD_SIZE) < half
 
@@ -1160,21 +1249,15 @@
     tz_out[:, model:] = (low_part + br_in[:, model:].astype(FLOAT)).astype(BFLOAT)
     tz_copy = remote(tz_out, tz_in, tz_sem.at[0], tz_sem.at[1], tensor=1 - tensor)
     tz_copy.start()
+    ff_start(1, 1)
     qg[...] = t_product(normed_ref[...], gp[...]).astype(BFLOAT)
     for copy in q_copies:
         copy.start()
-    grads_middle(o_copies, og, o_in, o_dp_out, o_across)
-    ff_start(2, 1)
-    ff_start(0, 0)
-    ff_start(1, 0)
-    ff_start(2, 0)
     ups_rows = t_product(low_ref[...], gp[...])[: 3 * rank]
     wide_down = jnp.concatenate(
         [down_rows, jnp.zeros((rank, gp.shape[1] - q_width), FLOAT)], axis=1
     )
     small_start(2, jnp.concatenate([ups_rows, wide_down], axis=0))
-    small_middle(1)
-    small_middle(0)
     tz_copy.wait_recv()
     low = (tz_out[:, model:].astype(FLOAT) + tz_in[:, model:].astype(FLOAT)).astype(BFLOAT)
     grad_normed = (
@@ -1185,10 +1268,17 @@
     igrad_ref[...] = (dres[...] + back_rows).astype(BFLOAT)
     filler = jnp.zeros((rank - 1, model), FLOAT)
     small_start(3, jnp.concatenate([low_rows, gain_row, filler], axis=0))
-    small_end(1)
-    small_end(0)
+    for copy in os_copies[1:]:
+        copy.start()
+    ff_start(1, 0)
+    ff_start(2, 0)
+    grads_middle(o_copies, og, o_in, o_dp_out, o_across)
+    ff_start(2, 1)
+    small_middle(1)
+    small_middle(0)
     small_middle(2)
-    grads_end(og, o_in, o_dp_in, o_across, o_own, o_core, o_over)
+    grads_middle(q_copies, qg, q_in, q_dp_out, q_across)
+    small_middle(3)
 
     os_buf = tz_in.at[:, pl.ds(0, model)]
     load = pltpu.make_async_copy(out_ref.at[0], os_buf, o_load.at[0])
@@ -1206,9 +1296,9 @@
     oz_out[...] = dres[...].astype(BFLOAT)
     oz_copy = remote(oz_out, oz_in, oz_sem.at[0], oz_sem.at[1], tensor=1 - tensor)
     oz_copy.start()
-    grads_middle(q_copies, qg, q_in, q_dp_out, q_across)
-    small_end(2)
-    small_middle(3)
+    grads_end(og, o_in, o_dp_in, o_across, o_own, o_core, o_over)
+    for which in range(3):
+        small_end(which)
     oz_copy.wait()
     block_ref[...] = (
         res_ref[...] + (oz_out[...].astype(FLOAT) + oz_in[...].astype(FLOAT))
@@ -1350,17 +1440,21 @@
 
 
 def carry_coefs(lengths, tokens):
-    count = lax.axis_size("chip")
+    chips = lax.axis_size("chip")
     me = lax.axis_index("chip")
-    starts = jnp.arange(count, dtype=jnp.int32) * tokens
-    open_chip = locate(starts - 1, lengths)[0] == locate(starts + tokens - 1, lengths)[0]
-    source = jnp.arange(count)[:, None]
-    between = jnp.arange(count)[None, :]
-    after = (between > source) & (between < me)
-    before = (between < source) & (between > me)
-    forward = jnp.all(open_chip[None, :] | ~after, axis=1) & (source[:, 0] < me)
-    backward = jnp.all(open_chip[None, :] | ~before, axis=1) & (source[:, 0] > me)
-    return forward.astype(FLOAT), backward.astype(FLOAT)
+    steps = jnp.arange(1, chips, dtype=jnp.int32)
+    behind, ahead = lax.rem(me + chips - steps, chips), lax.rem(me + steps, chips)
+    places = jnp.stack(
+        [behind * tokens + tokens - 1, ahead * tokens - 1, 0 * steps + me * tokens - 1]
+        + [0 * steps + me * tokens + tokens - 1]
+    )
+    segment = locate(places, lengths)[0]
+    forward = (behind < me) & (segment[0] == segment[2])
+    backward = (ahead > me) & (segment[1] == segment[3])
+    return [
+        jnp.broadcast_to(row.astype(FLOAT)[:, None, None], (chips - 1, 1, 128))
+        for row in (forward, backward)
+    ]
 
 
 def on_device(
@@ -1423,19 +1517,18 @@
 
     first_row = chip * tokens
     lengths = doc_lengths[0]
-    seg_rows, pos_rows = locate(first_row + jnp.arange(tokens, dtype=jnp.int32), lengths)
-    seg_rim = locate(first_row - SOFTMAX_KEYS + jnp.arange(SOFTMAX_KEYS, dtype=jnp.int32), lengths)[
-        0
-    ]
-    seg_first = locate(jnp.reshape(first_row - 1, (1,)), lengths)[0][0]
     gap = 128 - SOFTMAX_KEYS
-    seg_ext = jnp.concatenate([jnp.full((gap,), -2, jnp.int32), seg_rim, seg_rows])
-    seg_last = seg_rows[tokens - 1]
+    spots = jnp.arange(tokens + 128, dtype=jnp.int32)
+    seg_ext, pos_ext = locate(first_row + spots - 128, lengths)
+    seg_ext = jnp.where(spots < gap, -2, seg_ext)
+    seg_rows, pos_rows = seg_ext[128:], pos_ext[128:]
+    seg_first = locate(first_row - 1, lengths)[0]
+    seg_last = locate(first_row + tokens - 1, lengths)[0]
     continuing = (seg_rows == seg_first).astype(FLOAT)[:, None]
     carry = ((jnp.arange(tokens + 128) < tokens + gap) & (seg_ext == seg_last)).astype(FLOAT)[:, None]
     seg_column, seg_line = seg_rows[:, None], seg_ext[None, :]
     forward_coefs, backward_coefs = carry_coefs(lengths, tokens)
-    cosine_table, sine_table = rotation(pos_rows, HEAD_SIZE)
+    wide_cosine, wide_sine = rotation(pos_rows, HEAD_SIZE)
     query_table = own_heads(query_feature_maps, heads, core)
     key_table = own_heads(key_feature_maps, heads, core)
     query_table = jnp.concatenate([query_table, -query_table], axis=2)
@@ -1456,20 +1549,12 @@
         axis=0,
     )
     extent = tokens + 128
-    behind = [lax.rem(chip + chips - step, chips) for step in range(1, chips)]
-    ahead = [lax.rem(chip + step, chips) for step in range(1, chips)]
-
-    def coef_rows(coefs, places):
-        rows = jnp.stack([coefs[at] for at in places])
-        return jnp.broadcast_to(rows[:, None, None], (chips - 1, 1, 128))
-
-    wide_cosine, wide_sine = spread(cosine_table, 128), spread(sine_table, 128)
     wide_downs = jnp.pad(downs, ((0, 0), (0, pad)))
     wide_output_down = jnp.pad(own_output_down, ((0, 0), (0, 128 - rank)))
     wide_output_up = jnp.pad(output_up, ((0, 128 - rank), (0, 0)))
     (
         full_qkv, full_out, normed, low_rank, low_mid, residual, queries, key_ext, value_ext,
-        phi_q, phi_k, attended, denominator, state, full_ff, cotangents, gathered,
+        phi_q, phi_k, attended, denominator, state, normed_ff, full_ff, cotangents,
     ) = front(
         chips,
         kv_heads,
@@ -1489,13 +1574,13 @@
             seg_line,
             continuing,
             carry,
-            coef_rows(forward_coefs, behind),
+            forward_coefs,
             wide_output_down,
             wide_output_up,
         ],
         [wqkv, wout, gate_weight, up_weight, down_weight.T, block_cotangent],
     )
-    grad_normed_ff, out_sums, ff_grads, _ = feed(gathered, cotangents, full_ff)
+    grad_normed_ff, out_sums, ff_grads, _, _ = feed(normed_ff, cotangents, full_ff)
     rear_outs = rear(
         chips,
         kv_heads,
@@ -1526,7 +1611,7 @@
             seg_line,
             continuing,
             carry,
-            coef_rows(backward_coefs, ahead),
+            backward_coefs,
             wide_cosine,
             wide_sine,
             normed,
@@ -1549,8 +1634,8 @@
     key_shard = by_core(1, qkv_keep[:, at_key:at_value], qkv_other[:, at_key:at_value])
     value_shard = by_core(1, qkv_keep[:, at_value:], qkv_other[:, at_value:])
     output_shard = by_core(1, out_keep, out_other).T
-    ff_shards = rear_outs[14].astype(FLOAT)
-    ff_shards = ff_shards[:, 0] + ff_shards[:, 1]
+    ff_both = rear_outs[14]
+    ff_shards = [ff_both[at, 0].astype(FLOAT) + ff_both[at, 1].astype(FLOAT) for at in range(3)]
 
     tables = by_core(0, own_small[0], sib_small[0]).reshape(CORES * heads, HEAD_SIZE, 128)
     early = own_small[1] + sib_small[1]

time: 729 us -> 696 us (0.955)
  Pallas kernels: 666 us -> 642 us
    pallas_call x1, Pallas kernels: 304 us -> 256 us  [rear(): pl.pallas_call(functools.partial(rear_kernel, chips, kv_heads, group, ran...]
    pallas_call x1, Pallas kernels: 112 us -> 158 us  [feed(): pl.pallas_call(functools.partial(feed_kernel, chips), in_specs=[far, far,...]
    pallas_call x1, Pallas kernels: 251 us -> 228 us  [front(): pl.pallas_call(functools.partial(front_kernel, chips, kv_heads, group), i...]
where the time goes in v3:
time: 696 us; the launch traced here: 690 us
  Pallas kernels  642 us (92%)
  local copies, waits for them, and re-layouts  23 us (3%)
  other arithmetic  20.9 us (3%)
    pallas_call x1, Pallas kernels, rear(): pl.pallas_call(functools.partial(rear_kernel, chips, kv_heads, group, ran...  256 us
    pallas_call x1, Pallas kernels, front(): pl.pallas_call(functools.partial(front_kernel, chips, kv_heads, group), i...  228 us
    pallas_call x1, Pallas kernels, feed(): pl.pallas_call(functools.partial(feed_kernel, chips), in_specs=[far, far,...  158 us

profile of v3, /device:TPU:15, one launch (start us, length us, event | category | flops | bytes accessed | tf_op | source)
XLA Modules:
  0.0 689.8 jit_solution(5745139248992500928)
XLA Ops:
  0.7 1.3 fusion.43
  4.7 0.9 copy.80.cont_ref
  6.2 1.5 fusion.10.carry_ref
  7.9 0.7 add_select_fusion
  9.3 0.7 constant_dynamic-slice_fusion.3
  10.1 0.8 fusion.13.ups_ref
  10.8 1.0 fusion.30
  11.8 0.8 pad_maximum_fusion.1.fq_ref
  12.6 0.8 pad_maximum_fusion.2.fk_ref
  13.4 1.8 fusion.11
  15.2 0.9 copy.79.seg_q_ref
  16.1 1.2 compare_select_fusion.1.seg_k_ref
  17.5 0.7 pad.28.odown_ref
  18.3 0.8 pad_maximum_fusion.wqkv_ref
  19.4 0.9 pad.24.downs_ref
  20.3 1.3 copy.78
  21.6 0.8 pad.29.oup_ref
  22.5 0.9 copy.77
  23.3 227.8 %shard_map.391 = (bf16[2048,768]{1,0:T(8,128)(2,1)}, bf16[2048,512]{1,0:T(8,128)(2,1)}, bf16[512,2048]{1,0:T(8,128)(2,1)}, bf16[512,128]{1,0:T(8,128)(2,1)}, bf1...) custom-call(bf16[256,2048]{1,0:T(8,128)(2,1)} %hid_ref.3, ...), custom_call_target="tpu_custom_call" | custom-call | flops 10000000000 | bytes 100000000 | tf_op jit(solution)/shard_map/pallas_call | solution.py:915
  251.1 157.7 %shard_map.392 = (f32[256,2048]{1,0:T(8,128)}, bf16[4,256,2048]{2,1,0:T(8,128)(2,1)}, bf16[3,2048,512]{2,1,0:T(8,128)(2,1)}, bf16[3,256,2048]{2,1,0:T(8,128)(2,1)}, bf16[4,512,2048]{2,1,0:T(8,128)(2,1)}) custom-call(bf16[256,2048]{1,0:T(8,128)(2,1)} %get-tuple-element.56.x_ref, bf16[4,512,2048]{2,1,0:T(8,128)(2,1)} %get-tuple-element.57.c_ref, ...), custom_call_target="tpu_custom_call" | custom-call | flops 38654705664 | bytes 33554432 | tf_op jit(solution)/shard_map/pallas_call | solution.py:551
  410.8 256.2 %shard_map.393 = (bf16[256,2048]{1,0:T(8,128)(2,1)}, bf16[256,2048]{1,0:T(8,128)(2,1)}, f32[128,768]{1,0:T(8,128)}, bf16[128,768]{1,0:T(8,128)(2,1)}, f32[128,51...) custom-call(f32[256,2048]{1,0:T(8,128)} %get-tuple-element.59.gnf_re, ...), custom_call_target="tpu_custom_call" | custom-call | flops 40000000000 | bytes 100000000 | tf_op jit(solution)/shard_map/pallas_call | solution.py:1376
  667.0 6.0 add_bitcast_fusion
  673.0 1.8 copy.84
  674.9 1.1 fusion.32
  677.3 0.7 fusion.37
  678.1 0.7 fusion.38
  679.4 0.7 fusion.39
  680.1 0.7 fusion.40
  682.7 1.0 copy.83
  685.2 0.8 maximum_select_fusion
  687.4 1.0 copy.90
  688.3 1.0 copy.91
  (95 shorter events, 10.7 us)
Async XLA Ops:
  0.7 8.6 %copy-start = (bf16[8,1024]{1,0:T(8,128)(2,1)S(1)}, bf16[8,1024]{1,0:T(8,128)(2,1)}, u32[]{:S(2)}) copy-start(bf16[8,1024]{1,0:T(8,128)(2,1)} %param.32) | copy-start | bytes 49156
  0.7 12.7 %copy-start.24 = (f32[128]{0:T(128)S(1)}, f32[128]{0:T(128)}, u32[]{:S(2)}) copy-start(f32[128]{0:T(128)} %constant.79) | copy-start | bytes 1540
  0.7 12.7 %copy-start.25 = (f32[128]{0:T(128)S(1)}, f32[128]{0:T(128)}, u32[]{:S(2)}) copy-start(f32[128]{0:T(128)} %constant.80) | copy-start | bytes 1540
  0.7 16.6 %copy-start.23 = (bf16[1024,8]{0,1:T(8,128)(2,1)S(1)}, bf16[1024,8]{0,1:T(8,128)(2,1)}, u32[]{:S(2)}) copy-start(bf16[1024,8]{0,1:T(8,128)(2,1)} %param.37) | copy-start | bytes 49156
  0.7 17.5 %copy-start.9 = (bf16[128,1024]{1,0:T(8,128)(2,1)S(1)}, bf16[128,1024]{1,0:T(8,128)(2,1)}, u32[]{:S(2)}) copy-start(bf16[128,1024]{1,0:T(8,128)(2,1)} %param.27) | copy-start | bytes 786436
  4.7 13.5 %copy-start.18 = (bf16[128,256]{1,0:T(8,128)(2,1)S(1)}, bf16[128,256]{1,0:T(8,128)(2,1)}, u32[]{:S(2)}) copy-start(bf16[128,256]{1,0:T(8,128)(2,1)} %param.28) | copy-start | bytes 196612
  5.6 12.7 %copy-start.19 = (bf16[128,256]{1,0:T(8,128)(2,1)S(1)}, bf16[128,256]{1,0:T(8,128)(2,1)}, u32[]{:S(2)}) copy-start(bf16[128,256]{1,0:T(8,128)(2,1)} %param.29) | copy-start | bytes 196612
  12.6 6.5 copy-start.20
  12.6 6.5 copy-start.21
  12.6 6.5 copy-start.22
  18.2 2.1 copy-start.2
  19.1 2.5 copy-start.17
  19.1 3.4 copy-start.10
  673.0 1.8 copy-start.12
  673.0 1.8 copy-start.13
  674.8 1.2 copy-start.15
  674.8 1.2 copy-start.16
  674.8 7.8 %copy-start.14 = (bf16[128,512]{1,0:T(8,128)(2,1)S(1)}, bf16[128,512]{1,0:T(8,128)(2,1)}, u32[]{:S(2)}) copy-start(bf16[128,512]{1,0:T(8,128)(2,1)} %get-tuple-element.83) | copy-start | bytes 393220
  674.9 7.8 %copy-start.11 = (f32[128,512]{1,0:T(8,128)S(1)}, f32[128,512]{1,0:T(8,128)}, u32[]{:S(2)}) copy-start(f32[128,512]{1,0:T(8,128)} %get-tuple-element.82) | copy-start | bytes 786436
  676.0 7.7 %copy-start.6 = (f32[128,768]{1,0:T(8,128)S(1)}, f32[128,768]{1,0:T(8,128)}, u32[]{:S(2)}) copy-start(f32[128,768]{1,0:T(8,128)} %get-tuple-element.80) | copy-start | bytes 1179652
  676.0 7.7 %copy-start.5 = (bf16[128,768]{1,0:T(8,128)(2,1)S(1)}, bf16[128,768]{1,0:T(8,128)(2,1)}, u32[]{:S(2)}) copy-start(bf16[128,768]{1,0:T(8,128)(2,1)} %get-tuple-element.81) | copy-start | bytes 589828
  682.7 3.3 copy-start.7
  682.7 3.3 copy-start.8
  683.8 3.6 copy-start.4
  686.0 2.3 copy-start.3
  687.4 2.0 copy-start.1

commit v4 on v3

--- a/solution.py
+++ b/solution.py
@@ -323,7 +323,7 @@
 def feed_kernel(
     chips, x_ref, c_ref, ff_ref,
     grad_ref, out_ref, ffg_ref, got_ref, xall_ref,
-    x_buf, c_buf, gg_ref, gu_ref, gd_ref, keep, sib_out, sib_in, part, stage, wide,
+    x_buf, c_buf, gg_ref, gu_ref, gd_ref, keep, sib_out, sib_in, part, stage, cross_in,
     load_sems, stage_sems, sib_send, sib_recv, part_send, part_recv, cross_sems, ffg_sems, free_sem,
     x_send, x_recv, xf_send, xf_recv, x_sem,
 ):
@@ -387,15 +387,24 @@
         slot = lax.rem(step, 2)
         return pltpu.make_async_copy(stage.at[slot], out_ref.at[place(step)], stage_sems.at[slot])
 
+    halves = [pl.ds(0, rows // 2), pl.ds(rows // 2, rows // 2)]
+
     def to_chip(step):
         slot = place(step)
-        return remote(
-            part.at[step - 1],
-            got_ref.at[slot - 1],
-            part_send.at[step - 1],
-            part_recv.at[slot - 1],
-            chip=lax.rem(chip + slot, chips),
-        )
+        return [
+            remote(
+                part.at[step - 1, piece],
+                got_ref.at[slot - 1, piece],
+                part_send.at[step - 1, at],
+                part_recv.at[slot - 1, at],
+                chip=lax.rem(chip + slot, chips),
+            )
+            for at, piece in enumerate(halves)
+        ]
+
+    def send_part(step):
+        for copy in to_chip(step):
+            copy.start()
 
     def total(step, which):
         slot = lax.rem(step, 2)
@@ -469,7 +478,7 @@
             @pl.when(before > 0)
             def _():
                 part[before - 1] = total(before, 0).astype(BFLOAT)
-                to_chip(before).start()
+                send_part(before)
 
             @pl.when(step > 2)
             def _():
@@ -494,7 +503,7 @@
     last = chips - 1
     to_sibling(last).wait_recv()
     part[last - 1] = total(last, 0).astype(BFLOAT)
-    to_chip(last).start()
+    send_part(last)
     if chips > 2:
         stage_copy(last).wait()
     stage[last % 2] = total(last, 1).astype(BFLOAT)
@@ -512,21 +521,33 @@
             copy.start()
             ffg_copies.append(copy)
 
-    def finish(step, nothing):
-        to_chip(step).wait_recv()
-        fetch = pltpu.make_async_copy(got_ref.at[place(step) - 1], wide.at[0], load_sems.at[0, 0])
-        fetch.start()
-        fetch.wait()
-        grad_ref[...] += wide[0].astype(FLOAT)
-        return nothing
-
-    lax.fori_loop(1, chips, finish, 0)
-    wide[0] = grad_ref[...].astype(BFLOAT)
-    across = remote(wide.at[0], wide.at[1], cross_sems.at[0], cross_sems.at[1], tensor=1 - tensor)
-    across.start()
+    wide = keep.at[0, 0]
+    across = []
+    for at, piece in enumerate(halves):
+
+        def finish(step, nothing, at=at, piece=piece):
+            to_chip(step)[at].wait_recv()
+            fetch = pltpu.make_async_copy(
+                got_ref.at[place(step) - 1, piece], wide.at[piece], load_sems.at[0, 0]
+            )
+            fetch.start()
+            fetch.wait()
+            grad_ref[piece] += wide[piece].astype(FLOAT)
+            return nothing
+
+        lax.fori_loop(1, chips, finish, 0)
+        wide[piece] = grad_ref[piece].astype(BFLOAT)
+        across.append(
+            remote(
+                wide.at[piece], cross_in.at[piece], cross_sems.at[0, at], cross_sems.at[1, at],
+                tensor=1 - tensor,
+            )
+        )
+        across[at].start()
 
     def drain(step, nothing):
-        to_chip(step).wait_send()
+        for copy in to_chip(step):
+            copy.wait_send()
         return nothing
 
     lax.fori_loop(1, chips, drain, 0)
@@ -538,8 +559,9 @@
         to_sibling(step).wait_send()
         stage_copy(step).wait()
     pl.semaphore_wait(free_sem, min(1, chips - 1))
-    across.wait()
-    grad_ref[...] = wide[0].astype(FLOAT) + wide[1].astype(FLOAT)
+    for at, piece in enumerate(halves):
+        across[at].wait()
+        grad_ref[piece] = wide[piece].astype(FLOAT) + cross_in[piece].astype(FLOAT)
 
 
 def feed(tokens, cotangent, weights):
@@ -550,7 +572,7 @@
     far = pl.BlockSpec(memory_space=pl.ANY)
     return pl.pallas_call(
         functools.partial(feed_kernel, chips),
-        in_specs=[far, far, near],
+        in_specs=[near, far, near],
         out_specs=[near, far, far, far, far],
         out_shape=[
             jax.ShapeDtypeStruct((rows, model), FLOAT),
@@ -570,14 +592,14 @@
             pltpu.VMEM((2, 2, rows, model), BFLOAT),
             pltpu.VMEM((chips - 1, rows, model), BFLOAT),
             pltpu.VMEM((2, rows, model), BFLOAT),
-            pltpu.VMEM((2, rows, model), BFLOAT),
+            pltpu.VMEM((rows, model), BFLOAT),
             pltpu.SemaphoreType.DMA((2, 2)),
             dma_row(2),
             dma_row(2),
             dma_row(2),
-            dma_row(chips - 1),
-            dma_row(chips - 1),
-            dma_row(2),
+            pltpu.SemaphoreType.DMA((chips - 1, 2)),
+            pltpu.SemaphoreType.DMA((chips - 1, 2)),
+            pltpu.SemaphoreType.DMA((2, 2)),
             dma_row(3 * model // count),
             pltpu.SemaphoreType.REGULAR,
             dma_row(chips),

time: 696 us -> 663 us (0.953)
  Pallas kernels: 642 us -> 609 us
    pallas_call x1, Pallas kernels: 158 us -> 128 us  [feed(): pl.pallas_call(functools.partial(feed_kernel, chips), in_specs=[near, far...]
where the time goes in v4:
time: 663 us; the launch traced here: 657 us
  Pallas kernels  609 us (92%)
  local copies, waits for them, and re-layouts  23 us (3%)
  other arithmetic  20.9 us (3%)
    pallas_call x1, Pallas kernels, rear(): pl.pallas_call(functools.partial(rear_kernel, chips, kv_heads, group, ran...  253 us
    pallas_call x1, Pallas kernels, front(): pl.pallas_call(functools.partial(front_kernel, chips, kv_heads, group), i...  228 us
    pallas_call x1, Pallas kernels, feed(): pl.pallas_call(functools.partial(feed_kernel, chips), in_specs=[near, far...  128 us

profile of v4, /device:TPU:15, one launch (start us, length us, event | category | flops | bytes accessed | tf_op | source)
XLA Modules:
  0.0 657.3 jit_solution(1887073450260003704)
XLA Ops:
  0.7 1.3 fusion.43
  4.7 0.9 copy.80.cont_ref
  6.2 1.5 fusion.10.carry_ref
  7.9 0.7 add_select_fusion
  9.3 0.7 constant_dynamic-slice_fusion.3
  10.1 0.8 fusion.13.ups_ref
  10.8 1.0 fusion.30
  11.8 0.8 pad_maximum_fusion.1.fq_ref
  12.6 0.8 pad_maximum_fusion.2.fk_ref
  13.4 1.8 fusion.11
  15.2 0.9 copy.79.seg_q_ref
  16.1 1.2 compare_select_fusion.1.seg_k_ref
  17.5 0.7 pad.28.odown_ref
  18.3 0.8 pad_maximum_fusion.wqkv_ref
  19.4 0.9 pad.24.downs_ref
  20.3 1.3 copy.78
  21.6 0.8 pad.29.oup_ref
  22.5 0.9 copy.77
  23.3 227.8 %shard_map.391 = (bf16[2048,768]{1,0:T(8,128)(2,1)}, bf16[2048,512]{1,0:T(8,128)(2,1)}, bf16[512,2048]{1,0:T(8,128)(2,1)}, bf16[512,128]{1,0:T(8,128)(2,1)}, bf1...) custom-call(bf16[256,2048]{1,0:T(8,128)(2,1)} %hid_ref.3, ...), custom_call_target="tpu_custom_call" | custom-call | flops 10000000000 | bytes 100000000 | tf_op jit(solution)/shard_map/pallas_call | solution.py:937
  251.1 128.5 %shard_map.392 = (f32[256,2048]{1,0:T(8,128)}, bf16[4,256,2048]{2,1,0:T(8,128)(2,1)}, bf16[3,2048,512]{2,1,0:T(8,128)(2,1)}, bf16[3,256,2048]{2,1,0:T(8,128)(2,1)}, bf16[4,512,2048]{2,1,0:T(8,128)(2,1)}) custom-call(bf16[256,2048]{1,0:T(8,128)(2,1)} %get-tuple-element.56.x_ref, bf16[4,512,2048]{2,1,0:T(8,128)(2,1)} %get-tuple-element.57.c_ref, ...), custom_call_target="tpu_custom_call" | custom-call | flops 38654705664 | bytes 33554432 | tf_op jit(solution)/shard_map/pallas_call | solution.py:573
  381.6 252.9 %shard_map.393 = (bf16[256,2048]{1,0:T(8,128)(2,1)}, bf16[256,2048]{1,0:T(8,128)(2,1)}, f32[128,768]{1,0:T(8,128)}, bf16[128,768]{1,0:T(8,128)(2,1)}, f32[128,51...) custom-call(f32[256,2048]{1,0:T(8,128)} %get-tuple-element.59.gnf_re, ...), custom_call_target="tpu_custom_call" | custom-call | flops 40000000000 | bytes 100000000 | tf_op jit(solution)/shard_map/pallas_call | solution.py:1398
  634.5 6.0 add_bitcast_fusion
  640.5 1.8 copy.84
  642.4 1.1 fusion.32
  644.8 0.7 fusion.37
  645.5 0.7 fusion.38
  646.9 0.7 fusion.39
  647.6 0.7 fusion.40
  650.2 1.0 copy.83
  652.6 0.8 maximum_select_fusion
  654.8 1.0 copy.90
  655.8 1.0 copy.91
  (95 shorter events, 10.7 us)
Async XLA Ops:
  0.7 8.6 %copy-start = (bf16[8,1024]{1,0:T(8,128)(2,1)S(1)}, bf16[8,1024]{1,0:T(8,128)(2,1)}, u32[]{:S(2)}) copy-start(bf16[8,1024]{1,0:T(8,128)(2,1)} %param.32) | copy-start | bytes 49156
  0.7 12.7 %copy-start.24 = (f32[128]{0:T(128)S(1)}, f32[128]{0:T(128)}, u32[]{:S(2)}) copy-start(f32[128]{0:T(128)} %constant.79) | copy-start | bytes 1540
  0.7 12.7 %copy-start.25 = (f32[128]{0:T(128)S(1)}, f32[128]{0:T(128)}, u32[]{:S(2)}) copy-start(f32[128]{0:T(128)} %constant.80) | copy-start | bytes 1540
  0.7 16.6 %copy-start.23 = (bf16[1024,8]{0,1:T(8,128)(2,1)S(1)}, bf16[1024,8]{0,1:T(8,128)(2,1)}, u32[]{:S(2)}) copy-start(bf16[1024,8]{0,1:T(8,128)(2,1)} %param.37) | copy-start | bytes 49156
  0.7 17.5 %copy-start.9 = (bf16[128,1024]{1,0:T(8,128)(2,1)S(1)}, bf16[128,1024]{1,0:T(8,128)(2,1)}, u32[]{:S(2)}) copy-start(bf16[128,1024]{1,0:T(8,128)(2,1)} %param.27) | copy-start | bytes 786436
  4.7 13.5 %copy-start.18 = (bf16[128,256]{1,0:T(8,128)(2,1)S(1)}, bf16[128,256]{1,0:T(8,128)(2,1)}, u32[]{:S(2)}) copy-start(bf16[128,256]{1,0:T(8,128)(2,1)} %param.28) | copy-start | bytes 196612
  5.6 12.7 %copy-start.19 = (bf16[128,256]{1,0:T(8,128)(2,1)S(1)}, bf16[128,256]{1,0:T(8,128)(2,1)}, u32[]{:S(2)}) copy-start(bf16[128,256]{1,0:T(8,128)(2,1)} %param.29) | copy-start | bytes 196612
  12.6 6.5 copy-start.20
  12.6 6.5 copy-start.21
  12.6 6.5 copy-start.22
  18.2 2.1 copy-start.2
  19.1 2.5 copy-start.17
  19.1 3.4 copy-start.10
  640.5 1.8 copy-start.12
  640.5 1.8 copy-start.13
  642.3 1.2 copy-start.15
  642.3 1.2 copy-start.16
  642.3 7.8 %copy-start.14 = (bf16[128,512]{1,0:T(8,128)(2,1)S(1)}, bf16[128,512]{1,0:T(8,128)(2,1)}, u32[]{:S(2)}) copy-start(bf16[128,512]{1,0:T(8,128)(2,1)} %get-tuple-element.83) | copy-start | bytes 393220
  642.3 7.8 %copy-start.11 = (f32[128,512]{1,0:T(8,128)S(1)}, f32[128,512]{1,0:T(8,128)}, u32[]{:S(2)}) copy-start(f32[128,512]{1,0:T(8,128)} %get-tuple-element.82) | copy-start | bytes 786436
  643.5 7.7 %copy-start.6 = (f32[128,768]{1,0:T(8,128)S(1)}, f32[128,768]{1,0:T(8,128)}, u32[]{:S(2)}) copy-start(f32[128,768]{1,0:T(8,128)} %get-tuple-element.80) | copy-start | bytes 1179652
  643.5 7.7 %copy-start.5 = (bf16[128,768]{1,0:T(8,128)(2,1)S(1)}, bf16[128,768]{1,0:T(8,128)(2,1)}, u32[]{:S(2)}) copy-start(bf16[128,768]{1,0:T(8,128)(2,1)} %get-tuple-element.81) | copy-start | bytes 589828
  650.2 3.3 copy-start.7
  650.2 3.3 copy-start.8
  651.2 3.6 copy-start.4
  653.5 2.3 copy-start.3
  654.8 2.0 copy-start.1

commit v5 on v4

--- a/solution.py
+++ b/solution.py
@@ -825,10 +825,10 @@
     o_first[2].wait_recv()
     for copy in o_second[1]:
         copy.start()
-    ff_start(1, 0)
     c_forward[0].start()
     for copy in c_copies[0]:
         copy.start()
+    ff_start(1, 0)
     for at in range(kv_heads):
         heads, one, wide = views(at)
         intra_kernel(

time: 663 us -> 663 us (level)
  no operation moved by 1% of the time
where the time goes in v5:
time: 663 us; the launch traced here: 657 us
  Pallas kernels  609 us (92%)
  local copies, waits for them, and re-layouts  23 us (3%)
  other arithmetic  20.9 us (3%)
    pallas_call x1, Pallas kernels, rear(): pl.pallas_call(functools.partial(rear_kernel, chips, kv_heads, group, ran...  253 us
    pallas_call x1, Pallas kernels, front(): pl.pallas_call(functools.partial(front_kernel, chips, kv_heads, group), i...  228 us
    pallas_call x1, Pallas kernels, feed(): pl.pallas_call(functools.partial(feed_kernel, chips), in_specs=[near, far...  128 us

profile of v5, /device:TPU:15, one launch (start us, length us, event | category | flops | bytes accessed | tf_op | source)
XLA Modules:
  0.0 657.3 jit_solution(745802373353816988)
XLA Ops:
  0.7 1.3 fusion.43
  4.7 0.9 copy.80.cont_ref
  6.2 1.5 fusion.10.carry_ref
  7.9 0.7 add_select_fusion
  9.3 0.7 constant_dynamic-slice_fusion.3
  10.1 0.8 fusion.13.ups_ref
  10.8 1.0 fusion.30
  11.8 0.8 pad_maximum_fusion.1.fq_ref
  12.6 0.8 pad_maximum_fusion.2.fk_ref
  13.4 1.8 fusion.11
  15.2 0.9 copy.79.seg_q_ref
  16.1 1.2 compare_select_fusion.1.seg_k_ref
  17.5 0.7 pad.28.odown_ref
  18.3 0.8 pad_maximum_fusion.wqkv_ref
  19.4 0.9 pad.24.downs_ref
  20.3 1.3 copy.78
  21.6 0.8 pad.29.oup_ref
  22.5 0.9 copy.77
  23.3 227.8 %shard_map.391 = (bf16[2048,768]{1,0:T(8,128)(2,1)}, bf16[2048,512]{1,0:T(8,128)(2,1)}, bf16[512,2048]{1,0:T(8,128)(2,1)}, bf16[512,128]{1,0:T(8,128)(2,1)}, bf1...) custom-call(bf16[256,2048]{1,0:T(8,128)(2,1)} %hid_ref.3, ...), custom_call_target="tpu_custom_call" | custom-call | flops 10000000000 | bytes 100000000 | tf_op jit(solution)/shard_map/pallas_call | solution.py:937
  251.1 128.5 %shard_map.392 = (f32[256,2048]{1,0:T(8,128)}, bf16[4,256,2048]{2,1,0:T(8,128)(2,1)}, bf16[3,2048,512]{2,1,0:T(8,128)(2,1)}, bf16[3,256,2048]{2,1,0:T(8,128)(2,1)}, bf16[4,512,2048]{2,1,0:T(8,128)(2,1)}) custom-call(bf16[256,2048]{1,0:T(8,128)(2,1)} %get-tuple-element.56.x_ref, bf16[4,512,2048]{2,1,0:T(8,128)(2,1)} %get-tuple-element.57.c_ref, ...), custom_call_target="tpu_custom_call" | custom-call | flops 38654705664 | bytes 33554432 | tf_op jit(solution)/shard_map/pallas_call | solution.py:573
  381.6 252.9 %shard_map.393 = (bf16[256,2048]{1,0:T(8,128)(2,1)}, bf16[256,2048]{1,0:T(8,128)(2,1)}, f32[128,768]{1,0:T(8,128)}, bf16[128,768]{1,0:T(8,128)(2,1)}, f32[128,51...) custom-call(f32[256,2048]{1,0:T(8,128)} %get-tuple-element.59.gnf_re, ...), custom_call_target="tpu_custom_call" | custom-call | flops 40000000000 | bytes 100000000 | tf_op jit(solution)/shard_map/pallas_call | solution.py:1398
  634.5 6.0 add_bitcast_fusion
  640.5 1.8 copy.84
  642.4 1.1 fusion.32
  644.8 0.7 fusion.37
  645.5 0.7 fusion.38
  646.9 0.7 fusion.39
  647.6 0.7 fusion.40
  650.2 1.0 copy.83
  652.6 0.8 maximum_select_fusion
  654.8 1.0 copy.90
  655.8 1.0 copy.91
  (95 shorter events, 10.7 us)
Async XLA Ops:
  0.7 8.6 %copy-start = (bf16[8,1024]{1,0:T(8,128)(2,1)S(1)}, bf16[8,1024]{1,0:T(8,128)(2,1)}, u32[]{:S(2)}) copy-start(bf16[8,1024]{1,0:T(8,128)(2,1)} %param.32) | copy-start | bytes 49156
  0.7 12.7 %copy-start.24 = (f32[128]{0:T(128)S(1)}, f32[128]{0:T(128)}, u32[]{:S(2)}) copy-start(f32[128]{0:T(128)} %constant.79) | copy-start | bytes 1540
  0.7 12.7 %copy-start.25 = (f32[128]{0:T(128)S(1)}, f32[128]{0:T(128)}, u32[]{:S(2)}) copy-start(f32[128]{0:T(128)} %constant.80) | copy-start | bytes 1540
  0.7 16.6 %copy-start.23 = (bf16[1024,8]{0,1:T(8,128)(2,1)S(1)}, bf16[1024,8]{0,1:T(8,128)(2,1)}, u32[]{:S(2)}) copy-start(bf16[1024,8]{0,1:T(8,128)(2,1)} %param.37) | copy-start | bytes 49156
  0.7 17.5 %copy-start.9 = (bf16[128,1024]{1,0:T(8,128)(2,1)S(1)}, bf16[128,1024]{1,0:T(8,128)(2,1)}, u32[]{:S(2)}) copy-start(bf16[128,1024]{1,0:T(8,128)(2,1)} %param.27) | copy-start | bytes 786436
  4.7 13.5 %copy-start.18 = (bf16[128,256]{1,0:T(8,128)(2,1)S(1)}, bf16[128,256]{1,0:T(8,128)(2,1)}, u32[]{:S(2)}) copy-start(bf16[128,256]{1,0:T(8,128)(2,1)} %param.28) | copy-start | bytes 196612
  5.6 12.7 %copy-start.19 = (bf16[128,256]{1,0:T(8,128)(2,1)S(1)}, bf16[128,256]{1,0:T(8,128)(2,1)}, u32[]{:S(2)}) copy-start(bf16[128,256]{1,0:T(8,128)(2,1)} %param.29) | copy-start | bytes 196612
  12.6 6.5 copy-start.20
  12.6 6.5 copy-start.21
  12.6 6.5 copy-start.22
  18.2 2.1 copy-start.2
  19.1 2.5 copy-start.17
  19.1 3.4 copy-start.10
  640.5 1.8 copy-start.12
  640.5 1.8 copy-start.13
  642.3 1.2 copy-start.15
  642.3 1.2 copy-start.16
  642.3 7.8 %copy-start.14 = (bf16[128,512]{1,0:T(8,128)(2,1)S(1)}, bf16[128,512]{1,0:T(8,128)(2,1)}, u32[]{:S(2)}) copy-start(bf16[128,512]{1,0:T(8,128)(2,1)} %get-tuple-element.83) | copy-start | bytes 393220
  642.3 7.8 %copy-start.11 = (f32[128,512]{1,0:T(8,128)S(1)}, f32[128,512]{1,0:T(8,128)}, u32[]{:S(2)}) copy-start(f32[128,512]{1,0:T(8,128)} %get-tuple-element.82) | copy-start | bytes 786436
  643.5 7.7 %copy-start.6 = (f32[128,768]{1,0:T(8,128)S(1)}, f32[128,768]{1,0:T(8,128)}, u32[]{:S(2)}) copy-start(f32[128,768]{1,0:T(8,128)} %get-tuple-element.80) | copy-start | bytes 1179652
  643.5 7.7 %copy-start.5 = (bf16[128,768]{1,0:T(8,128)(2,1)S(1)}, bf16[128,768]{1,0:T(8,128)(2,1)}, u32[]{:S(2)}) copy-start(bf16[128,768]{1,0:T(8,128)(2,1)} %get-tuple-element.81) | copy-start | bytes 589828
  650.2 3.3 copy-start.7
  650.2 3.3 copy-start.8
  651.2 3.6 copy-start.4
  653.5 2.3 copy-start.3
  654.8 2.0 copy-start.1
